TPU v7x, 32 devices: a whole 2x2x4 slice. The times are simulated.
32 devices in a mesh: batch: 8 (over y, x, core), seq: 4 (over z).
Axes of the slice: x: 2, y: 2, z: 4, core: 2. Of those that a mesh axis runs over, the one named last changes fastest.
Arguments:
- inputs: bfloat16 [16, 1024, 1024], P('batch', 'seq'), may hold values from -6 to 6
- skip_input: bfloat16 [16, 1024, 1024], P('batch', 'seq'), may hold values from -6 to 6
- lengths: int32 [16], P('batch'), may hold values from 128 to 1024, as said below
- skip_weight: bfloat16 [2048, 1024], P('batch', 'seq'), may hold values from -0.125 to 0.125
- query_weight: bfloat16 [1024, 1024], P('batch', 'seq'), may hold values from -0.1875 to 0.1875
- key_weight: bfloat16 [1024, 1024], P('batch', 'seq'), may hold values from -0.1875 to 0.1875
- value_weight: bfloat16 [1024, 1024], P('batch', 'seq'), may hold values from -0.1875 to 0.1875
- out_weight: bfloat16 [1024, 1024], P('seq', 'batch'), may hold values from -0.75 to 0.75
- up_weight: bfloat16 [1024, 4096], P('batch', 'seq'), may hold values from -0.1875 to 0.1875
- down_weight: bfloat16 [4096, 1024], P('seq', 'batch'), may hold values from -0.09375 to 0.09375
- first_gain: bfloat16 [1024], P('seq'), may hold values from 0.25 to 1.75
- first_shift: bfloat16 [1024], P('seq'), may hold values from -3 to 3
- second_gain: bfloat16 [1024], P('seq'), may hold values from 0.25 to 1.75
- second_shift: bfloat16 [1024], P('seq'), may hold values from -3 to 3
- cotangent: bfloat16 [16, 1024, 1024], P('batch', 'seq'), may hold values from -6 to 6
Outputs:
- output: bfloat16 [16, 1024, 1024], P('batch', 'seq')
- input_grad: float32 [16, 1024, 1024], P('batch', 'seq')
- skip_grad: float32 [16, 1024, 1024], P('batch', 'seq')
- skip_weight_grad: float32 [2048, 1024], P('batch', 'seq')
- query_weight_grad: float32 [1024, 1024], P('batch', 'seq')
- key_weight_grad: float32 [1024, 1024], P('batch', 'seq')
- value_weight_grad: float32 [1024, 1024], P('batch', 'seq')
- out_weight_grad: float32 [1024, 1024], P('seq', 'batch')
- up_weight_grad: float32 [1024, 4096], P('batch', 'seq')
- down_weight_grad: float32 [4096, 1024], P('seq', 'batch')
- first_gain_grad: float32 [1024], P('seq')
- first_shift_grad: float32 [1024], P('seq')
- second_gain_grad: float32 [1024], P('seq')
- second_shift_grad: float32 [1024], P('seq')
Inputs may be any that keep to these rules, and one draw needn't show every extreme that they name: `lengths`: the utterances of one batch group are 2 consecutive rows; in every group at least one of them, drawn from the seed, has exactly 1024 frames.
All inputs are finite; a program needn't handle non-finite values.
Results may differ from a plain program's by a relative error of at most 0.02.
Values may be sent and summed in bfloat16 or wider, within the bound.
A program may use at most 192 MiB of HBM per device.

v0:
```python
import jax
import jax.numpy as jnp
from jax import lax
from jax.sharding import PartitionSpec as P

HEADS = 16
HEAD_DIM = 64


EPSILON = 1e-05


def layer_norm(values, norm_gain, norm_shift):
    average = jnp.mean(values, -1, keepdims=True)
    centred = values - average
    spread = jnp.mean(centred * centred, -1, keepdims=True)
    return centred * lax.rsqrt(spread + EPSILON) * norm_gain + norm_shift


def gelu_exact(values):
    return jax.nn.gelu(values, approximate=False)


def block_scores(queries, key_heads, key_valid, slopes, first_row, block_rows):
    query_block = lax.dynamic_slice_in_dim(queries, first_row, block_rows, 1)
    score_scale = queries.shape[3] ** (-0.5)
    products = (
        jnp.einsum("iqhd,ikhd->ihqk", query_block, key_heads, preferred_element_type=jnp.float32)
        * score_scale
    )
    query_pos = (first_row + jnp.arange(block_rows)).astype(jnp.float32)
    key_pos = jnp.arange(key_heads.shape[1]).astype(jnp.float32)
    distance = jnp.abs(query_pos[:, None] - key_pos[None, :])
    scores = products - slopes[None, :, None, None] * distance[None, None]
    return (jnp.where(key_valid[:, None, None, :], scores, -1e30), query_block)


def shards(
    inputs,
    skip_input,
    lengths,
    skip_weight,
    query_weight,
    key_weight,
    value_weight,
    out_weight,
    up_weight,
    down_weight,
    first_gain,
    first_shift,
    second_gain,
    second_shift,
    cotangent,
):
    (
        skip_part,
        query_part,
        key_part,
        value_part,
        out_part,
        up_part,
        down_part,
        gain_one,
        shift_one,
        gain_two,
        shift_two,
    ) = (
        lax.all_gather(skip_weight, "seq", axis=1, tiled=True),
        lax.all_gather(query_weight, "seq", axis=1, tiled=True),
        lax.all_gather(key_weight, "seq", axis=1, tiled=True),
        lax.all_gather(value_weight, "seq", axis=1, tiled=True),
        lax.all_gather(out_weight, "seq", axis=0, tiled=True),
        lax.all_gather(up_weight, "seq", axis=1, tiled=True),
        lax.all_gather(down_weight, "seq", axis=0, tiled=True),
        lax.all_gather(first_gain, "seq", axis=0, tiled=True),
        lax.all_gather(first_shift, "seq", axis=0, tiled=True),
        lax.all_gather(second_gain, "seq", axis=0, tiled=True),
        lax.all_gather(second_shift, "seq", axis=0, tiled=True),
    )
    skip_full, query_full, key_full, value_full, out_full, up_full, down_full = (
        lax.all_gather(skip_part, "batch", axis=0, tiled=True),
        lax.all_gather(query_part, "batch", axis=0, tiled=True),
        lax.all_gather(key_part, "batch", axis=0, tiled=True),
        lax.all_gather(value_part, "batch", axis=0, tiled=True),
        lax.all_gather(out_part, "batch", axis=1, tiled=True),
        lax.all_gather(up_part, "batch", axis=0, tiled=True),
        lax.all_gather(down_part, "batch", axis=1, tiled=True),
    )
    gain_first = gain_one.astype(jnp.float32)
    shift_first = shift_one.astype(jnp.float32)
    gain_second = gain_two.astype(jnp.float32)
    shift_second = shift_two.astype(jnp.float32)
    joined = jnp.concatenate([inputs, skip_input], -1)
    mixed_stream = jnp.einsum("ifc,cd->ifd", joined, skip_full, preferred_element_type=jnp.float32)
    normed = layer_norm(mixed_stream, gain_first, shift_first).astype(jnp.bfloat16)
    stacked = jnp.stack([query_full, key_full, value_full])
    projected = jnp.einsum(
        "ifd,cde->ifce", normed, stacked, preferred_element_type=jnp.float32
    ).astype(jnp.bfloat16)
    heads_view = lax.all_to_all(projected, "seq", split_axis=3, concat_axis=1, tiled=True)
    item_count = heads_view.shape[0]
    frames = heads_view.shape[1]
    local_width = heads_view.shape[3]
    local_heads = local_width // HEAD_DIM
    head_shape = (item_count, frames, local_heads, HEAD_DIM)
    queries = heads_view[:, :, 0].reshape(head_shape)
    key_heads = heads_view[:, :, 1].reshape(head_shape)
    values = heads_view[:, :, 2].reshape(head_shape)
    head_numbers = lax.axis_index("seq") * local_heads + jnp.arange(local_heads)
    slopes = 2.0 ** (-8.0 * (head_numbers + 1).astype(jnp.float32) / HEADS)
    key_valid = jnp.arange(frames)[None, :] < lengths[:, None]
    block_rows = min(512, frames)
    block_count = frames // block_rows
    score_scale = HEAD_DIM ** (-0.5)

    def forward_block(block_index):
        scores, query_block = block_scores(
            queries, key_heads, key_valid, slopes, block_index * block_rows, block_rows
        )
        highest = jnp.max(scores, -1, keepdims=True)
        weights = jnp.exp(scores - highest)
        row_total = jnp.sum(weights, -1, keepdims=True)
        weights_low = (weights / row_total).astype(jnp.bfloat16)
        block_out = jnp.einsum(
            "ihqk,ikhd->iqhd", weights_low, values, preferred_element_type=jnp.float32
        ).astype(jnp.bfloat16)
        return (block_out, (highest + jnp.log(row_total))[..., 0])

    block_outputs, logsum = lax.map(forward_block, jnp.arange(block_count))
    attended = jnp.moveaxis(block_outputs, 0, 1).reshape(item_count, frames, local_width)
    attended_frames = lax.all_to_all(attended, "seq", split_axis=1, concat_axis=2, tiled=True)
    middle = mixed_stream + jnp.einsum(
        "ifd,de->ife", attended_frames, out_full, preferred_element_type=jnp.float32
    )
    ffn_input = layer_norm(middle, gain_second, shift_second).astype(jnp.bfloat16)
    hidden = jnp.einsum("ifd,dk->ifk", ffn_input, up_full, preferred_element_type=jnp.float32)
    active = gelu_exact(hidden).astype(jnp.bfloat16)
    output = (
        middle + jnp.einsum("ifk,kd->ifd", active, down_full, preferred_element_type=jnp.float32)
    ).astype(jnp.bfloat16)
    down_grad = jnp.einsum("ifk,ifd->kd", active, cotangent, preferred_element_type=jnp.float32)
    active_grad = jnp.einsum(
        "ifd,kd->ifk", cotangent, down_full, preferred_element_type=jnp.float32
    )
    hidden_grad = jax.vjp(gelu_exact, hidden)[1](active_grad)[0].astype(jnp.bfloat16)
    up_grad = jnp.einsum("ifd,ifk->dk", ffn_input, hidden_grad, preferred_element_type=jnp.float32)
    ffn_input_grad = jnp.einsum(
        "ifk,dk->ifd", hidden_grad, up_full, preferred_element_type=jnp.float32
    )
    second_pull = jax.vjp(layer_norm, middle, gain_second, shift_second)[1]
    middle_part, gain_second_grad, shift_second_grad = second_pull(ffn_input_grad)
    middle_grad = cotangent.astype(jnp.float32) + middle_part
    middle_low = middle_grad.astype(jnp.bfloat16)
    out_grad = jnp.einsum(
        "ifd,ife->de", attended_frames, middle_low, preferred_element_type=jnp.float32
    )
    attended_grad = jnp.einsum(
        "ife,de->ifd", middle_low, out_full, preferred_element_type=jnp.float32
    ).astype(jnp.bfloat16)
    heads_grad = lax.all_to_all(
        attended_grad, "seq", split_axis=2, concat_axis=1, tiled=True
    ).reshape(head_shape)

    def backward_block(running, block_data):
        key_grad, value_grad = running
        block_index, block_logsum = block_data
        first_row = block_index * block_rows
        scores, query_block = block_scores(
            queries, key_heads, key_valid, slopes, first_row, block_rows
        )
        out_block_grad = lax.dynamic_slice_in_dim(heads_grad, first_row, block_rows, 1)
        probabilities = jnp.exp(scores - block_logsum[..., None])
        weights_low = probabilities.astype(jnp.bfloat16)
        value_grad = value_grad + jnp.einsum(
            "ihqk,iqhd->ikhd", weights_low, out_block_grad, preferred_element_type=jnp.float32
        )
        prob_grad = jnp.einsum(
            "iqhd,ikhd->ihqk", out_block_grad, values, preferred_element_type=jnp.float32
        )
        inner_sum = jnp.sum(prob_grad * probabilities, -1, keepdims=True)
        score_grad = (probabilities * (prob_grad - inner_sum)).astype(jnp.bfloat16)
        query_block_grad = (
            jnp.einsum("ihqk,ikhd->iqhd", score_grad, key_heads, preferred_element_type=jnp.float32)
            * score_scale
        ).astype(jnp.bfloat16)
        key_grad = (
            key_grad
            + jnp.einsum(
                "ihqk,iqhd->ikhd", score_grad, query_block, preferred_element_type=jnp.float32
            )
            * score_scale
        )
        return ((key_grad, value_grad), query_block_grad)

    empty_grad = jnp.zeros(head_shape, jnp.float32)
    (key_grad, value_grad), query_blocks = lax.scan(
        backward_block, (empty_grad, empty_grad), (jnp.arange(block_count), logsum)
    )
    query_grad = jnp.moveaxis(query_blocks, 0, 1).reshape(item_count, frames, local_width)
    key_grad_low = key_grad.reshape(item_count, frames, local_width).astype(jnp.bfloat16)
    value_grad_low = value_grad.reshape(item_count, frames, local_width).astype(jnp.bfloat16)
    grads_heads = jnp.stack([query_grad, key_grad_low, value_grad_low], 2)
    grads_frames = lax.all_to_all(grads_heads, "seq", split_axis=1, concat_axis=3, tiled=True)
    qkv_grad = jnp.einsum("ifd,ifce->cde", normed, grads_frames, preferred_element_type=jnp.float32)
    normed_grad = jnp.einsum(
        "ifce,cde->ifd", grads_frames, stacked, preferred_element_type=jnp.float32
    )
    first_pull = jax.vjp(layer_norm, mixed_stream, gain_first, shift_first)[1]
    mixed_part, gain_first_grad, shift_first_grad = first_pull(normed_grad)
    mixed_low = (middle_grad + mixed_part).astype(jnp.bfloat16)
    skip_w_grad = jnp.einsum("ifc,ifd->cd", joined, mixed_low, preferred_element_type=jnp.float32)
    joined_grad = jnp.einsum(
        "ifd,cd->ifc", mixed_low, skip_full, preferred_element_type=jnp.float32
    )
    model_width = mixed_stream.shape[2]
    input_grad = joined_grad[:, :, :model_width]
    skip_grad = joined_grad[:, :, model_width:]
    skip_share, query_share, key_share, value_share, out_share, up_share, down_share = (
        lax.psum_scatter(
            skip_w_grad.astype(jnp.bfloat16), "batch", scatter_dimension=0, tiled=True
        ).astype(jnp.float32),
        lax.psum_scatter(
            qkv_grad[0].astype(jnp.bfloat16), "batch", scatter_dimension=0, tiled=True
        ).astype(jnp.float32),
        lax.psum_scatter(
            qkv_grad[1].astype(jnp.bfloat16), "batch", scatter_dimension=0, tiled=True
        ).astype(jnp.float32),
        lax.psum_scatter(
            qkv_grad[2].astype(jnp.bfloat16), "batch", scatter_dimension=0, tiled=True
        ).astype(jnp.float32),
        lax.psum_scatter(
            out_grad.astype(jnp.bfloat16), "batch", scatter_dimension=1, tiled=True
        ).astype(jnp.float32),
        lax.psum_scatter(
            up_grad.astype(jnp.bfloat16), "batch", scatter_dimension=0, tiled=True
        ).astype(jnp.float32),
        lax.psum_scatter(
            down_grad.astype(jnp.bfloat16), "batch", scatter_dimension=1, tiled=True
        ).astype(jnp.float32),
    )
    (
        skip_share,
        query_share,
        key_share,
        value_share,
        out_share,
        up_share,
        down_share,
        gain_one_grad,
        shift_one_grad,
        gain_two_grad,
        shift_two_grad,
    ) = (
        lax.psum_scatter(
            skip_share.astype(jnp.bfloat16), "seq", scatter_dimension=1, tiled=True
        ).astype(jnp.float32),
        lax.psum_scatter(
            query_share.astype(jnp.bfloat16), "seq", scatter_dimension=1, tiled=True
        ).astype(jnp.float32),
        lax.psum_scatter(
            key_share.astype(jnp.bfloat16), "seq", scatter_dimension=1, tiled=True
        ).astype(jnp.float32),
        lax.psum_scatter(
            value_share.astype(jnp.bfloat16), "seq", scatter_dimension=1, tiled=True
        ).astype(jnp.float32),
        lax.psum_scatter(
            out_share.astype(jnp.bfloat16), "seq", scatter_dimension=0, tiled=True
        ).astype(jnp.float32),
        lax.psum_scatter(
            up_share.astype(jnp.bfloat16), "seq", scatter_dimension=1, tiled=True
        ).astype(jnp.float32),
        lax.psum_scatter(
            down_share.astype(jnp.bfloat16), "seq", scatter_dimension=0, tiled=True
        ).astype(jnp.float32),
        lax.psum_scatter(
            gain_first_grad.astype(jnp.bfloat16), "seq", scatter_dimension=0, tiled=True
        ).astype(jnp.float32),
        lax.psum_scatter(
            shift_first_grad.astype(jnp.bfloat16), "seq", scatter_dimension=0, tiled=True
        ).astype(jnp.float32),
        lax.psum_scatter(
            gain_second_grad.astype(jnp.bfloat16), "seq", scatter_dimension=0, tiled=True
        ).astype(jnp.float32),
        lax.psum_scatter(
            shift_second_grad.astype(jnp.bfloat16), "seq", scatter_dimension=0, tiled=True
        ).astype(jnp.float32),
    )
    gain_one_grad, shift_one_grad, gain_two_grad, shift_two_grad = lax.psum(
        (gain_one_grad, shift_one_grad, gain_two_grad, shift_two_grad), "batch"
    )
    return (
        output,
        input_grad,
        skip_grad,
        skip_share,
        query_share,
        key_share,
        value_share,
        out_share,
        up_share,
        down_share,
        gain_one_grad,
        shift_one_grad,
        gain_two_grad,
        shift_two_grad,
    )


def solution(mesh):
    in_specs = (
        P("batch", "seq", None),
        P("batch", "seq", None),
        P("batch"),
        P("batch", "seq"),
        P("batch", "seq"),
        P("batch", "seq"),
        P("batch", "seq"),
        P("seq", "batch"),
        P("batch", "seq"),
        P("seq", "batch"),
        P("seq"),
        P("seq"),
        P("seq"),
        P("seq"),
        P("batch", "seq", None),
    )
    out_specs = (
        P("batch", "seq", None),
        P("batch", "seq", None),
        P("batch", "seq", None),
        P("batch", "seq"),
        P("batch", "seq"),
        P("batch", "seq"),
        P("batch", "seq"),
        P("seq", "batch"),
        P("batch", "seq"),
        P("seq", "batch"),
        P("seq"),
        P("seq"),
        P("seq"),
        P("seq"),
    )
    return jax.shard_map(shards, mesh=mesh, in_specs=in_specs, out_specs=out_specs, check_vma=False)
```

profile of v0, /device:TPU:0, one launch (start us, length us, event | category | flops | bytes accessed | tf_op | source)
XLA Modules:
  0.0 1201.4 jit_solution(12095531755110334735)
XLA Ops:
  8.0 21.1 %all_gather.54 = bf16[256,1024]{1,0:T(8,128)(2,1)} all-gather(bf16[256,256]{1,0:T(8,128)(2,1)} %param.22), channel_id=1, replica_groups=mesh['batch'=8,'seq'=4] {'seq'}, dimensions={1}, use_global_device_ids=true | all-gather | bytes 655360 | tf_op jit(solution)/shard_map/all_gather | solution.py:68
  29.2 18.0 %all_gather.58 = bf16[128,1024]{1,0:T(8,128)(2,1)} all-gather(bf16[128,256]{1,0:T(8,128)(2,1)} %param.23), channel_id=1, replica_groups=mesh['batch'=8,'seq'=4] {'seq'}, dimensions={1}, use_global_device_ids=true | all-gather | bytes 327680 | tf_op jit(solution)/shard_map/all_gather | solution.py:69
  47.3 15.0 %all_gather.60 = bf16[128,1024]{1,0:T(8,128)(2,1)} all-gather(bf16[128,256]{1,0:T(8,128)(2,1)} %param.24), channel_id=1, replica_groups=mesh['batch'=8,'seq'=4] {'seq'}, dimensions={1}, use_global_device_ids=true | all-gather | bytes 327680 | tf_op jit(solution)/shard_map/all_gather | solution.py:70
  62.4 15.2 %all_gather.62 = bf16[128,1024]{1,0:T(8,128)(2,1)} all-gather(bf16[128,256]{1,0:T(8,128)(2,1)} %param.25), channel_id=1, replica_groups=mesh['batch'=8,'seq'=4] {'seq'}, dimensions={1}, use_global_device_ids=true | all-gather | bytes 327680 | tf_op jit(solution)/shard_map/all_gather | solution.py:71
  78.3 14.8 %all_gather.64 = bf16[1024,128]{1,0:T(8,128)(2,1)} all-gather(bf16[256,128]{1,0:T(8,128)(2,1)} %param.26), channel_id=1, replica_groups=mesh['batch'=8,'seq'=4] {'seq'}, dimensions={0}, use_global_device_ids=true | all-gather | bytes 327680 | tf_op jit(solution)/shard_map/all_gather | solution.py:72
  93.9 10.0 all-gather.1
  120.2 24.4 %all-gather.18.cloned.1.call-done = bf16[1024,1024]{1,0:T(8,128)(2,1)} async-done(((bf16[128,1024]{1,0:T(8,128)(2,1)}), bf16[1024,1024]{1,0:T(8,128)(2,1)}) %all-gather.18.cloned.1.call-update) | async-done | bytes 2097168 | tf_op jit(solution)/shard_map/all_gather | solution.py:83
  144.6 29.7 %all-gather.20.cloned.1.call-done = bf16[1024,1024]{1,0:T(8,128)(2,1)} async-done(((bf16[128,1024]{1,0:T(8,128)(2,1)}), bf16[1024,1024]{1,0:T(8,128)(2,1)}) %all-gather.20.cloned.1.call-update) | async-done | bytes 2097168 | tf_op jit(solution)/shard_map/all_gather | solution.py:84
  174.2 8.0 fusion.58
  182.3 8.8 copy.125
  195.9 27.3 %all-gather.28.cloned.1.call-done = bf16[4096,128]{1,0:T(8,128)(2,1)} async-done(((bf16[1024,128]{1,0:T(8,128)(2,1)}), bf16[4096,128]{1,0:T(8,128)(2,1)}) %all-gather.28.cloned.1.call-update) | async-done | bytes 1048592 | tf_op jit(solution)/shard_map/all_gather | solution.py:74
  223.2 48.1 %all-to-all-done = bf16[2,256,3,1024]{1,0,2,3:T(2,128)(2,1)S(1)} async-done(((bf16[2,256,3,1024]{1,0,2,3:T(2,128)(2,1)}), bf16[2,256,3,1024]{1,0,2,3:T(2,128)(2,1)S(1)}, u32[]{:S(2)}, u32[]{:S(2)}) %all-to-all-start) | async-done | bytes 3145760 | tf_op jit(solution)/shard_map/all_to_all | solution.py:100
  284.0 55.9 %while.28 = (s32[]{:T(128)}, bf16[2,2,512,4,64]{2,4,3,1,0:T(8,128)(2,1)}, f32[2,2,4,512]{3,2,1,0:T(4,128)}, s32[2]{0:T(128)S(1)}, bf16[2,1024,4,64]{1,3,2,0:T(8,...) while((s32[]{:T(128)}, ...), condition=%wide.region_5.6_spmd.clone, body=%wide.region_2.5_spmd.clone.sunk | while | flops 1140064256 | bytes 99770672 | solution.py:129
  294.2 8.3 fusion.130
  302.5 8.4 fusion.131
  322.4 8.2 fusion.130
  330.7 8.3 fusion.131
  353.3 23.3 %all-gather.3 = bf16[4,1,256]{2,1,0:T(2,128)(2,1)S(1)} all-gather(bf16[1,1,256]{2,1,0:T(2,128)(2,1)S(1)} %reshape.255), channel_id=1, replica_groups=mesh['batch'=8,'seq'=4] {'seq'}, dimensions={0}, use_global_device_ids=true | all-gather | bytes 2560 | tf_op jit(solution)/shard_map/all_gather | solution.py:78
  376.6 13.9 %all-gather.2 = bf16[4,1,256]{2,1,0:T(2,128)(2,1)S(1)} all-gather(bf16[1,1,256]{2,1,0:T(2,128)(2,1)S(1)} %reshape.253), channel_id=1, replica_groups=mesh['batch'=8,'seq'=4] {'seq'}, dimensions={0}, use_global_device_ids=true | all-gather | bytes 2560 | tf_op jit(solution)/shard_map/all_gather | solution.py:77
  398.7 11.3 fusion.65
  413.3 20.2 %multiply_convert_fusion.1 = (bf16[2,256,4096]{2,1,0:T(8,128)(2,1)}, f32[2,256,4096]{2,1,0:T(8,128)}) fusion(f32[2,256,4096]{2,1,0:T(8,128)S(1)} %get-tuple-element.383, u8[256,4096]{1,0:T(8,128)(4,1)S(1)} %get-tuple-element.305, u8[256,4096]{1,0:T(8,128)(4,1)S(1)} %get-tuple-element.304), kind=kLoop, calls=%fused_computation.72 | loop fusion | flops 146800640 | bytes 23068672 | tf_op jit(solution)/shard_map/convert_element_type | solution.py:137
  433.5 13.1 %add_convert_fusion.2 = bf16[2,256,4096]{2,1,0:T(8,128)(2,1)S(1)} fusion(f32[2,256,4096]{2,1,0:T(8,128)} %get-tuple-element.366, f32[2,256,4096]{2,1,0:T(8,128)} %copy-done.14, bf16[2,256,1024]{2,1,0:T(8,128)(2,1)} %param.33, bf16[4096,1024]{1,0:T(8,128)(2,1)} %all-gather.30.cloned.1.call-done), kind=kOutput, calls=%fused_computation.71 | convolution fusion | flops 4324327424 | bytes 30408704 | tf_op jit(solution)/shard_map/ifd,kd->ifk/dot_general | solution.py:142
  446.6 9.6 multiply_reduce_fusion.1
  469.9 22.4 %all-to-all-done.2 = bf16[2,256,1024]{1,0,2:T(2,128)(2,1)} async-done(((bf16[2,256,1024]{1,0,2:T(2,128)(2,1)}), bf16[2,256,1024]{1,0,2:T(2,128)(2,1)}, u32[]{:S(2)}, u32[]{:S(2)}) %all-to-all-start.2) | async-done | bytes 1048608 | tf_op jit(solution)/shard_map/all_to_all | solution.py:160
  499.0 97.9 %while.29 = (s32[]{:T(128)}, f32[2,1024,4,64]{1,3,2,0:T(8,128)}, f32[2,1024,4,64]{1,3,2,0:T(8,128)}, bf16[2,2,512,4,64]{2,4,3,1,0:T(8,128)(2,1)}, s32[2]{0:T(128...) while((s32[]{:T(128)}, f32[2,1024,4,64]{1,3,2,0:T(8,128)}, ...), condition=%wide.region_12.13_spmd.clone, body=%wide.region_10.12_spmd.clone.sunk | while | flops 2732589056 | bytes 215581136 | solution.py:196
  516.0 10.3 multiply_reduce_fusion.7
  526.3 9.9 multiply_convert_fusion.3
  564.9 10.3 multiply_reduce_fusion.7
  575.2 9.9 multiply_convert_fusion.3
  621.3 60.9 %all-to-all-done.3 = bf16[2,1024,3,256]{3,0,2,1:T(2,128)(2,1)S(1)} async-done(((bf16[2,1024,3,256]{3,0,2,1:T(2,128)(2,1)}), bf16[2,1024,3,256]{3,0,2,1:T(2,128)(2,1)S(1)}, u32[]{:S(2)}, u32[]{:S(2)}) %all-to-all-start.3) | async-done | bytes 3145760 | tf_op jit(solution)/shard_map/all_to_all | solution.py:203
  703.9 8.2 bitcast_reduce_fusion
  723.5 9.3 bitcast_convert_fusion.1
  732.8 9.2 bitcast_convert_fusion
  742.0 12.1 %copy.165 = bf16[4096,1024]{0,1:T(8,128)(2,1)} copy(bf16[4096,1024]{1,0:T(8,128)(2,1)} %bitcast_convert_fusion) | data formatting | bytes 16777216
  758.0 22.4 %reduce-scatter.45.cloned.1.call-done = bf16[128,1024]{1,0:T(8,128)(2,1)} async-done(((bf16[1024,1024]{1,0:T(8,128)(2,1)}), bf16[128,1024]{1,0:T(8,128)(2,1)}) %reduce-scatter.45.cloned.1.call-update) | async-done | bytes 262160
  782.2 43.6 %reduce-scatter.43.cloned.1.call-done = bf16[128,1024]{1,0:T(8,128)(2,1)} async-done(((bf16[1024,1024]{1,0:T(8,128)(2,1)}), bf16[128,1024]{1,0:T(8,128)(2,1)}) %reduce-scatter.43.cloned.1.call-update) | async-done | bytes 262160
  827.7 52.7 %reduce-scatter.25.cloned.1.call-done = bf16[256,1024]{1,0:T(8,128)(2,1)} async-done(((bf16[2048,1024]{1,0:T(8,128)(2,1)}), bf16[256,1024]{1,0:T(8,128)(2,1)}) %reduce-scatter.25.cloned.1.call-update) | async-done | bytes 524304 | tf_op jit(solution)/shard_map/reduce_scatter | solution.py:219
  880.5 75.0 %reduce-scatter.37.cloned.1.call-done = bf16[128,4096]{1,0:T(8,128)(2,1)} async-done(((bf16[1024,4096]{1,0:T(8,128)(2,1)}), bf16[128,4096]{1,0:T(8,128)(2,1)}) %reduce-scatter.37.cloned.1.call-update) | async-done | bytes 1048592 | tf_op jit(solution)/shard_map/reduce_scatter | solution.py:234
  956.8 73.3 %reduce-scatter.51.cloned.1.call-done = bf16[128,4096]{1,0:T(8,128)(2,1)} async-done(((bf16[1024,4096]{1,0:T(8,128)(2,1)}), bf16[128,4096]{1,0:T(8,128)(2,1)}) %reduce-scatter.51.cloned.1.call-update) | async-done | bytes 1048592
  1032.6 10.2 add_convert_fusion.4
  1042.8 9.7 reduce-scatter.35.cloned.1.call-done
  1053.9 9.1 all-reduce.5
  1063.2 13.1 %all-reduce.4 = (f32[256]{0:T(256)}, f32[256]{0:T(256)}, f32[256]{0:T(256)}, f32[256]{0:T(256)}) all-reduce(f32[256]{0:T(256)S(1)} %get-tuple-element.389, f32[256]{0:T(256)S(1)} %get-tuple-element.388, f32[256]{0:T(256)S(1)} %get-tuple-element.387, f32[256]{0:T(256)S(1)} %get-tuple-element.386), channel_id=1, replica_groups=mesh['batch'=8,'seq'=4] {'batch'}, use_global_device_ids=true, to_apply=%region_31.32 | all-reduce | flops 1024 | bytes 8192 | tf_op jit(solution)/shard_map/psum | solution.py:288
  1085.1 8.7 reduce-scatter.31.cloned.1.call-done
  1095.5 19.1 %reduce-scatter.29.cloned.1.call-done = bf16[128,256]{0,1:T(8,128)(2,1)} async-done(((bf16[128,1024]{0,1:T(8,128)(2,1)}), bf16[128,256]{0,1:T(8,128)(2,1)}) %reduce-scatter.29.cloned.1.call-update) | async-done | bytes 65552 | tf_op jit(solution)/shard_map/reduce_scatter | solution.py:257
  1116.2 20.7 %reduce-scatter.27.cloned.1.call-done = bf16[256,256]{1,0:T(8,128)(2,1)} async-done(((bf16[256,1024]{1,0:T(8,128)(2,1)}), bf16[256,256]{1,0:T(8,128)(2,1)}) %reduce-scatter.27.cloned.1.call-update) | async-done | bytes 131088 | tf_op jit(solution)/shard_map/reduce_scatter | solution.py:254
  1138.5 26.3 %reduce-scatter.39.cloned.1.call-done = bf16[128,1024]{1,0:T(8,128)(2,1)} async-done(((bf16[128,4096]{1,0:T(8,128)(2,1)}), bf16[128,1024]{1,0:T(8,128)(2,1)}) %reduce-scatter.39.cloned.1.call-update) | async-done | bytes 262160 | tf_op jit(solution)/shard_map/reduce_scatter | solution.py:269
  1166.6 26.3 %reduce-scatter.41.cloned.1.call-done = bf16[1024,128]{1,0:T(8,128)(2,1)} async-done(((bf16[4096,128]{1,0:T(8,128)(2,1)}), bf16[1024,128]{1,0:T(8,128)(2,1)}) %reduce-scatter.41.cloned.1.call-update) | async-done | bytes 262160 | tf_op jit(solution)/shard_map/reduce_scatter | solution.py:272
  (311 shorter events, 244.8 us)
Async XLA Ops:
  7.2 86.6 %copy-start.50 = (bf16[256]{0:T(256)(128)(2,1)S(1)}, bf16[256]{0:T(256)(128)(2,1)}, u32[]{:S(2)}) copy-start(bf16[256]{0:T(256)(128)(2,1)} %param.29) | copy-start | bytes 1540
  7.2 86.6 %copy-start.51 = (bf16[256]{0:T(256)(128)(2,1)S(1)}, bf16[256]{0:T(256)(128)(2,1)}, u32[]{:S(2)}) copy-start(bf16[256]{0:T(256)(128)(2,1)} %param.30) | copy-start | bytes 1540
  7.2 104.3 %copy-start.23 = (bf16[2,256,1024]{2,1,0:T(8,128)(2,1)S(1)}, bf16[2,256,1024]{2,1,0:T(8,128)(2,1)}, u32[]{:S(2)}) copy-start(bf16[2,256,1024]{2,1,0:T(8,128)(2,1)} %param.19) | copy-start | bytes 3145732
  7.2 105.3 %copy-start.24 = (bf16[2,256,1024]{2,1,0:T(8,128)(2,1)S(1)}, bf16[2,256,1024]{2,1,0:T(8,128)(2,1)}, u32[]{:S(2)}) copy-start(bf16[2,256,1024]{2,1,0:T(8,128)(2,1)} %param.20) | copy-start | bytes 3145732
  7.2 85.9 %all-gather.24.cloned.1.call-start = ((), (), s32[]{:S(2)}) async-start(), calls=%async_computation.23 | async-start | bytes 1310720 | tf_op jit(solution)/shard_map/all_gather | solution.py:73
  8.0 105.6 %all-gather.14.cloned.1.call-start = ((), (), s32[]{:S(2)}) async-start(), calls=%async_computation.18 | async-start | bytes 4718592 | tf_op jit(solution)/shard_map/all_gather | solution.py:81
  29.1 91.0 %all-gather.16.cloned.1.call-start = ((), (), s32[]{:S(2)}) async-start(), calls=%async_computation.19 | async-start | bytes 2359296 | tf_op jit(solution)/shard_map/all_gather | solution.py:82
  47.2 97.4 %all-gather.18.cloned.1.call-start = ((), (), s32[]{:S(2)}) async-start(), calls=%async_computation.20 | async-start | bytes 2359296 | tf_op jit(solution)/shard_map/all_gather | solution.py:83
  62.3 111.9 %all-gather.20.cloned.1.call-start = ((), (), s32[]{:S(2)}) async-start(), calls=%async_computation.21 | async-start | bytes 2359296 | tf_op jit(solution)/shard_map/all_gather | solution.py:84
  77.6 145.5 %all-gather.28.cloned.1.call-start = ((), (), s32[]{:S(2)}) async-start(), calls=%async_computation.25 | async-start | bytes 1310720 | tf_op jit(solution)/shard_map/all_gather | solution.py:74
  78.2 314.8 %all-gather.22.cloned.1.call-start = ((), (), s32[]{:S(2)}) async-start(), calls=%async_computation.22 | async-start | bytes 2359296 | tf_op jit(solution)/shard_map/all_gather | solution.py:85
  93.1 305.6 %all-gather.26.cloned.1.call-start = ((), (), s32[]{:S(2)}) async-start(), calls=%async_computation.24 | async-start | bytes 9437184 | tf_op jit(solution)/shard_map/all_gather | solution.py:86
  103.9 70.4 %copy-start.43 = (f32[4,1,256]{2,1,0:T(1,128)}, f32[4,1,256]{2,1,0:T(1,128)S(1)}, u32[]{:S(2)}) copy-start(f32[4,1,256]{2,1,0:T(1,128)S(1)} %convert_element_type.245) | copy-start | bytes 12292
  111.5 62.8 %copy-start.27 = (f32[4,1,256]{2,1,0:T(1,128)}, f32[4,1,256]{2,1,0:T(1,128)S(1)}, u32[]{:S(2)}) copy-start(f32[4,1,256]{2,1,0:T(1,128)S(1)} %convert_element_type.244) | copy-start | bytes 12292
  118.8 63.5 %copy-start.7 = (f32[2,256,1024]{2,1,0:T(8,128)}, f32[2,256,1024]{2,1,0:T(8,128)S(1)}, u32[]{:S(2)}) copy-start(f32[2,256,1024]{2,1,0:T(8,128)S(1)} %get-tuple-element.380) | copy-start | bytes 6291460
  118.8 63.5 %copy-start.29 = (f32[2,256]{1,0:T(2,128)}, f32[2,256]{1,0:T(2,128)S(1)}, u32[]{:S(2)}) copy-start(f32[2,256]{1,0:T(2,128)S(1)} %broadcast_multiply_fusion.3) | copy-start | bytes 6148
  120.1 62.2 %copy-start.31 = (f32[2,256]{1,0:T(2,128)}, f32[2,256]{1,0:T(2,128)S(1)}, u32[]{:S(2)}) copy-start(f32[2,256]{1,0:T(2,128)S(1)} %fusion.77) | copy-start | bytes 6148
  191.1 80.1 %all-to-all-start = ((bf16[2,256,3,1024]{1,0,2,3:T(2,128)(2,1)}), bf16[2,256,3,1024]{1,0,2,3:T(2,128)(2,1)S(1)}, u32[]{:S(2)}, u32[]{:S(2)}) async-start(bf16[2,256,3,1024]{1,0,2,3:T(2,128)(2,1)} %copy.125), calls=%async_computation | async-start | bytes 6291456 | tf_op jit(solution)/shard_map/all_to_all | solution.py:100
  195.7 237.8 %all-gather.30.cloned.1.call-start = ((), (), s32[]{:S(2)}) async-start(), calls=%async_computation.26 | async-start | bytes 9437184 | tf_op jit(solution)/shard_map/all_gather | solution.py:87
  339.9 13.3 %copy-start.52 = (bf16[256]{0:T(256)(128)(2,1)S(1)}, bf16[256]{0:T(256)(128)(2,1)}, u32[]{:S(2)}) copy-start(bf16[256]{0:T(256)(128)(2,1)} %param.31) | copy-start | bytes 1540
  340.0 13.3 %copy-start.53 = (bf16[256]{0:T(256)(128)(2,1)S(1)}, bf16[256]{0:T(256)(128)(2,1)}, u32[]{:S(2)}) copy-start(bf16[256]{0:T(256)(128)(2,1)} %param.32) | copy-start | bytes 1540
  349.0 41.5 %all-to-all-start.1 = ((bf16[2,1024,256]{2,0,1:T(2,128)(2,1)}), bf16[2,1024,256]{2,0,1:T(2,128)(2,1)}, u32[]{:S(2)}, u32[]{:S(2)}) async-start(bf16[2,1024,256]{2,0,1:T(2,128)(2,1)} %reshape.273), calls=%async_computation.1 | async-start | bytes 2097152 | tf_op jit(solution)/shard_map/all_to_all | solution.py:131
  376.6 22.1 %copy-start.45 = (f32[4,1,256]{2,1,0:T(1,128)}, f32[4,1,256]{2,1,0:T(1,128)S(1)}, u32[]{:S(2)}) copy-start(f32[4,1,256]{2,1,0:T(1,128)S(1)} %convert_element_type.247) | copy-start | bytes 12292
  390.5 65.7 %copy-start.39 = (f32[4,1,256]{2,1,0:T(1,128)}, f32[4,1,256]{2,1,0:T(1,128)S(1)}, u32[]{:S(2)}) copy-start(f32[4,1,256]{2,1,0:T(1,128)S(1)} %convert_element_type.246) | copy-start | bytes 12292
  396.9 59.3 %copy-start.35 = (f32[2,256]{1,0:T(2,128)}, f32[2,256]{1,0:T(2,128)S(1)}, u32[]{:S(2)}) copy-start(f32[2,256]{1,0:T(2,128)S(1)} %broadcast_multiply_fusion.2) | copy-start | bytes 6148
  398.6 57.6 %copy-start.41 = (f32[2,256]{1,0:T(2,128)}, f32[2,256]{1,0:T(2,128)S(1)}, u32[]{:S(2)}) copy-start(f32[2,256]{1,0:T(2,128)S(1)} %fusion.78) | copy-start | bytes 6148
  433.5 13.1 %copy-start.12 = (f32[2,256,1024]{2,1,0:T(8,128)S(1)}, f32[2,256,1024]{2,1,0:T(8,128)}, u32[]{:S(2)}) copy-start(f32[2,256,1024]{2,1,0:T(8,128)} %copy-done.11) | copy-start | bytes 6291460
  446.6 9.6 copy-start.55
  465.5 26.9 %all-to-all-start.2 = ((bf16[2,256,1024]{1,0,2:T(2,128)(2,1)}), bf16[2,256,1024]{1,0,2:T(2,128)(2,1)}, u32[]{:S(2)}, u32[]{:S(2)}) async-start(bf16[2,256,1024]{1,0,2:T(2,128)(2,1)} %copy.135), calls=%async_computation.2 | async-start | bytes 2097152 | tf_op jit(solution)/shard_map/all_to_all | solution.py:160
  609.3 72.9 %all-to-all-start.3 = ((bf16[2,1024,3,256]{3,0,2,1:T(2,128)(2,1)}), bf16[2,1024,3,256]{3,0,2,1:T(2,128)(2,1)S(1)}, u32[]{:S(2)}, u32[]{:S(2)}) async-start(bf16[2,1024,3,256]{3,0,2,1:T(2,128)(2,1)} %copy.138), calls=%async_computation.3 | async-start | bytes 6291456 | tf_op jit(solution)/shard_map/all_to_all | solution.py:203
  613.1 141.1 %reduce-scatter.49.cloned.1.call-start = ((), (), s32[]{:S(2)}) async-start(), calls=%async_computation.39 | async-start | bytes 2359296
  621.3 134.8 %reduce-scatter.47.cloned.1.call-start = ((), (), s32[]{:S(2)}) async-start(), calls=%async_computation.38 | async-start | bytes 2359296
  695.7 84.7 %reduce-scatter.45.cloned.1.call-start = ((), (), s32[]{:S(2)}) async-start(), calls=%async_computation.37 | async-start | bytes 2359296
  699.7 126.2 %reduce-scatter.43.cloned.1.call-start = ((), (), s32[]{:S(2)}) async-start(), calls=%async_computation.36 | async-start | bytes 2359296
  703.8 176.6 %reduce-scatter.25.cloned.1.call-start = ((), (), s32[]{:S(2)}) async-start(), calls=%async_computation.27 | async-start | bytes 4718592 | tf_op jit(solution)/shard_map/reduce_scatter | solution.py:219
  721.9 233.6 %reduce-scatter.37.cloned.1.call-start = ((), (), s32[]{:S(2)}) async-start(), calls=%async_computation.33 | async-start | bytes 9437184 | tf_op jit(solution)/shard_map/reduce_scatter | solution.py:234
  732.8 297.3 %reduce-scatter.51.cloned.1.call-start = ((), (), s32[]{:S(2)}) async-start(), calls=%async_computation.40 | async-start | bytes 9437184
  754.1 201.4 %copy-start.54 = (u32[32]{0:T(128)S(1)}, u32[32]{0:T(128)}, u32[]{:S(2)}) copy-start(u32[32]{0:T(128)} %constant.147) | copy-start | bytes 388
  754.1 298.3 %reduce-scatter.35.cloned.1.call-start = ((), (), s32[]{:S(2)}) async-start(), calls=%async_computation.32 | async-start | bytes 327680 | tf_op jit(solution)/shard_map/reduce_scatter | solution.py:266
  756.0 327.5 %reduce-scatter.33.cloned.1.call-start = ((), (), s32[]{:S(2)}) async-start(), calls=%async_computation.31 | async-start | bytes 327680 | tf_op jit(solution)/shard_map/reduce_scatter | solution.py:263
  757.9 336.0 %reduce-scatter.31.cloned.1.call-start = ((), (), s32[]{:S(2)}) async-start(), calls=%async_computation.30 | async-start | bytes 327680 | tf_op jit(solution)/shard_map/reduce_scatter | solution.py:260
  782.2 332.4 %reduce-scatter.29.cloned.1.call-start = ((), (), s32[]{:S(2)}) async-start(), calls=%async_computation.29 | async-start | bytes 327680 | tf_op jit(solution)/shard_map/reduce_scatter | solution.py:257
  827.7 309.2 %reduce-scatter.27.cloned.1.call-start = ((), (), s32[]{:S(2)}) async-start(), calls=%async_computation.28 | async-start | bytes 655360 | tf_op jit(solution)/shard_map/reduce_scatter | solution.py:254
  880.5 284.3 %reduce-scatter.39.cloned.1.call-start = ((), (), s32[]{:S(2)}) async-start(), calls=%async_computation.34 | async-start | bytes 1310720 | tf_op jit(solution)/shard_map/reduce_scatter | solution.py:269
  955.5 237.4 %reduce-scatter.41.cloned.1.call-start = ((), (), s32[]{:S(2)}) async-start(), calls=%async_computation.35 | async-start | bytes 1310720 | tf_op jit(solution)/shard_map/reduce_scatter | solution.py:272
  1032.5 21.4 %copy-start.47 = (bf16[1024]{0:T(1024)(128)(2,1)S(1)}, bf16[1024]{0:T(1024)(128)(2,1)}, u32[]{:S(2)}) copy-start(bf16[1024]{0:T(1024)(128)(2,1)} %get-tuple-element.308) | copy-start | bytes 6148
  1032.5 21.4 %copy-start.48 = (bf16[1024]{0:T(1024)(128)(2,1)S(1)}, bf16[1024]{0:T(1024)(128)(2,1)}, u32[]{:S(2)}) copy-start(bf16[1024]{0:T(1024)(128)(2,1)} %get-tuple-element.310) | copy-start | bytes 6148
  1032.6 43.8 %copy-start.22 = (bf16[2,256,1024]{2,1,0:T(8,128)(2,1)S(1)}, bf16[2,256,1024]{2,1,0:T(8,128)(2,1)}, u32[]{:S(2)}) copy-start(bf16[2,256,1024]{2,1,0:T(8,128)(2,1)} %copy-done.21) | copy-start | bytes 3145732
  (43 other events, 143.1 us)
Sparse Core Ops, SparseCore 0:
  9.6 36.8 all-gather.23
  48.4 36.6 all-gather.13
  87.0 27.8 all-gather.15
  116.6 27.8 all-gather.17
  146.3 27.8 all-gather.19
  175.7 47.4 all-gather.27
  225.0 26.8 all-gather.21
  253.8 54.3 all-gather.25
  310.1 55.9 all-gather.29
  621.4 42.3 reduce-scatter.48
  695.8 40.1 reduce-scatter.46
  739.1 41.2 reduce-scatter.44
  784.6 41.2 reduce-scatter.42
  829.1 51.3 reduce-scatter.24
  884.1 71.2 reduce-scatter.36
  958.8 71.2 reduce-scatter.50
  1032.8 19.5 reduce-scatter.34
  1055.1 17.9 reduce-scatter.32
  1076.1 17.7 reduce-scatter.30
  1096.6 17.9 reduce-scatter.28
  1117.0 19.8 reduce-scatter.26
  1139.3 25.4 reduce-scatter.38
  1167.1 25.7 reduce-scatter.40
where the time goes:
time: 1210 us; the launch traced here: 1200 us
  waiting for transfers between devices  593 us (49%)
  matrix products  205 us (17%)
  blocking collectives  161 us (13%)
  local copies, waits for them, and re-layouts  122 us (10%)
  other arithmetic  83.4 us (7%)
  starting transfers between devices  18 us (1%)
  between operations  15.7 us (1%)
    unnamed x28, waiting for transfers between devices  142 us
    reduce_scatter x1, waiting for transfers between devices, shards(): lax.psum_scatter(up_grad.astype(jnp.bfloat16), 'batch', scatter_dimension...  75 us
    all_to_all x1, waiting for transfers between devices, shards(): lax.all_to_all(grads_heads, 'seq', split_axis=1, concat_axis=3, tiled=True)  60.9 us
    unnamed x115, local copies, waits for them, and re-layouts  56.8 us
    reduce_scatter x1, waiting for transfers between devices, shards(): lax.psum_scatter(skip_w_grad.astype(jnp.bfloat16), 'batch', scatter_dimen...  52.7 us
    all_to_all x1, waiting for transfers between devices, shards(): lax.all_to_all(projected, 'seq', split_axis=3, concat_axis=1, tiled=True)  48.1 us
    all_gather x1, waiting for transfers between devices, shards(): lax.all_gather(value_part, 'batch', axis=0, tiled=True)  29.7 us
    dot_general x4, matrix products, block_scores(): jnp.einsum('iqhd,ikhd->ihqk', query_block, key_heads, preferred_element_t...  29.4 us
  transfers between devices with their start and end apart: 27, of which 17 were waited for; matrix products, arithmetic and copies ran while one was open for 21% of the time, Pallas kernels for 0%

commit v1 on v0

--- a/solution.py
+++ b/solution.py
@@ -1,7 +1,387 @@
+import functools
 import jax
 import jax.numpy as jnp
 from jax import lax
+from jax.experimental import pallas as pl
+from jax.experimental.pallas import tpu as pltpu
+
 from jax.sharding import PartitionSpec as P
+
+MESH = pl.DeviceIdType.MESH
+F32 = jnp.float32
+BF16 = jnp.bfloat16
+
+
+def flip(index, mask):
+    result = index
+    bit = 0
+    while mask >> bit:
+        if (mask >> bit) & 1:
+            on = lax.rem(lax.div(index, 1 << bit), 2)
+            result = result + (1 << bit) * (1 - 2 * on)
+        bit += 1
+    return result
+
+
+def span(bits):
+    masks = [0]
+    for bit in bits:
+        masks = masks + [m | (1 << bit) for m in masks]
+    return masks
+
+
+class Place:
+    def __init__(self, nb, nz):
+        self.nb, self.nz = nb, nz
+        self.b = lax.axis_index("batch")
+        self.z = lax.axis_index("seq")
+        count = nb.bit_length() - 1
+        rest = list(range(1, count))
+        self.rest = rest
+        self.orders = (rest, rest[::-1])
+
+    def at(self, mask):
+        return (flip(self.b, mask), self.z)
+
+    def greet(self, barrier):
+        targets = [self.at(1 << k) for k in [0] + self.rest]
+        for t in targets:
+            pl.semaphore_signal(barrier, inc=1, device_id=t, device_id_type=MESH)
+        for step, ok in ((1, self.z < self.nz - 1), (-1, self.z > 0)):
+            @pl.when(ok)
+            def _():
+                pl.semaphore_signal(
+                    barrier, inc=1, device_id=(self.b, self.z + step), device_id_type=MESH
+                )
+        ends = jnp.where(self.z < self.nz - 1, 1, 0) + jnp.where(self.z > 0, 1, 0)
+        pl.semaphore_wait(barrier, len(targets) + ends)
+
+
+def remote(src, dst, send, recv, device):
+    return pltpu.make_async_remote_copy(
+        src_ref=src, dst_ref=dst, send_sem=send, recv_sem=recv, device_id=device, device_id_type=MESH
+    )
+
+
+class Gather:
+    @staticmethod
+    def sems(nb, nz):
+        count = nb.bit_length() - 1
+        return 2 * (nz - 1) + 2 * (nb // 2 - 1) + nb
+
+    def __init__(self, place, shard, full, local, send, recv):
+        self.p, self.shard, self.full = place, shard, full
+        self.local, self.send, self.recv = local, send, recv
+        self.r, self.c = shard.shape
+        nb, nz = place.nb, place.nz
+        self.xy0 = 2 * (nz - 1)
+        self.core0 = self.xy0 + 2 * (nb // 2 - 1)
+        self.stages = nz + len(place.rest) + 1
+        self.pending = []
+
+    def zcopy(self, way, step):
+        p = self.p
+        n = p.nz
+        sem = (0 if way > 0 else n - 1) + step - 1
+        sent = p.z - way * (step - 1)
+        got = p.z - way * step
+        inside = lambda v: (v >= 0) & (v < n)
+        can_send = inside(sent) & inside(p.z + way)
+        can_get = inside(got)
+        clip = lambda v: jnp.clip(v, 0, n - 1)
+        block = self.full.at[p.b, :, pl.ds(pl.multiple_of(clip(sent) * self.c, self.c), self.c)]
+        src = self.shard if step == 1 else block
+        out = remote(src, block, self.send.at[sem], self.recv.at[sem], (p.b, clip(p.z + way)))
+        land = self.full.at[p.b, :, pl.ds(pl.multiple_of(clip(got) * self.c, self.c), self.c)]
+        into = remote(self.shard, land, self.send.at[sem], self.recv.at[sem], (p.b, clip(p.z + way)))
+        return out, into, can_send, can_get
+
+    def zstart(self, step):
+        for way in (1, -1):
+            out, _, can_send, _ = self.zcopy(way, step)
+            pl.when(can_send)(out.start)
+            self.pending.append((out, can_send))
+
+    def zwait(self, step):
+        for way in (1, -1):
+            _, into, _, can_get = self.zcopy(way, step)
+            pl.when(can_get)(into.wait_recv)
+
+    def rows(self, mask, half):
+        return self.full.at[flip(self.p.b, mask), pl.ds(half * (self.r // 2), self.r // 2)]
+
+    def xycopies(self, j):
+        p = self.p
+        made = []
+        for half in (0, 1):
+            order = p.orders[half]
+            bit = 1 << order[j]
+            for i, m in enumerate(span(order[:j])):
+                sem = self.xy0 + half * (p.nb // 2 - 1) + (1 << j) - 1 + i
+                made.append((half, m | bit, remote(
+                    self.rows(m, half), self.rows(m, half), self.send.at[sem], self.recv.at[sem], p.at(bit)
+                ), remote(
+                    self.rows(m | bit, half), self.rows(m | bit, half), self.send.at[sem], self.recv.at[sem], p.at(bit)
+                )))
+        return made
+
+    def corecopy(self, mask, half):
+        p = self.p
+        sem = self.core0 + (mask >> 1) * 2 + half
+        out = remote(self.rows(mask, half), self.rows(mask, half), self.send.at[sem], self.recv.at[sem], p.at(1))
+        into = remote(self.rows(mask | 1, half), self.rows(mask | 1, half), self.send.at[sem], self.recv.at[sem], p.at(1))
+        return out, into
+
+    def corestart(self, mask, half):
+        out, _ = self.corecopy(mask, half)
+        out.start()
+        self.pending.append((out, None))
+
+    def stage(self, t):
+        p = self.p
+        n = p.nz
+        nx = len(p.rest)
+        if t == 0:
+            mine = self.full.at[p.b, :, pl.ds(pl.multiple_of(p.z * self.c, self.c), self.c)]
+            self.own = pltpu.make_async_copy(self.shard, mine, self.local)
+            self.own.start()
+            if n > 1:
+                self.zstart(1)
+        if 1 <= t <= n - 1:
+            self.zwait(t)
+            if t < n - 1:
+                self.zstart(t + 1)
+        if t == max(n - 1, 0):
+            self.own.wait()
+        j = t - (n - 1)
+        if j >= 1 and j <= nx:
+            for half, m, _, into in self.xycopies(j - 1):
+                into.wait_recv()
+        if 0 <= j < nx:
+            for _, _, out, _ in self.xycopies(j):
+                out.start()
+                self.pending.append((out, None))
+        if j == 0:
+            for half in (0, 1):
+                self.corestart(0, half)
+        if 1 <= j <= nx:
+            for half, m, _, _ in self.xycopies(j - 1):
+                self.corestart(m, half)
+        if j == nx + 1:
+            for m in span(p.rest):
+                for half in (0, 1):
+                    self.corecopy(m, half)[1].wait_recv()
+            for out, ok in self.pending:
+                if ok is None:
+                    out.wait_send()
+                else:
+                    pl.when(ok)(out.wait_send)
+
+
+def gather_kernel(nb, nz, count, lag, *refs):
+    shards, fulls = refs[:count], refs[count:2 * count]
+    local, sends, recvs = refs[2 * count], refs[2 * count + 1:3 * count + 1], refs[3 * count + 1:]
+    place = Place(nb, nz)
+    place.greet(pltpu.get_barrier_semaphore())
+    jobs = [Gather(place, shards[i], fulls[i], local.at[i], sends[i], recvs[i]) for i in range(count)]
+    total = max(lag[i] + jobs[i].stages for i in range(count))
+    for slot in range(total):
+        for i, job in enumerate(jobs):
+            if 0 <= slot - lag[i] < job.stages:
+                job.stage(slot - lag[i])
+
+
+def gather_all(nb, nz, shards, lag, collective_id):
+    count = len(shards)
+    sems = Gather.sems(nb, nz)
+    return pl.pallas_call(
+        functools.partial(gather_kernel, nb, nz, count, lag),
+        out_shape=[jax.ShapeDtypeStruct((nb, s.shape[0], nz * s.shape[1]), BF16) for s in shards],
+        in_specs=[pl.BlockSpec(memory_space=pl.ANY)] * count,
+        out_specs=[pl.BlockSpec(memory_space=pl.ANY)] * count,
+        scratch_shapes=[pltpu.SemaphoreType.DMA((count,))]
+        + [pltpu.SemaphoreType.DMA((sems,))] * (2 * count),
+        compiler_params=pltpu.CompilerParams(collective_id=collective_id, has_side_effects=True),
+    )(*shards)
+
+
+class Scatter:
+    @staticmethod
+    def sems(nb, nz):
+        return nb // 2 + 2 * (nb // 2 - 1) + 2 * (nz - 1)
+
+    @staticmethod
+    def scratch(nb, nz, r, wide):
+        c = wide // nz
+        return [
+            pltpu.VMEM((nb // 2, r, wide), BF16),
+            pltpu.VMEM((nb // 2, r, wide), BF16),
+            pltpu.VMEM((2 * (nb // 2 - 1), r // 2, wide), BF16),
+            pltpu.VMEM((2 * (nz - 1), r, c), BF16),
+            pltpu.SemaphoreType.DMA((nb // 2,)),
+            pltpu.SemaphoreType.DMA((Scatter.sems(nb, nz),)),
+            pltpu.SemaphoreType.DMA((Scatter.sems(nb, nz),)),
+        ]
+
+    def __init__(self, place, full, share, scratch):
+        self.p, self.full, self.share = place, full, share
+        self.sums, self.core, self.plane, self.line, self.local, self.send, self.recv = scratch
+        _, self.r, self.wide = full.shape
+        self.c = self.wide // place.nz
+        self.stages = 1 + 1 + len(place.rest) + (place.nz - 1) + 1
+        self.pending = []
+
+    def start(self, copy, ok=None):
+        if ok is None:
+            copy.start()
+        else:
+            pl.when(ok)(copy.start)
+        self.pending.append((copy, ok))
+
+    def add(self, target, *sources):
+        rows = target.shape[0]
+        step = 16
+        def body(i, carry):
+            at = pl.ds(pl.multiple_of(i * step, step), step)
+            value = target[at].astype(F32)
+            for s in sources:
+                value = value + s[at].astype(F32)
+            target[at] = value.astype(target.dtype)
+            return carry
+        lax.fori_loop(0, rows // step, body, 0)
+
+    def corecopy(self, i, m):
+        p = self.p
+        return remote(self.full.at[flip(p.b, m | 1)], self.core.at[i], self.send.at[i], self.recv.at[i], p.at(1))
+
+    def planecopies(self, j):
+        p = self.p
+        made = []
+        for half in (0, 1):
+            order = p.orders[half]
+            bit = 1 << order[j]
+            at = pl.ds(half * (self.r // 2), self.r // 2)
+            base = half * (p.nb // 2 - 1)
+            for jj in range(j):
+                base += len(span(order[jj + 1:]))
+            for i, m in enumerate(span(order[j + 1:])):
+                slot = base + i
+                sem = p.nb // 2 + slot
+                made.append((half, m, slot, remote(
+                    self.sums.at[(m | bit) >> 1, at], self.plane.at[slot], self.send.at[sem], self.recv.at[sem], p.at(bit)
+                )))
+        return made
+
+    def linecopy(self, way, step):
+        p = self.p
+        n = p.nz
+        here = p.z if way > 0 else n - 1 - p.z
+        goes = n + here - step
+        comes = goes - 1
+        can_send = (goes > here) & (goes <= n - 1)
+        can_get = (comes >= here) & (comes <= n - 1) & (here > 0)
+        unfold = lambda d: jnp.clip(d if way > 0 else n - 1 - d, 0, n - 1)
+        slot = (0 if way > 0 else n - 1) + step - 1
+        sem = p.nb // 2 + 2 * (p.nb // 2 - 1) + slot
+        src = self.sums.at[0, :, pl.ds(pl.multiple_of(unfold(goes) * self.c, self.c), self.c)]
+        copy = remote(src, self.line.at[slot], self.send.at[sem], self.recv.at[sem], (p.b, jnp.clip(p.z + way, 0, n - 1)))
+        return copy, can_send, can_get, unfold(comes), slot
+
+    def stage(self, t):
+        p = self.p
+        n, nx = p.nz, len(p.rest)
+        masks = sorted(span(p.rest))
+        if t == 0:
+            for i, m in enumerate(masks):
+                self.start(self.corecopy(i, m))
+            self.loads = [pltpu.make_async_copy(self.full.at[flip(p.b, m)], self.sums.at[i], self.local.at[i]) for i, m in enumerate(masks)]
+            for load in self.loads:
+                load.start()
+        if t == 1:
+            for i, m in enumerate(masks):
+                self.loads[i].wait()
+                self.corecopy(i, m).wait_recv()
+                self.add(self.sums.at[i], self.core.at[i])
+        j = t - 1
+        if 1 <= j <= nx:
+            for half, m, slot, copy in self.planecopies(j - 1):
+                copy.wait_recv()
+                self.add(self.sums.at[m >> 1, pl.ds(half * (self.r // 2), self.r // 2)], self.plane.at[slot])
+        if 0 <= j < nx:
+            for half, m, slot, copy in self.planecopies(j):
+                self.start(copy)
+        s = t - 1 - nx
+        if 1 <= s <= n - 1:
+            for way in (1, -1):
+                copy, can_send, can_get, place, slot = self.linecopy(way, s)
+                @pl.when(can_get)
+                def _():
+                    copy.wait_recv()
+                    if s < n - 1:
+                        self.add(self.sums.at[0, :, pl.ds(pl.multiple_of(place * self.c, self.c), self.c)], self.line.at[slot])
+        if 0 <= s < n - 1:
+            for way in (1, -1):
+                copy, can_send, can_get, place, slot = self.linecopy(way, s + 1)
+                self.start(copy, can_send)
+        if t == self.stages - 1:
+            self.finish()
+
+    def finish(self):
+        p = self.p
+        n = p.nz
+        mine = pl.ds(pl.multiple_of(p.z * self.c, self.c), self.c)
+        step = 16
+        def body(i, carry):
+            at = pl.ds(pl.multiple_of(i * step, step), step)
+            self.share[at] = self.sums[0, at, mine].astype(F32)
+            return carry
+        lax.fori_loop(0, self.r // step, body, 0)
+        for way, ok in ((1, p.z > 0), (-1, p.z < n - 1)):
+            slot = (0 if way > 0 else n - 1) + n - 2
+            @pl.when(ok)
+            def _():
+                def more(i, carry):
+                    at = pl.ds(pl.multiple_of(i * step, step), step)
+                    self.share[at] = self.share[at] + self.line[slot, at].astype(F32)
+                    return carry
+                lax.fori_loop(0, self.r // step, more, 0)
+        for copy, ok in self.pending:
+            if ok is None:
+                copy.wait_send()
+            else:
+                pl.when(ok)(copy.wait_send)
+
+
+def scatter_kernel(nb, nz, count, lag, *refs):
+    fulls, shares = refs[:count], refs[count:2 * count]
+    scratch = refs[2 * count:]
+    per = len(scratch) // count
+    place = Place(nb, nz)
+    place.greet(pltpu.get_barrier_semaphore())
+    jobs = [Scatter(place, fulls[i], shares[i], scratch[i * per:(i + 1) * per]) for i in range(count)]
+    total = max(lag[i] + jobs[i].stages for i in range(count))
+    for slot in range(total):
+        for i, job in enumerate(jobs):
+            if 0 <= slot - lag[i] < job.stages:
+                job.stage(slot - lag[i])
+
+
+def scatter_all(nb, nz, fulls, lag, collective_id):
+    count = len(fulls)
+    scratch = []
+    for f in fulls:
+        scratch += Scatter.scratch(nb, nz, f.shape[1], f.shape[2])
+    return pl.pallas_call(
+        functools.partial(scatter_kernel, nb, nz, count, lag),
+        out_shape=[jax.ShapeDtypeStruct((f.shape[1], f.shape[2] // nz), F32) for f in fulls],
+        in_specs=[pl.BlockSpec(memory_space=pl.ANY)] * count,
+        out_specs=[pl.BlockSpec(memory_space=pltpu.VMEM)] * count,
+        scratch_shapes=scratch,
+        compiler_params=pltpu.CompilerParams(
+            collective_id=collective_id, has_side_effects=True, vmem_limit_bytes=60 * 2**20
+        ),
+    )(*fulls)
+
 
 HEADS = 16
 HEAD_DIM = 64
@@ -52,40 +432,20 @@
     second_shift,
     cotangent,
 ):
-    (
-        skip_part,
-        query_part,
-        key_part,
-        value_part,
-        out_part,
-        up_part,
-        down_part,
-        gain_one,
-        shift_one,
-        gain_two,
-        shift_two,
-    ) = (
-        lax.all_gather(skip_weight, "seq", axis=1, tiled=True),
-        lax.all_gather(query_weight, "seq", axis=1, tiled=True),
-        lax.all_gather(key_weight, "seq", axis=1, tiled=True),
-        lax.all_gather(value_weight, "seq", axis=1, tiled=True),
-        lax.all_gather(out_weight, "seq", axis=0, tiled=True),
-        lax.all_gather(up_weight, "seq", axis=1, tiled=True),
-        lax.all_gather(down_weight, "seq", axis=0, tiled=True),
-        lax.all_gather(first_gain, "seq", axis=0, tiled=True),
-        lax.all_gather(first_shift, "seq", axis=0, tiled=True),
-        lax.all_gather(second_gain, "seq", axis=0, tiled=True),
-        lax.all_gather(second_shift, "seq", axis=0, tiled=True),
-    )
-    skip_full, query_full, key_full, value_full, out_full, up_full, down_full = (
-        lax.all_gather(skip_part, "batch", axis=0, tiled=True),
-        lax.all_gather(query_part, "batch", axis=0, tiled=True),
-        lax.all_gather(key_part, "batch", axis=0, tiled=True),
-        lax.all_gather(value_part, "batch", axis=0, tiled=True),
-        lax.all_gather(out_part, "batch", axis=1, tiled=True),
-        lax.all_gather(up_part, "batch", axis=0, tiled=True),
-        lax.all_gather(down_part, "batch", axis=1, tiled=True),
-    )
+    gain_one, shift_one, gain_two, shift_two = (
+        lax.all_gather(jnp.stack([first_gain, first_shift, second_gain, second_shift]), "seq", axis=1, tiled=True)
+    )
+    nb, nz = lax.axis_size("batch"), lax.axis_size("seq")
+    mix_shard = jnp.concatenate([query_weight, key_weight, value_weight, out_weight.T], 1)
+    skip_full, mix_full, up_full, down_t = gather_all(
+        nb, nz, [skip_weight, mix_shard, up_weight, down_weight.T], (0, 2, 4, 6), 0
+    )
+    flat = lambda w: w.reshape(w.shape[0] * w.shape[1], w.shape[2])
+    skip_full, up_full, down_t = flat(skip_full), flat(up_full), flat(down_t)
+    width = query_weight.shape[1]
+    split = flat(mix_full).reshape(-1, nz, 4, width)
+    pick = lambda i: split[:, :, i].reshape(-1, nz * width)
+    query_full, key_full, value_full, out_t = lax.optimization_barrier((pick(0), pick(1), pick(2), pick(3)))
     gain_first = gain_one.astype(jnp.float32)
     shift_first = shift_one.astype(jnp.float32)
     gain_second = gain_two.astype(jnp.float32)
@@ -128,19 +488,19 @@
 
     block_outputs, logsum = lax.map(forward_block, jnp.arange(block_count))
     attended = jnp.moveaxis(block_outputs, 0, 1).reshape(item_count, frames, local_width)
-    attended_frames = lax.all_to_all(attended, "seq", split_axis=1, concat_axis=2, tiled=True)
+    attended_frames = lax.optimization_barrier(lax.all_to_all(attended, "seq", split_axis=1, concat_axis=2, tiled=True))
     middle = mixed_stream + jnp.einsum(
-        "ifd,de->ife", attended_frames, out_full, preferred_element_type=jnp.float32
+        "ifd,ed->ife", attended_frames, out_t, preferred_element_type=jnp.float32
     )
     ffn_input = layer_norm(middle, gain_second, shift_second).astype(jnp.bfloat16)
     hidden = jnp.einsum("ifd,dk->ifk", ffn_input, up_full, preferred_element_type=jnp.float32)
     active = gelu_exact(hidden).astype(jnp.bfloat16)
     output = (
-        middle + jnp.einsum("ifk,kd->ifd", active, down_full, preferred_element_type=jnp.float32)
+        middle + jnp.einsum("ifk,dk->ifd", active, down_t, preferred_element_type=jnp.float32)
     ).astype(jnp.bfloat16)
-    down_grad = jnp.einsum("ifk,ifd->kd", active, cotangent, preferred_element_type=jnp.float32)
+    down_grad = jnp.einsum("ifd,ifk->dk", cotangent, active, preferred_element_type=jnp.float32)
     active_grad = jnp.einsum(
-        "ifd,kd->ifk", cotangent, down_full, preferred_element_type=jnp.float32
+        "ifd,dk->ifk", cotangent, down_t, preferred_element_type=jnp.float32
     )
     hidden_grad = jax.vjp(gelu_exact, hidden)[1](active_grad)[0].astype(jnp.bfloat16)
     up_grad = jnp.einsum("ifd,ifk->dk", ffn_input, hidden_grad, preferred_element_type=jnp.float32)
@@ -152,11 +512,11 @@
     middle_grad = cotangent.astype(jnp.float32) + middle_part
     middle_low = middle_grad.astype(jnp.bfloat16)
     out_grad = jnp.einsum(
-        "ifd,ife->de", attended_frames, middle_low, preferred_element_type=jnp.float32
-    )
-    attended_grad = jnp.einsum(
-        "ife,de->ifd", middle_low, out_full, preferred_element_type=jnp.float32
-    ).astype(jnp.bfloat16)
+        "ifd,ife->ed", attended_frames, middle_low, preferred_element_type=jnp.float32
+    )
+    attended_grad = lax.optimization_barrier(jnp.einsum(
+        "ife,ed->ifd", middle_low, out_t, preferred_element_type=jnp.float32
+    ).astype(jnp.bfloat16))
     heads_grad = lax.all_to_all(
         attended_grad, "seq", split_axis=2, concat_axis=1, tiled=True
     ).reshape(head_shape)
@@ -200,7 +560,7 @@
     key_grad_low = key_grad.reshape(item_count, frames, local_width).astype(jnp.bfloat16)
     value_grad_low = value_grad.reshape(item_count, frames, local_width).astype(jnp.bfloat16)
     grads_heads = jnp.stack([query_grad, key_grad_low, value_grad_low], 2)
-    grads_frames = lax.all_to_all(grads_heads, "seq", split_axis=1, concat_axis=3, tiled=True)
+    grads_frames = lax.optimization_barrier(lax.all_to_all(grads_heads, "seq", split_axis=1, concat_axis=3, tiled=True))
     qkv_grad = jnp.einsum("ifd,ifce->cde", normed, grads_frames, preferred_element_type=jnp.float32)
     normed_grad = jnp.einsum(
         "ifce,cde->ifd", grads_frames, stacked, preferred_element_type=jnp.float32
@@ -215,78 +575,21 @@
     model_width = mixed_stream.shape[2]
     input_grad = joined_grad[:, :, :model_width]
     skip_grad = joined_grad[:, :, model_width:]
-    skip_share, query_share, key_share, value_share, out_share, up_share, down_share = (
-        lax.psum_scatter(
-            skip_w_grad.astype(jnp.bfloat16), "batch", scatter_dimension=0, tiled=True
-        ).astype(jnp.float32),
-        lax.psum_scatter(
-            qkv_grad[0].astype(jnp.bfloat16), "batch", scatter_dimension=0, tiled=True
-        ).astype(jnp.float32),
-        lax.psum_scatter(
-            qkv_grad[1].astype(jnp.bfloat16), "batch", scatter_dimension=0, tiled=True
-        ).astype(jnp.float32),
-        lax.psum_scatter(
-            qkv_grad[2].astype(jnp.bfloat16), "batch", scatter_dimension=0, tiled=True
-        ).astype(jnp.float32),
-        lax.psum_scatter(
-            out_grad.astype(jnp.bfloat16), "batch", scatter_dimension=1, tiled=True
-        ).astype(jnp.float32),
-        lax.psum_scatter(
-            up_grad.astype(jnp.bfloat16), "batch", scatter_dimension=0, tiled=True
-        ).astype(jnp.float32),
-        lax.psum_scatter(
-            down_grad.astype(jnp.bfloat16), "batch", scatter_dimension=1, tiled=True
-        ).astype(jnp.float32),
-    )
-    (
-        skip_share,
-        query_share,
-        key_share,
-        value_share,
-        out_share,
-        up_share,
-        down_share,
-        gain_one_grad,
-        shift_one_grad,
-        gain_two_grad,
-        shift_two_grad,
-    ) = (
-        lax.psum_scatter(
-            skip_share.astype(jnp.bfloat16), "seq", scatter_dimension=1, tiled=True
-        ).astype(jnp.float32),
-        lax.psum_scatter(
-            query_share.astype(jnp.bfloat16), "seq", scatter_dimension=1, tiled=True
-        ).astype(jnp.float32),
-        lax.psum_scatter(
-            key_share.astype(jnp.bfloat16), "seq", scatter_dimension=1, tiled=True
-        ).astype(jnp.float32),
-        lax.psum_scatter(
-            value_share.astype(jnp.bfloat16), "seq", scatter_dimension=1, tiled=True
-        ).astype(jnp.float32),
-        lax.psum_scatter(
-            out_share.astype(jnp.bfloat16), "seq", scatter_dimension=0, tiled=True
-        ).astype(jnp.float32),
-        lax.psum_scatter(
-            up_share.astype(jnp.bfloat16), "seq", scatter_dimension=1, tiled=True
-        ).astype(jnp.float32),
-        lax.psum_scatter(
-            down_share.astype(jnp.bfloat16), "seq", scatter_dimension=0, tiled=True
-        ).astype(jnp.float32),
-        lax.psum_scatter(
-            gain_first_grad.astype(jnp.bfloat16), "seq", scatter_dimension=0, tiled=True
-        ).astype(jnp.float32),
-        lax.psum_scatter(
-            shift_first_grad.astype(jnp.bfloat16), "seq", scatter_dimension=0, tiled=True
-        ).astype(jnp.float32),
-        lax.psum_scatter(
-            gain_second_grad.astype(jnp.bfloat16), "seq", scatter_dimension=0, tiled=True
-        ).astype(jnp.float32),
-        lax.psum_scatter(
-            shift_second_grad.astype(jnp.bfloat16), "seq", scatter_dimension=0, tiled=True
-        ).astype(jnp.float32),
-    )
-    gain_one_grad, shift_one_grad, gain_two_grad, shift_two_grad = lax.psum(
-        (gain_one_grad, shift_one_grad, gain_two_grad, shift_two_grad), "batch"
+    mix_grad = jnp.concatenate([qkv_grad, out_grad[None]], 0)
+    mix_grad = mix_grad.reshape(4, -1, nz, width).transpose(1, 2, 0, 3).reshape(-1, nz * 4 * width)
+    blocked = lambda g: g.astype(jnp.bfloat16).reshape(nb, g.shape[0] // nb, g.shape[1])
+    down_share, up_share, mix_share, skip_share = scatter_all(
+        nb, nz, [blocked(down_grad), blocked(up_grad), blocked(mix_grad), blocked(skip_w_grad)], (0, 1, 2, 3), 1
+    )
+    down_share = down_share.T
+    query_share, key_share, value_share, out_share = [
+        mix_share[:, i * width : (i + 1) * width] for i in range(4)
+    ]
+    out_share = out_share.T
+    norm_grads = jnp.stack([gain_first_grad, shift_first_grad, gain_second_grad, shift_second_grad])
+    norm_grads = lax.psum(norm_grads, ("batch", "seq"))
+    gain_one_grad, shift_one_grad, gain_two_grad, shift_two_grad = lax.dynamic_slice_in_dim(
+        norm_grads, lax.axis_index("seq") * width, width, 1
     )
     return (
         output,

time: 1210 us -> 1050 us (0.87)
  waiting for transfers between devices: 593 us -> 126 us
  Pallas kernels: 0 us -> 303 us
  local copies, waits for them, and re-layouts: 122 us -> 213 us
  blocking collectives: 161 us -> 80.2 us
  other arithmetic: 83.4 us -> 98.6 us
  between operations: 15.7 us -> 1.45 us
    pallas_call x0 -> x2, Pallas kernels: none -> 303 us  [the longest x1 157 us: scatter_all(): pl.pallas_call(functools.partial(scatter_kernel, nb, nz, count, lag), out...]
    reduce_scatter x9 -> x0, waiting for transfers between devices: 238 us -> none  [the longest x1 75 us: shards(): lax.psum_scatter(up_grad.astype(jnp.bfloat16), 'batch', scatter_dimension...]
    unnamed x28 -> x0, waiting for transfers between devices: 142 us -> none
    all_gather x9 -> x1, blocking collectives: 139 us -> 11.9 us  [shards(): lax.all_gather(jnp.stack([first_gain, first_shift, second_gain, second_sh...]
    all_gather x9 -> x0, waiting for transfers between devices: 81.4 us -> none  [the longest x1 29.7 us: shards(): lax.all_gather(value_part, 'batch', axis=0, tiled=True)]
    all_to_all x1, waiting for transfers between devices: 60.9 us -> 32 us  [shards(): lax.all_to_all(grads_heads, 'seq', split_axis=1, concat_axis=3, tiled=True)]
    all_to_all x0 -> x1, blocking collectives: none -> 28.1 us  [shards(): lax.all_to_all(attended, 'seq', split_axis=1, concat_axis=2, tiled=True)]
    psum x1, blocking collectives: 13.1 us -> 40.3 us  [shards(): norm_grads = lax.psum(norm_grads, ('batch', 'seq'))]
  transfers between devices with their start and end apart: 27 -> 3, of which waited for: 17 -> 3; matrix products, arithmetic and copies ran while one was open for 21% -> 4% of each run, Pallas kernels for 0% -> 0%
where the time goes in v1:
time: 1050 us; the launch traced here: 1040 us
  Pallas kernels  303 us (29%)
  local copies, waits for them, and re-layouts  213 us (20%)
  matrix products  205 us (20%)
  waiting for transfers between devices  126 us (12%)
  other arithmetic  98.6 us (9%)
  blocking collectives  80.2 us (8%)
  starting transfers between devices  12.9 us (1%)
    pallas_call x1, Pallas kernels, scatter_all(): pl.pallas_call(functools.partial(scatter_kernel, nb, nz, count, lag), out...  157 us
    pallas_call x1, Pallas kernels, gather_all(): pl.pallas_call(functools.partial(gather_kernel, nb, nz, count, lag), out_...  145 us
    all_to_all x1, waiting for transfers between devices, shards(): lax.all_to_all(projected, 'seq', split_axis=3, concat_axis=1, tiled=True)  68.9 us
    unnamed x115, local copies, waits for them, and re-layouts  57.1 us
    psum x1, blocking collectives, shards(): norm_grads = lax.psum(norm_grads, ('batch', 'seq'))  40.3 us
    dot_general x4, matrix products, block_scores(): jnp.einsum('iqhd,ikhd->ihqk', query_block, key_heads, preferred_element_t...  39.6 us
    all_to_all x1, waiting for transfers between devices, shards(): lax.all_to_all(grads_heads, 'seq', split_axis=1, concat_axis=3, tiled=True)  32 us
    all_to_all x1, blocking collectives, shards(): lax.all_to_all(attended, 'seq', split_axis=1, concat_axis=2, tiled=True)  28.1 us
  transfers between devices with their start and end apart: 3, of which 3 were waited for; matrix products, arithmetic and copies ran while one was open for 4% of the time, Pallas kernels for 0%

profile of v1, /device:TPU:0, one launch (start us, length us, event | category | flops | bytes accessed | tf_op | source)
XLA Modules:
  0.0 1041.9 jit_solution(10139763763102270026)
XLA Ops:
  7.3 145.4 %shard_map.254 = (bf16[8,256,1024]{2,1,0:T(8,128)(2,1)}, bf16[8,128,4096]{2,1,0:T(8,128)(2,1)}, bf16[8,128,4096]{2,1,0:T(8,128)(2,1)}, bf16[8,128,4096]{2,1,0:T(8,128)(2,1)}) custom-call(bf16[256,256]{1,0:T(8,128)(2,1)} %refs_0_.1, bf16[128,1024]{1,0:T(8,128)(2,1)} %pad_maximum_fusion.4.refs_1_, bf16[128,1024]{1,0:T(8,128)(2,1)} %refs_2_.1, ...), custom_call_target="tpu_custom_call" | custom-call | tf_op jit(solution)/shard_map/pallas_call | solution.py:197
  152.6 14.6 %reshape_reshape.3 = bf16[1024,4,4,256]{3,2,1,0:T(4,128)(2,1)} reshape(bf16[8,128,4096]{2,1,0:T(8,128)(2,1)} %get-tuple-element.139) | data formatting | bytes 16777216 | tf_op jit(solution)/shard_map/reshape;reshape | solution.py:446
  167.3 27.0 %fusion.79 = (bf16[1024,4,1,256]{3,2,1,0:T(2,128)(2,1)}, bf16[1024,4,1,256]{3,2,1,0:T(2,128)(2,1)}, bf16[1024,4,1,256]{3,2,1,0:T(2,128)(2,1)}, bf16[1024,4,1,256]{3,2,1,0:T(2,128)(2,1)}) fusion(bf16[1024,4,4,256]{3,2,1,0:T(4,128)(2,1)} %reshape_reshape.3), kind=kLoop, calls=%fused_computation.147 | loop fusion | bytes 16777216 | tf_op jit(solution)/shard_map/slice | solution.py:447
  194.2 9.0 copy.236
  203.2 10.6 %copy.237 = bf16[1024,4,1,256]{0,3,1,2:T(8,128)(2,1)} copy(bf16[1024,4,1,256]{3,2,1,0:T(2,128)(2,1)} %get-tuple-element.388) | data formatting | bytes 4194304
  213.9 10.5 %copy.238 = bf16[1024,4,1,256]{0,3,1,2:T(8,128)(2,1)} copy(bf16[1024,4,1,256]{3,2,1,0:T(2,128)(2,1)} %get-tuple-element.387) | data formatting | bytes 4194304
  224.4 10.6 %copy.239 = bf16[1024,4,1,256]{0,3,1,2:T(8,128)(2,1)} copy(bf16[1024,4,1,256]{3,2,1,0:T(2,128)(2,1)} %get-tuple-element.386) | data formatting | bytes 4194304
  245.6 11.9 %all_gather.3 = bf16[4,1024]{1,0:T(4,128)(2,1)S(1)} all-gather(bf16[4,256]{1,0:T(4,128)(2,1)S(1)} %pad_maximum_fusion.6), channel_id=1, replica_groups=mesh['batch'=8,'seq'=4] {'seq'}, dimensions={1}, use_global_device_ids=true | all-gather | bytes 10240 | tf_op jit(solution)/shard_map/all_gather | solution.py:436
  259.1 5.4 fusion.83
  269.5 5.8 copy.191
  279.2 68.9 %all-to-all-done = bf16[2,256,3,1024]{1,0,2,3:T(2,128)(2,1)S(1)} async-done(((bf16[2,256,3,1024]{1,0,2,3:T(2,128)(2,1)}), bf16[2,256,3,1024]{1,0,2,3:T(2,128)(2,1)S(1)}, u32[]{:S(2)}, u32[]{:S(2)}) %all-to-all-start) | async-done | bytes 3145760 | tf_op jit(solution)/shard_map/all_to_all | solution.py:460
  361.2 70.7 %while.28 = (s32[]{:T(128)}, bf16[2,2,512,4,64]{2,4,3,1,0:T(8,128)(2,1)S(1)}, f32[2,2,4,512]{3,2,1,0:T(4,128)S(1)}, s32[2]{0:T(128)S(1)}, bf16[2,1024,4,64]{1,3,...) while((s32[]{:T(128)}, ...), condition=%wide.region_5.6_spmd.clone, body=%wide.region_2.5_spmd.clone.sunk | while | flops 1140064256 | bytes 124934416 | solution.py:489
  367.2 12.8 %fusion.132 = (f32[2,4,512]{2,1,0:T(4,128)S(1)}, f32[2,4,512,1024]{3,2,1,0:T(8,128)}) fusion(f32[4,512,1024]{2,1,0:T(8,128)} %broadcast_multiply_fusion.6, pred[2,1024]{1,0:T(4,128)(4,1)S(1)} %iota_compare_fusion.4, bf16[2,1024,4,64]{1,3,2,0:T(8,128)(2,1)} %get-tuple-element.582, bf16[2,1024,4,64]{1,3,2,0:T(8,128)(2,1)} %get-tuple-element.581, ...), kind=kOutput, calls=%fused_computation.8.clone.1 | convolution fusion | flops 553644032 | bytes 26757124 | tf_op jit(solution)/shard_map/while/body/eval_jaxpr/iqhd,ikhd->ihqk/dot_general | solution.py:408
  379.9 8.2 fusion.133
  388.1 8.4 fusion.134
  402.5 12.8 %fusion.132 = (f32[2,4,512]{2,1,0:T(4,128)S(1)}, f32[2,4,512,1024]{3,2,1,0:T(8,128)}) fusion(f32[4,512,1024]{2,1,0:T(8,128)} %broadcast_multiply_fusion.6, pred[2,1024]{1,0:T(4,128)(4,1)S(1)} %iota_compare_fusion.4, bf16[2,1024,4,64]{1,3,2,0:T(8,128)(2,1)} %get-tuple-element.582, bf16[2,1024,4,64]{1,3,2,0:T(8,128)(2,1)} %get-tuple-element.581, ...), kind=kOutput, calls=%fused_computation.8.clone.1 | convolution fusion | flops 553644032 | bytes 26757124 | tf_op jit(solution)/shard_map/while/body/eval_jaxpr/iqhd,ikhd->ihqk/dot_general | solution.py:408
  415.3 8.2 fusion.133
  423.4 8.4 fusion.134
  438.8 28.1 %all_to_all.69 = bf16[2,1024,256]{2,0,1:T(2,128)(2,1)S(1)} all-to-all(bf16[2,1024,256]{2,0,1:T(2,128)(2,1)S(1)} %reshape.326), channel_id=1, replica_groups=mesh['batch'=8,'seq'=4] {'seq'}, dimensions={1} | all-to-all | bytes 2097152 | tf_op jit(solution)/shard_map/all_to_all | solution.py:491
  472.1 10.3 fusion.61
  482.4 20.1 %multiply_convert_fusion.1 = (bf16[2,256,4096]{2,1,0:T(8,128)(2,1)}, f32[2,256,4096]{2,1,0:T(8,128)}) fusion(f32[2,256,4096]{2,1,0:T(8,128)S(1)} %get-tuple-element.411, u8[256,4096]{1,0:T(8,128)(4,1)S(1)} %get-tuple-element.329, u8[256,4096]{1,0:T(8,128)(4,1)S(1)} %get-tuple-element.328), kind=kLoop, calls=%fused_computation.73 | loop fusion | flops 146800640 | bytes 23068672 | tf_op jit(solution)/shard_map/convert_element_type | solution.py:497
  502.5 14.1 %fusion.41 = bf16[2,256,4096]{2,1,0:T(8,128)(2,1)} fusion(f32[2,256,4096]{2,1,0:T(8,128)} %get-tuple-element.381, f32[2,256,4096]{2,1,0:T(8,128)S(1)} %get-tuple-element.411, bf16[1024,4096,1]{1,0,2:T(8,128)(2,1)} %bitcast.282, bf16[2,256,1024]{2,1,0:T(8,128)(2,1)S(1)} %copy-done.11), kind=kOutput, calls=%fused_computation.71 | convolution fusion | flops 4324327424 | bytes 30408704 | tf_op jit(solution)/shard_map/ifd,dk->ifk/dot_general | solution.py:502
  516.7 9.3 multiply_reduce_fusion.1
  536.6 24.7 %all-to-all-done.2 = bf16[2,256,1024]{1,0,2:T(2,128)(2,1)S(1)} async-done(((bf16[2,256,1024]{1,0,2:T(2,128)(2,1)}), bf16[2,256,1024]{1,0,2:T(2,128)(2,1)S(1)}, u32[]{:S(2)}, u32[]{:S(2)}) %all-to-all-start.2) | async-done | bytes 1048608 | tf_op jit(solution)/shard_map/all_to_all | solution.py:520
  564.8 105.2 %while.29 = (s32[]{:T(128)}, f32[2,1024,4,64]{1,3,2,0:T(8,128)}, f32[2,1024,4,64]{1,3,2,0:T(8,128)}, bf16[2,2,512,4,64]{2,4,3,1,0:T(8,128)(2,1)}, s32[2]{0:T(128...) while((s32[]{:T(128)}, f32[2,1024,4,64]{1,3,2,0:T(8,128)}, ...), condition=%wide.region_12.13_spmd.clone, body=%wide.region_10.12_spmd.clone.sunk | while | flops 2732589056 | bytes 320438688 | solution.py:556
  570.7 7.0 subtract_exponential_fusion.3
  577.8 10.9 %multiply_reduce_fusion.7 = (f32[2,4,512]{2,1,0:T(4,128)S(1)}, f32[2,4,512,1024]{3,2,1,0:T(8,128)}) fusion(f32[2,4,512,1024]{3,2,1,0:T(8,128)S(1)} %subtract_exponential_fusion.3, bf16[2,1024,4,64]{1,3,2,0:T(8,128)(2,1)} %get-tuple-element.631, bf16[2,1024,4,64]{1,3,2,0:T(8,128)(2,1)} %get-tuple-element.630, s32[]{:T(128)S(6)} %select_n.48), kind=kOutput, calls=%fused_computation.26.clone.1 | convolution fusion | flops 545255424 | bytes 35143684 | tf_op jit(solution)/shard_map/while/body/eval_jaxpr/iqhd,ikhd->ihqk/dot_general | solution.py:537
  588.9 9.9 multiply_convert_fusion.3
  598.8 6.6 bitcast_add_fusion.4
  622.7 7.0 subtract_exponential_fusion.3
  629.8 10.9 %multiply_reduce_fusion.7 = (f32[2,4,512]{2,1,0:T(4,128)S(1)}, f32[2,4,512,1024]{3,2,1,0:T(8,128)}) fusion(f32[2,4,512,1024]{3,2,1,0:T(8,128)S(1)} %subtract_exponential_fusion.3, bf16[2,1024,4,64]{1,3,2,0:T(8,128)(2,1)} %get-tuple-element.631, bf16[2,1024,4,64]{1,3,2,0:T(8,128)(2,1)} %get-tuple-element.630, s32[]{:T(128)S(6)} %select_n.48), kind=kOutput, calls=%fused_computation.26.clone.1 | convolution fusion | flops 545255424 | bytes 35143684 | tf_op jit(solution)/shard_map/while/body/eval_jaxpr/iqhd,ikhd->ihqk/dot_general | solution.py:537
  640.9 9.9 multiply_convert_fusion.3
  650.8 7.2 bitcast_add_fusion.4
  678.9 5.9 copy.209
  684.8 5.3 all-to-all-start.3
  692.7 11.0 %copy.215 = bf16[1,1024,4,256]{3,0,2,1:T(2,128)(2,1)} copy(bf16[1,1024,4,256]{1,3,2,0:T(8,128)(2,1)} %bitcast.249) | data formatting | bytes 4194304 | tf_op jit(solution)/shard_map/concatenate | solution.py:578
  703.7 10.3 add_convert_fusion.3
  714.0 7.2 bitcast_convert_fusion
  721.3 7.0 bitcast_convert_fusion.1
  728.2 32.0 %all-to-all-done.3 = bf16[2,1024,3,256]{3,0,2,1:T(2,128)(2,1)} async-done(((bf16[2,1024,3,256]{3,0,2,1:T(2,128)(2,1)}), bf16[2,1024,3,256]{3,0,2,1:T(2,128)(2,1)}, u32[]{:S(2)}, u32[]{:S(2)}) %all-to-all-start.3) | async-done | bytes 3145760 | tf_op jit(solution)/shard_map/all_to_all | solution.py:563
  760.3 8.6 copy.210
  768.9 7.2 multiply_reduce_fusion.2
  776.2 5.9 bitcast_convert_fusion.2
  795.3 14.4 %copy.214 = bf16[3,1024,4,256]{3,0,2,1:T(4,128)(2,1)} copy(bf16[3,1024,4,256]{1,3,2,0:T(8,128)(2,1)} %bitcast.237) | data formatting | bytes 12582912 | tf_op jit(solution)/shard_map/concatenate | solution.py:578
  809.7 11.2 %maximum_bitcast_fusion = bf16[1024,4,4,256]{3,2,1,0:T(4,128)(2,1)} fusion(bf16[1,1024,4,256]{3,0,2,1:T(2,128)(2,1)} %copy.215, bf16[3,1024,4,256]{3,0,2,1:T(4,128)(2,1)} %copy.214), kind=kLoop, calls=%fused_computation.62 | loop fusion | flops 16777216 | bytes 16777216 | tf_op jit(solution)/shard_map/convert_element_type | solution.py:580
  821.0 14.4 %convert_element_type.195.refs_2_ = bf16[8,128,4096]{2,1,0:T(8,128)(2,1)} reshape(bf16[1024,4,4,256]{3,2,1,0:T(4,128)(2,1)} %maximum_bitcast_fusion) | data formatting | bytes 16777216 | tf_op jit(solution)/shard_map/convert_element_type | solution.py:580
  835.3 157.3 %shard_map.255 = (f32[128,1024]{1,0:T(8,128)}, f32[128,1024]{1,0:T(8,128)}, f32[128,1024]{1,0:T(8,128)}, f32[256,256]{1,0:T(8,128)}) custom-call(bf16[8,128,4096]{2,1,0:T(8,128)(2,1)} %bitcast.233, bf16[8,128,4096]{2,1,0:T(8,128)(2,1)} %bitcast.232, bf16[8,128,4096]{2,1,0:T(8,128)(2,1)} %convert_element_type.195.refs_2_, bf16[8,256,1024]{2,1,0:T(8,128)(2,1)} %bitcast.238), custom_call_target="tpu_custom_call" | custom-call | tf_op jit(solution)/shard_map/pallas_call | solution.py:374
  997.3 40.3 %psum.7 = f32[4,1024]{1,0:T(4,128)S(1)} all-reduce(f32[4,1024]{1,0:T(4,128)S(1)} %pad_maximum_fusion.5), channel_id=1, replica_groups=mesh['batch'=8,'seq'=4] {'batch','seq'}, use_global_device_ids=true, to_apply=%region_19.20 | all-reduce | flops 4096 | bytes 32768 | tf_op jit(solution)/shard_map/psum | solution.py:590
  (231 shorter events, 145.3 us)
Async XLA Ops:
  238.9 6.6 copy-start.50
  238.9 6.6 copy-start.51
  238.9 6.6 copy-start.52
  238.9 6.7 copy-start.53
  238.9 19.2 %copy-start.21 = (bf16[2,256,1024]{2,1,0:T(8,128)(2,1)S(1)}, bf16[2,256,1024]{2,1,0:T(8,128)(2,1)}, u32[]{:S(2)}) copy-start(bf16[2,256,1024]{2,1,0:T(8,128)(2,1)} %param.20) | copy-start | bytes 3145732
  258.1 7.7 copy-start.27
  258.1 7.7 copy-start.43
  259.1 6.7 copy-start.18
  259.1 6.7 copy-start.19
  259.1 6.7 copy-start.20
  275.3 72.8 %all-to-all-start = ((bf16[2,256,3,1024]{1,0,2,3:T(2,128)(2,1)}), bf16[2,256,3,1024]{1,0,2,3:T(2,128)(2,1)S(1)}, u32[]{:S(2)}, u32[]{:S(2)}) async-start(bf16[2,256,3,1024]{1,0,2,3:T(2,128)(2,1)} %copy.191), calls=%async_computation | async-start | bytes 6291456 | tf_op jit(solution)/shard_map/all_to_all | solution.py:460
  355.1 4.7 copy-start.14
  355.1 6.1 copy-start.26
  367.2 12.8 %copy-start.2 = (f32[4,512,1024]{2,1,0:T(8,128)S(1)}, f32[4,512,1024]{2,1,0:T(8,128)}, u32[]{:S(2)}) copy-start(f32[4,512,1024]{2,1,0:T(8,128)} %broadcast_multiply_fusion.6) | copy-start | bytes 25165828 | tf_op jit(solution)/shard_map/while
  402.5 12.8 %copy-start.2 = (f32[4,512,1024]{2,1,0:T(8,128)S(1)}, f32[4,512,1024]{2,1,0:T(8,128)}, u32[]{:S(2)}) copy-start(f32[4,512,1024]{2,1,0:T(8,128)} %broadcast_multiply_fusion.6) | copy-start | bytes 25165828 | tf_op jit(solution)/shard_map/while
  434.5 33.9 %copy-start.5 = (f32[2,256,1024]{2,1,0:T(8,128)S(1)}, f32[2,256,1024]{2,1,0:T(8,128)}, u32[]{:S(2)}) copy-start(f32[2,256,1024]{2,1,0:T(8,128)} %copy-done.4) | copy-start | bytes 6291460
  471.6 54.4 %copy-start.9 = (f32[2,256,1024]{2,1,0:T(8,128)}, f32[2,256,1024]{2,1,0:T(8,128)S(1)}, u32[]{:S(2)}) copy-start(f32[2,256,1024]{2,1,0:T(8,128)S(1)} %get-tuple-element.410) | copy-start | bytes 6291460
  471.7 54.4 %copy-start.35 = (f32[2,256]{1,0:T(2,128)}, f32[2,256]{1,0:T(2,128)S(1)}, u32[]{:S(2)}) copy-start(f32[2,256]{1,0:T(2,128)S(1)} %broadcast_multiply_fusion.2) | copy-start | bytes 6148
  472.0 54.0 %copy-start.41 = (f32[2,256]{1,0:T(2,128)}, f32[2,256]{1,0:T(2,128)S(1)}, u32[]{:S(2)}) copy-start(f32[2,256]{1,0:T(2,128)S(1)} %fusion.74) | copy-start | bytes 6148
  482.4 20.1 %copy-start.11 = (bf16[2,256,1024]{2,1,0:T(8,128)(2,1)S(1)}, bf16[2,256,1024]{2,1,0:T(8,128)(2,1)}, u32[]{:S(2)}) copy-start(bf16[2,256,1024]{2,1,0:T(8,128)(2,1)} %param.33) | copy-start | bytes 3145732
  532.8 28.5 %all-to-all-start.2 = ((bf16[2,256,1024]{1,0,2:T(2,128)(2,1)}), bf16[2,256,1024]{1,0,2:T(2,128)(2,1)S(1)}, u32[]{:S(2)}, u32[]{:S(2)}) async-start(bf16[2,256,1024]{1,0,2:T(2,128)(2,1)} %copy.206), calls=%async_computation.2 | async-start | bytes 2097152 | tf_op jit(solution)/shard_map/all_to_all | solution.py:520
  577.8 11.2 %copy-start = (f32[2,4,512,1024]{3,2,1,0:T(8,128)}, f32[2,4,512,1024]{3,2,1,0:T(8,128)S(1)}, u32[]{:S(2)}) copy-start(f32[2,4,512,1024]{3,2,1,0:T(8,128)S(1)} %subtract_exponential_fusion.3) | copy-start | bytes 50331652 | tf_op jit(solution)/shard_map/while
  598.8 9.1 copy-start.1
  598.8 13.2 %slice-start = ((s8[8388608]{0:T(1024)(128)(4,1)}), s8[4194304]{0:T(1024)(128)(4,1)S(1)}, s32[]{:S(2)}) async-start(s8[8388608]{0:T(1024)(128)(4,1)} %bitcast.228), calls=%async_computation.4 | async-start | bytes 8388608 | tf_op jit(solution)/shard_map/while
  629.7 11.2 %copy-start = (f32[2,4,512,1024]{3,2,1,0:T(8,128)}, f32[2,4,512,1024]{3,2,1,0:T(8,128)S(1)}, u32[]{:S(2)}) copy-start(f32[2,4,512,1024]{3,2,1,0:T(8,128)S(1)} %subtract_exponential_fusion.3) | copy-start | bytes 50331652 | tf_op jit(solution)/shard_map/while
  650.8 9.7 copy-start.1
  650.8 14.5 %slice-start = ((s8[8388608]{0:T(1024)(128)(4,1)}), s8[4194304]{0:T(1024)(128)(4,1)S(1)}, s32[]{:S(2)}) async-start(s8[8388608]{0:T(1024)(128)(4,1)} %bitcast.228), calls=%async_computation.4 | async-start | bytes 8388608 | tf_op jit(solution)/shard_map/while
  660.5 4.8 slice-start.1
  684.8 5.3 copy-start.22
  684.8 5.3 copy-start.24
  684.8 75.5 %all-to-all-start.3 = ((bf16[2,1024,3,256]{3,0,2,1:T(2,128)(2,1)}), bf16[2,1024,3,256]{3,0,2,1:T(2,128)(2,1)}, u32[]{:S(2)}, u32[]{:S(2)}) async-start(bf16[2,1024,3,256]{3,0,2,1:T(2,128)(2,1)} %copy.209), calls=%async_computation.3 | async-start | bytes 6291456 | tf_op jit(solution)/shard_map/all_to_all | solution.py:563
  692.7 11.0 %copy-start.10 = (f32[2,256,1024]{2,1,0:T(8,128)S(1)}, f32[2,256,1024]{2,1,0:T(8,128)}, u32[]{:S(2)}) copy-start(f32[2,256,1024]{2,1,0:T(8,128)} %copy-done.9) | copy-start | bytes 6291460
  703.6 10.3 copy-start.36
  703.7 10.3 copy-start.40
  703.7 10.3 copy-start.42
  703.7 10.3 copy-start.46
  703.7 10.3 copy-start.54
  714.0 7.3 copy-start.12
  714.0 7.3 copy-start.15
  728.2 40.6 %copy-start.6 = (f32[2,256,1024]{2,1,0:T(8,128)S(1)}, f32[2,256,1024]{2,1,0:T(8,128)}, u32[]{:S(2)}) copy-start(f32[2,256,1024]{2,1,0:T(8,128)} %copy-done.4) | copy-start | bytes 6291460
  728.2 40.6 %copy-start.28 = (f32[1,1024]{1,0:T(1,128)S(1)}, f32[1,1024]{1,0:T(1,128)}, u32[]{:S(2)}) copy-start(f32[1,1024]{1,0:T(1,128)} %copy-done.27) | copy-start | bytes 12292
  728.2 40.6 %copy-start.30 = (f32[2,256]{1,0:T(2,128)S(1)}, f32[2,256]{1,0:T(2,128)}, u32[]{:S(2)}) copy-start(f32[2,256]{1,0:T(2,128)} %copy-done.29) | copy-start | bytes 6148
  768.9 7.3 copy-start.16
  768.9 7.3 copy-start.32
  768.9 7.3 copy-start.44
  776.2 5.9 copy-start.38
  835.3 161.9 %copy-start.47 = (f32[1024]{0:T(1024)S(1)}, f32[1024]{0:T(1024)}, u32[]{:S(2)}) copy-start(f32[1024]{0:T(1024)} %get-tuple-element.332) | copy-start | bytes 12292
  835.3 161.9 %copy-start.48 = (f32[1024]{0:T(1024)S(1)}, f32[1024]{0:T(1024)}, u32[]{:S(2)}) copy-start(f32[1024]{0:T(1024)} %get-tuple-element.335) | copy-start | bytes 12292
  (17 other events, 38.0 us)

commit v2 on v0

v2 whole, which is shorter than its diff:
```python
import functools

import jax
import jax.numpy as jnp
from jax import lax
from jax.experimental import pallas as pl
from jax.experimental.pallas import tpu as pltpu
from jax.sharding import PartitionSpec as P

HEADS = 16
HEAD_DIM = 64
EPSILON = 1e-05
LOG2E = 1.4426950408889634
QUERIES = 256
F32 = jnp.float32
BF16 = jnp.bfloat16
MESH = pl.DeviceIdType.MESH
VMEM_LIMIT = 60 * 2**20
ANY = pl.BlockSpec(memory_space=pl.ANY)
WHOLE = pl.BlockSpec(memory_space=pltpu.VMEM)


def nt(a, b):
    return lax.dot_general(a, b, (((1,), (1,)), ((), ())), preferred_element_type=F32)


def nn(a, b):
    return jnp.dot(a, b, preferred_element_type=F32)


def part(index, size):
    if isinstance(index, int):
        return pl.ds(index * size, size)
    return pl.ds(pl.multiple_of(index * size, size), size)


def rowwise(rows, step, body):
    def run(i, carry):
        body(part(i, step))
        return carry

    lax.fori_loop(0, rows // step, run, 0)


def flip(index, mask):
    result = index
    bit = 0
    while mask >> bit:
        if (mask >> bit) & 1:
            on = lax.rem(lax.div(index, 1 << bit), 2)
            result = result + (1 << bit) * (1 - 2 * on)
        bit += 1
    return result


def span(bits):
    masks = [0]
    for bit in bits:
        masks = masks + [m | (1 << bit) for m in masks]
    return masks


class Place:
    def __init__(self, nb, nz):
        self.nb, self.nz = nb, nz
        self.b = lax.axis_index("batch")
        self.z = lax.axis_index("seq")
        self.half = nz // 2
        self.group = lax.div(self.z, self.half)
        self.k = lax.rem(self.z, self.half)
        self.partner = lax.rem(self.z + self.half, nz)
        self.rest = list(range(1, nb.bit_length() - 1))
        self.orders = (self.rest, self.rest[::-1])
        self.pending = []

    def at(self, mask):
        return (flip(self.b, mask), self.z)

    def mate(self, r):
        return self.group * self.half + lax.rem(self.k + r, self.half)

    def greet(self):
        barrier = pltpu.get_barrier_semaphore()
        targets = [self.at(1 << k) for k in [0] + self.rest]
        targets += [(self.b, lax.rem(self.z + r, self.nz)) for r in range(1, self.nz)]
        for t in targets:
            pl.semaphore_signal(barrier, inc=1, device_id=t, device_id_type=MESH)
        pl.semaphore_wait(barrier, len(targets))

    def start(self, make, *args):
        copy, ok = self.unpack(make(*args))
        if ok is None:
            copy.start()
        else:
            pl.when(ok)(lambda: copy.start())
        self.pending.append((make, args))

    def drain(self):
        for make, args in self.pending:
            copy, ok = self.unpack(make(*args))
            if ok is None:
                copy.wait_send()
            else:
                pl.when(ok)(lambda copy=copy: copy.wait_send())
        self.pending = []

    @staticmethod
    def unpack(made):
        return made if isinstance(made, tuple) else (made, None)


def remote(src, dst, send, recv, device):
    return pltpu.make_async_remote_copy(
        src_ref=src, dst_ref=dst, send_sem=send, recv_sem=recv, device_id=device, device_id_type=MESH
    )


class Gather:
    @staticmethod
    def sems(nb, nz):
        return 2 * (nz - 1) + 2 * (nb // 2 - 1) + nb

    @staticmethod
    def scratch(nb, nz):
        count = Gather.sems(nb, nz)
        return [pltpu.SemaphoreType.DMA] + [pltpu.SemaphoreType.DMA((count,))] * 2

    def __init__(self, place, shard, full, scratch, paired=False):
        self.p, self.shard, self.full, self.paired = place, shard, full, paired
        self.local, self.send, self.recv = scratch
        self.r, self.c = shard.shape
        nb, nz = place.nb, place.nz
        self.xy0 = 2 * (nz - 1)
        self.core0 = self.xy0 + 2 * (nb // 2 - 1)
        self.zsteps = 1 if paired else nz - 1
        self.stages = self.zsteps + len(place.rest) + 2

    def column(self, index):
        return self.full.at[part(self.p.b, self.r), part(index, self.c)]

    def line(self, way, step):
        p, n = self.p, self.p.nz
        sem = (0 if way > 0 else n - 1) + step - 1
        sent, got = p.z - way * (step - 1), p.z - way * step
        inside = lambda v: (v >= 0) & (v < n)
        clip = lambda v: jnp.clip(v, 0, n - 1)
        to = (p.b, clip(p.z + way))
        block = self.column(clip(sent))
        out = lambda: remote(self.shard if step == 1 else block, block, self.send.at[sem], self.recv.at[sem], to)
        land = self.column(clip(got))
        into = lambda: remote(land, land, self.send.at[sem], self.recv.at[sem], to)
        return out, into, inside(sent) & inside(p.z + way), inside(got)

    def zstart(self, step):
        p = self.p
        if self.paired:
            for t in (0, 1):
                p.start(self.paircopy, t)
            return
        for way in (1, -1):
            p.start(self.lineout, way, step)

    def lineout(self, way, step):
        out, _, can_send, _ = self.line(way, step)
        return out(), can_send

    def paircopy(self, t):
        p = self.p
        target = lax.div(p.z, 2) + t * p.half
        slot = lax.rem(p.z, 2)
        copy = remote(self.shard, self.column(slot), self.send.at[t], self.recv.at[slot], (p.b, target))
        return copy, target != p.z

    def zwait(self, step):
        p = self.p
        if self.paired:
            for s in (0, 1):
                land = self.column(s)
                copy = remote(land, land, self.send.at[s], self.recv.at[s], (p.b, p.partner))
                pl.when(2 * p.k + s != p.z)(lambda copy=copy: copy.wait_recv())
            return
        for way in (1, -1):
            _, into, _, can_get = self.line(way, step)
            pl.when(can_get)(lambda into=into: into().wait_recv())

    def owncopy(self):
        p = self.p
        if self.paired:
            mine = (2 * p.k == p.z) | (2 * p.k + 1 == p.z)
            return pltpu.make_async_copy(self.shard, self.column(lax.rem(p.z, 2)), self.local), mine
        return pltpu.make_async_copy(self.shard, self.column(p.z), self.local), None

    def rows(self, mask, half):
        h = self.r // 2
        return self.full.at[part(flip(self.p.b, mask) * 2 + half, h)]

    def hop(self, sem, mask, half, bit, incoming):
        block = self.rows(mask | bit if incoming else mask, half)
        return remote(block, block, self.send.at[sem], self.recv.at[sem], self.p.at(bit))

    def plane(self, j):
        made = []
        for half in (0, 1):
            order = self.p.orders[half]
            for i, m in enumerate(span(order[:j])):
                sem = self.xy0 + half * (self.p.nb // 2 - 1) + (1 << j) - 1 + i
                made.append((half, m, 1 << order[j], sem))
        return made

    def coresem(self, mask, half):
        return self.core0 + (mask >> 1) * 2 + half

    def corestart(self, mask, half):
        self.p.start(self.hop, self.coresem(mask, half), mask, half, 1, False)

    def stage(self, t):
        p = self.p
        nx = len(p.rest)
        if t == 0:
            own, mine = self.owncopy()
            if mine is None:
                own.start()
            else:
                pl.when(mine)(lambda: own.start())
            self.zstart(1)
        if 1 <= t <= self.zsteps:
            self.zwait(t)
            if t < self.zsteps:
                self.zstart(t + 1)
            else:
                own, mine = self.owncopy()
                if mine is None:
                    own.wait()
                else:
                    pl.when(mine)(lambda: own.wait())
        j = t - self.zsteps
        if 1 <= j <= nx:
            for half, m, bit, sem in self.plane(j - 1):
                self.hop(sem, m, half, bit, True).wait_recv()
        if 0 <= j < nx:
            for half, m, bit, sem in self.plane(j):
                p.start(self.hop, sem, m, half, bit, False)
        if j == 0:
            for half in (0, 1):
                self.corestart(0, half)
        if 1 <= j <= nx:
            for half, m, bit, _ in self.plane(j - 1):
                self.corestart(m | bit, half)
        if j == nx + 1:
            for m in span(p.rest):
                for half in (0, 1):
                    self.hop(self.coresem(m, half), m, half, 1, True).wait_recv()


class Scatter:
    @staticmethod
    def scratch(nb, nz, r, wide, paired=False):
        c = wide // (2 if paired else nz)
        lines = 2 if paired else 2 * (nz - 1)
        count = nb // 2 + 2 * (nb // 2 - 1) + lines
        return [
            pltpu.VMEM((nb // 2, r, wide), BF16),
            pltpu.VMEM((nb // 2, r, wide), BF16),
            pltpu.VMEM((2 * (nb // 2 - 1), r // 2, wide), BF16),
            pltpu.VMEM((lines, r, c), BF16),
            pltpu.SemaphoreType.DMA((nb // 2,)),
            pltpu.SemaphoreType.DMA((count,)),
            pltpu.SemaphoreType.DMA((count,)),
        ]

    def __init__(self, place, full, share, scratch, paired=False):
        self.p, self.full, self.share, self.paired = place, full, share, paired
        self.sums, self.core, self.flat, self.got, self.local, self.send, self.recv = scratch
        _, self.r, self.wide = self.sums.shape
        self.c = self.got.shape[2]
        self.zsteps = 1 if paired else place.nz - 1
        self.stages = 2 + len(place.rest) + self.zsteps
        self.zsem = place.nb // 2 + 2 * (place.nb // 2 - 1)
        self.masks = sorted(span(place.rest))

    def add(self, target, source):
        def body(at):
            target[at] = (target[at].astype(F32) + source[at].astype(F32)).astype(target.dtype)

        rowwise(target.shape[0], 16, body)

    def block(self, mask):
        return self.full.at[part(flip(self.p.b, mask), self.r)]

    def corecopy(self, i, m):
        return remote(self.block(m | 1), self.core.at[i], self.send.at[i], self.recv.at[i], self.p.at(1))

    def load(self, i, m):
        return pltpu.make_async_copy(self.block(m), self.sums.at[i], self.local.at[i])

    def rows(self, m, half):
        return self.sums.at[m >> 1, part(half, self.r // 2)]

    def plane(self, j):
        p = self.p
        made = []
        for half in (0, 1):
            order = p.orders[half]
            base = half * (p.nb // 2 - 1) + sum(len(span(order[q + 1 :])) for q in range(j))
            for i, m in enumerate(span(order[j + 1 :])):
                made.append((half, m, 1 << order[j], base + i))
        return made

    def planecopy(self, half, m, bit, slot):
        sem = self.p.nb // 2 + slot
        return remote(
            self.rows(m | bit, half), self.flat.at[slot], self.send.at[sem], self.recv.at[sem], self.p.at(bit)
        )

    def column(self, index):
        return self.sums.at[0, :, part(index, self.c)]

    def line(self, way, step):
        p, n = self.p, self.p.nz
        here = p.z if way > 0 else n - 1 - p.z
        goes = n + here - step
        comes = goes - 1
        can_send = (goes > here) & (goes <= n - 1)
        can_get = (comes >= here) & (comes <= n - 1) & (here > 0)
        unfold = lambda d: jnp.clip(d if way > 0 else n - 1 - d, 0, n - 1)
        slot = (0 if way > 0 else n - 1) + step - 1
        copy = remote(
            self.column(unfold(goes)),
            self.got.at[slot],
            self.send.at[self.zsem + slot],
            self.recv.at[self.zsem + slot],
            (p.b, jnp.clip(p.z + way, 0, n - 1)),
        )
        return copy, can_send, can_get, unfold(comes), slot

    def paircopy(self, s):
        p = self.p
        copy = remote(
            self.column(s),
            self.got.at[p.group],
            self.send.at[self.zsem + s],
            self.recv.at[self.zsem + p.group],
            (p.b, 2 * p.k + s),
        )
        return copy, 2 * p.k + s != p.z

    def zstart(self, step):
        p = self.p
        if self.paired:
            for s in (0, 1):
                p.start(self.paircopy, s)
            return
        for way in (1, -1):
            p.start(self.lineout, way, step)

    def lineout(self, way, step):
        return self.line(way, step)[:2]

    def zwait(self, step):
        p = self.p
        if self.paired:
            for t in (0, 1):
                copy = remote(
                    self.column(0),
                    self.got.at[t],
                    self.send.at[self.zsem + t],
                    self.recv.at[self.zsem + t],
                    (p.b, p.partner),
                )
                pl.when(lax.div(p.z, 2) + t * p.half != p.z)(lambda copy=copy: copy.wait_recv())
            return
        for way in (1, -1):
            copy, _, can_get, column, slot = self.line(way, step)

            @pl.when(can_get)
            def _(copy=copy, column=column, slot=slot):
                copy.wait_recv()
                if step < self.zsteps:
                    self.add(self.column(column), self.got.at[slot])

    def stage(self, t):
        p = self.p
        nx = len(p.rest)
        if t == 0:
            for i, m in enumerate(self.masks):
                p.start(self.corecopy, i, m)
                self.load(i, m).start()
        if t == 1:
            for i, m in enumerate(self.masks):
                self.load(i, m).wait()
                self.corecopy(i, m).wait_recv()
                self.add(self.sums.at[i], self.core.at[i])
        j = t - 1
        if 1 <= j <= nx:
            for half, m, bit, slot in self.plane(j - 1):
                self.planecopy(half, m, bit, slot).wait_recv()
                self.add(self.rows(m, half), self.flat.at[slot])
        if 0 <= j < nx:
            for half, m, bit, slot in self.plane(j):
                p.start(self.planecopy, half, m, bit, slot)
        s = t - 1 - nx
        if 1 <= s <= self.zsteps:
            self.zwait(s)
        if 0 <= s < self.zsteps:
            self.zstart(s + 1)
        if t == self.stages - 1:
            self.finish()

    def finish(self):
        p = self.p
        if self.paired:
            mine = (2 * p.k == p.z) | (2 * p.k + 1 == p.z)
            own = part(lax.rem(p.z, 2), self.c)
            terms = [(self.got.at[t], lax.div(p.z, 2) + t * p.half != p.z) for t in (0, 1)]
        else:
            mine = None
            own = part(p.z, self.c)
            n = p.nz
            terms = [(self.got.at[n - 2], p.z > 0), (self.got.at[2 * n - 3], p.z < n - 1)]

        def first(at):
            value = self.sums[0, at, own].astype(F32)
            self.share[at] = value if mine is None else jnp.where(mine, value, 0.0)

        rowwise(self.r, 16, first)
        for ref, ok in terms:

            @pl.when(ok)
            def _(ref=ref):
                def more(at):
                    self.share[at] = self.share[at] + ref[at].astype(F32)

                rowwise(self.r, 16, more)


def perform(steps):
    for job, t in steps:
        job.stage(t)


def normalise(v):
    centred = v - jnp.mean(v, 1, keepdims=True)
    scale = lax.rsqrt(jnp.mean(centred * centred, 1, keepdims=True) + EPSILON)
    return centred * scale, scale


def norm_back(g, v, gain, gain_sum, shift_sum):
    n, scale = normalise(v)
    fold = lambda a: sum(a[i * 8 : (i + 1) * 8] for i in range(a.shape[0] // 8))
    gain_sum[...] += fold(g * n)
    shift_sum[...] += fold(g)
    gg = g * gain
    return (gg - jnp.mean(gg, 1, keepdims=True) - n * jnp.mean(gg * n, 1, keepdims=True)) * scale


def own_half(value, i):
    lane = lax.broadcasted_iota(jnp.int32, value.shape, 1)
    return jnp.where((lane >= HEAD_DIM) if i else (lane < HEAD_DIM), value, jnp.zeros_like(value))


def merge_halves(a, b):
    lane = lax.broadcasted_iota(jnp.int32, a.shape, 1)
    return jnp.where(lane < HEAD_DIM, a, b)


def project(normed, weight, qkv, pz):
    c = pz * 128
    rows = normed.shape[0]
    for j in (0, 1):
        for t in range(3):
            for i in range(rows // 512):
                at = pl.ds(i * 512, 512)
                y = nn(normed[at, :], weight[:, pl.ds((j * 3 + t) * c, c)])
                if t == 0:
                    y = y.astype(BF16).astype(F32) * HEAD_DIM**-0.5
                for w in range(pz):
                    qkv[t, j * pz + w, at, :] = y[:, w * 128 : (w + 1) * 128].astype(BF16)


def distances(dist, length):
    rows, cols = dist.shape

    def body(i, carry):
        row = lax.broadcasted_iota(jnp.int32, (64, cols), 0) + i * 64
        col = lax.broadcasted_iota(jnp.int32, (64, cols), 1)
        gap = jnp.abs(row - col).astype(F32)
        dist[part(i, 64), :] = jnp.where(col < length, gap, 1e33)
        return carry

    lax.fori_loop(0, rows // 64, body, 0)


def forward_tile(qkv, dist, pair, first_head, at, store):
    q, k, v = qkv[0, pair, at, :], qkv[1, pair], qkv[2, pair]
    gap = dist[at, :]
    outs = []
    for i in range(2):
        head = (first_head + 2 * pair + i + 1).astype(F32)
        slope = jnp.exp2(jnp.full((1, 1), -8.0 / HEADS, F32) * head) * LOG2E
        x = nt(own_half(q, i), k) * LOG2E - gap * slope
        e = jnp.exp2(x - jnp.max(x, 1, keepdims=True))
        p = (e * (1.0 / jnp.sum(e, 1, keepdims=True))).astype(BF16)
        store(i, p)
        outs.append(nn(p, v))
    return merge_halves(*outs).astype(BF16)


def backward_tile(qkv, do, do_t, q_t, pair, probs, dk, dv):
    k, v = qkv[1, pair], qkv[2, pair]
    dq = []
    for i in range(2):
        p = probs(i)
        rows = pl.ds(i * HEAD_DIM, HEAD_DIM)
        t = p.astype(F32) * nt(own_half(do, i), v)
        ds = (t - p.astype(F32) * jnp.sum(t, 1, keepdims=True)).astype(BF16)
        dq.append(nn(ds, k))
        dv[rows, :] += nn(do_t[rows, :], p)
        dk[rows, :] += nn(q_t[rows, :], ds)
    return (merge_halves(*dq) * HEAD_DIM**-0.5).astype(BF16)


def forward_kernel(
    nb, nz, lengths, x, skip_x, norms, skip_w, qkv_w, out_w, up_w, down_w,
    mixed_out, normed_out, norms_out, skip_out, qkvw_out, out_out, up_out, down_out, qkv_out, probs, attended_out,
    skip, qkvw, joined, mixed, normed, everything, gains, qkv, dist, pbuf, attended,
    load, norm_send, norm_recv, swap_send, swap_recv, flush, psem, att_send, att_recv, *rest,
):
    place = Place(nb, nz)
    z, group, k, half = place.z, place.group, place.k, place.half
    frames = x.shape[0] // 2
    width = x.shape[1]
    keys = nz * frames
    c = norms.shape[1]
    pz = c // 128
    pairs = 2 * pz
    place.greet()

    skip_s, qkvw_s, out_s, up_s, down_s = [rest[3 * i : 3 * i + 3] for i in range(5)]
    skip_job = Gather(place, skip_w, skip, skip_s)
    qkv_job = Gather(place, qkv_w, qkvw, qkvw_s, True)
    out_job = Gather(place, out_w, out_out, out_s)
    up_job = Gather(place, up_w, up_out, up_s)
    down_job = Gather(place, down_w, down_out, down_s)
    last = nz - 1

    skip_job.stage(0)
    loads = [
        pltpu.make_async_copy(x, joined.at[:, pl.ds(0, width)], load.at[0]),
        pltpu.make_async_copy(skip_x, joined.at[:, pl.ds(width, width)], load.at[1]),
        pltpu.make_async_copy(norms, gains.at[:, part(z, c)], load.at[2]),
    ]
    for one in loads:
        one.start()
    norm_copy = lambda r: remote(
        norms, gains.at[:, part(z, c)], norm_send.at[r - 1], norm_recv.at[r - 1], (place.b, lax.rem(z + r, nz))
    )
    for r in range(1, nz):
        place.start(norm_copy, r)
    for t in range(1, last):
        skip_job.stage(t)
    qkv_job.stage(0)
    skip_job.stage(last)
    out_job.stage(0)
    qkv_job.stage(1)
    for t in range(1, last + 1):
        out_job.stage(t)
    skip_job.stage(last + 1)
    up_job.stage(0)
    for t in range(last + 2, skip_job.stages):
        skip_job.stage(t)
    up_job.stage(1)
    qkv_job.stage(2)
    out_job.stage(last + 1)
    flushes = []

    def out_copy(src, dst):
        copy = pltpu.make_async_copy(src, dst, flush.at[len(flushes)])
        flushes.append(copy)
        copy.start()

    out_copy(skip, skip_out)
    for one in loads:
        one.wait()
    for r in range(1, nz):
        norm_copy(r).wait_recv()
    out_copy(gains, norms_out)

    def across():
        return remote(
            normed.at[1 - group], everything.at[part(z, frames)], swap_send.at[0], swap_recv.at[0],
            (place.b, place.partner),
        )

    for turn in (0, 1):
        item = 1 - group if turn == 0 else group
        rows = part(item, frames)
        mixed[rows, :] = nn(joined[rows, :], skip[...])
        gain, shift = gains[0:1, :], gains[1:2, :]

        def body(i, carry):
            at = part(i, 32)
            at2 = pl.ds(pl.multiple_of(item * frames + i * 32, 32), 32)
            n, _ = normalise(mixed[at2, :])
            normed[item, at, :] = (n * gain + shift).astype(BF16)
            return carry

        lax.fori_loop(0, frames // 32, body, 0)
        if turn == 0:
            place.start(across)
        else:
            own = pltpu.make_async_copy(normed.at[item], everything.at[part(z, frames)], load.at[0])
            own.start()

    def mate_copy(src, block, r, sem):
        return remote(
            src, everything.at[part(block, frames)], swap_send.at[sem], swap_recv.at[sem], (place.b, place.mate(r))
        )

    for r in range(1, half):
        place.start(mate_copy, normed.at[group], z, r, r)
    out_copy(mixed, mixed_out)
    across().wait_recv()
    for r in range(1, half):
        block = everything.at[part(place.partner, frames)]
        place.start(mate_copy, block, place.partner, r, half - 1 + r)
    distances(dist, lengths[group])
    up_job.stage(2)
    qkv_job.stage(3)
    for t in range(last + 2, out_job.stages):
        out_job.stage(t)
    for t in range(4, qkv_job.stages):
        qkv_job.stage(t)
    out_copy(qkvw, qkvw_out)
    for t in range(3, last + 1):
        up_job.stage(t)
    down_job.stage(0)
    own.wait()
    for r in range(1, half):
        mate_copy(normed.at[group], z, r, r).wait_recv()
        mate_copy(normed.at[group], z, r, half - 1 + r).wait_recv()
    out_copy(everything, normed_out)

    project(everything, qkvw, qkv, pz)
    out_copy(qkv, qkv_out)
    first_head = k * 2 * pairs
    blocks = keys // QUERIES
    total = pairs * blocks

    def probs_copy(slot, pair, at):
        return pltpu.make_async_copy(pbuf.at[slot], probs.at[pair, :, at], psem.at[slot])

    def att_copy(pair, r):
        owner = lax.rem(z + r, nz)
        slot = pair * (nz - 1) + r - 1
        return remote(
            attended.at[pair, part(owner, frames)],
            attended_out.at[part(group, frames), part(k * pairs + pair, 128)],
            att_send.at[slot], att_recv.at[slot], (place.b, owner),
        )

    def att_own(pair):
        return pltpu.make_async_copy(
            attended.at[pair, part(z, frames)],
            attended_out.at[part(group, frames), part(k * pairs + pair, 128)],
            flush.at[len(flushes)],
        )

    hooks = {}

    def hook(it, *steps):
        hooks.setdefault(min(it, total - 1), []).extend(steps)

    for t in range(1, last):
        hook(t, (down_job, t))
    hook(last, (up_job, last + 1), (down_job, last))
    hook(total * 5 // 8, (up_job, last + 2))
    hook(total * 6 // 8, (down_job, last + 1))

    def body(it, carry):
        pair, q = lax.div(it, blocks), lax.rem(it, blocks)
        at, slot = part(q, QUERIES), lax.rem(it, 2)
        for when, steps in hooks.items():
            pl.when(it == when)(lambda steps=steps: perform(steps))

        @pl.when(it >= 2)
        def _():
            probs_copy(slot, pair, at).wait()

        def store(i, p):
            pbuf[slot, i] = p

        attended[pair, at, :] = forward_tile(qkv, dist, pair, first_head, at, store)
        probs_copy(slot, pair, at).start()

        @pl.when(q == blocks - 1)
        def _():
            for r in range(1, nz):
                att_copy(pair, r).start()

        return carry

    lax.fori_loop(0, total, body, 0)
    for pair in range(pairs):
        att_own(pair).start()
    for t in range(last + 3, up_job.stages):
        up_job.stage(t)
    for t in range(last + 2, down_job.stages):
        down_job.stage(t)
    for pair in range(pairs):
        for r in range(1, nz):
            att_copy(pair, r).wait()
    for pair in range(pairs):
        att_own(pair).wait()
    for slot in range(min(2, total)):
        probs_copy(slot, 0, pl.ds(0, QUERIES)).wait()
    for copy in flushes:
        copy.wait()
    place.drain()


def forward(nb, nz, lengths, x, skip_x, norms, skip_w, qkv_w, out_w, up_w, down_w):
    rows, width = x.shape
    frames = rows // 2
    keys = nz * frames
    pairs = 2 * norms.shape[1] // 128
    S, V, D = jax.ShapeDtypeStruct, pltpu.VMEM, pltpu.SemaphoreType.DMA
    full = lambda w, n: (nb * w.shape[0], n * w.shape[1])
    out_shape = [
        S((rows, width), F32),
        S((keys, width), BF16),
        S((norms.shape[0], width), F32),
        S(full(skip_w, nz), BF16),
        S(full(qkv_w, 2), BF16),
        S(full(out_w, nz), BF16),
        S(full(up_w, nz), BF16),
        S(full(down_w, nz), BF16),
        S((3, pairs, keys, 128), BF16),
        S((pairs, 2, keys, keys), BF16),
        S((rows, width), BF16),
    ]
    scratch = [
        V(full(skip_w, nz), BF16),
        V(full(qkv_w, 2), BF16),
        V((rows, 2 * width), BF16),
        V((rows, width), F32),
        V((2, frames, width), BF16),
        V((keys, width), BF16),
        V((norms.shape[0], width), F32),
        V((3, pairs, keys, 128), BF16),
        V((keys, keys), F32),
        V((2, 2, QUERIES, keys), BF16),
        V((pairs, keys, 128), BF16),
    ]
    scratch += [D((3,)), D((nz - 1,)), D((nz - 1,)), D((nz - 1,)), D((nz - 1,)), D((8,)), D((2,))]
    scratch += [D((pairs * (nz - 1),)), D((pairs * (nz - 1),))]
    for _ in range(5):
        scratch += Gather.scratch(nb, nz)
    return pl.pallas_call(
        functools.partial(forward_kernel, nb, nz),
        out_shape=out_shape,
        in_specs=[pl.BlockSpec(memory_space=pltpu.SMEM)] + [ANY] * 8,
        out_specs=[ANY] * len(out_shape),
        scratch_shapes=scratch,
        compiler_params=pltpu.CompilerParams(
            collective_id=0, has_side_effects=True, vmem_limit_bytes=VMEM_LIMIT
        ),
    )(lengths, x, skip_x, norms, skip_w, qkv_w, out_w, up_w, down_w)


def ffn_kernel(
    steps, mixed, attended, out_t, norms, cot, up, dn,
    output, middle_grad, att_grad, out_grad, up_grad, dn_grad, sums,
    middle, ffn_in, ffn_in_t, cot_t, acc, gacc,
):
    j = pl.program_id(0)
    rows = mixed.shape[0]
    gain, shift = norms[2:3, :], norms[3:4, :]

    @pl.when(j == 0)
    def _():
        middle[...] = nt(attended[...], out_t[...])

        def body(at):
            v = middle[at, :] + mixed[at, :]
            middle[at, :] = v
            n, _ = normalise(v)
            ffn_in[at, :] = (n * gain + shift).astype(BF16)

        rowwise(rows, 32, body)
        ffn_in_t[...] = ffn_in[...].T
        cot_t[...] = cot[...].T
        acc[...] = jnp.zeros_like(acc)
        gacc[...] = jnp.zeros_like(gacc)

    hidden = nn(ffn_in[...], up[...])
    active_grad = nn(cot[...], dn[...])
    cdf = 0.5 * (1.0 + lax.erf(hidden * 0.7071067811865476))
    active = (hidden * cdf).astype(BF16)
    density = jnp.exp2(hidden * hidden * (-0.5 * LOG2E)) * 0.3989422804014327
    hidden_grad = (active_grad * (cdf + hidden * density)).astype(BF16)
    acc[...] += nt(active, dn[...])
    gacc[...] += nt(hidden_grad, up[...])
    dn_grad[...] = nn(cot_t[...], active).astype(BF16)
    up_grad[...] = nn(ffn_in_t[...], hidden_grad).astype(BF16)

    @pl.when(j == steps - 1)
    def _():
        sums[...] = jnp.zeros_like(sums)

        def body(at):
            v = middle[at, :]
            output[at, :] = (v + acc[at, :]).astype(BF16)
            back = norm_back(gacc[at, :], v, gain, sums.at[0], sums.at[1])
            grad = cot[at, :].astype(F32) + back
            middle_grad[at, :] = grad
            ffn_in[at, :] = grad.astype(BF16)

        rowwise(rows, 32, body)
        att_grad[...] = nn(ffn_in[...], out_t[...]).astype(BF16)
        out_grad[...] = nn(ffn_in[...].T, attended[...]).astype(BF16)


def ffn(mixed, attended, out_t, norms, cot, up, dn):
    rows, d = mixed.shape
    ff = up.shape[1]
    block = min(512, ff)
    steps = ff // block
    V, S = pltpu.VMEM, jax.ShapeDtypeStruct
    column = pl.BlockSpec((d, block), lambda j: (0, j))
    return pl.pallas_call(
        functools.partial(ffn_kernel, steps),
        grid=(steps,),
        in_specs=[WHOLE] * 5 + [column, column],
        out_specs=[WHOLE] * 4 + [column, column, WHOLE],
        out_shape=[
            S((rows, d), BF16),
            S((rows, d), F32),
            S((rows, d), BF16),
            S((d, d), BF16),
            S((d, ff), BF16),
            S((d, ff), BF16),
            S((2, 8, d), F32),
        ],
        scratch_shapes=[
            V((rows, d), F32),
            V((rows, d), BF16),
            V((d, rows), BF16),
            V((d, rows), BF16),
            V((rows, d), F32),
            V((rows, d), F32),
        ],
        compiler_params=pltpu.CompilerParams(vmem_limit_bytes=VMEM_LIMIT),
    )(mixed, attended, out_t, norms, cot, up, dn)


def attention_kernel(
    nb, nz, att_grad, qkv_in, probs, up_grad, dn_grad, out_grad,
    dqkv, up_share, dn_share, out_share,
    qkv, dout, pbuf, dk, dv, q_t, do_t, load, psem, att_send, att_recv, *rest,
):
    place = Place(nb, nz)
    z, group, k = place.z, place.group, place.k
    pairs, keys = qkv.shape[1], qkv.shape[2]
    frames = keys // nz
    wide = pairs * 128
    pz = pairs // 2
    per = len(rest) // 3
    place.greet()

    def att_copy(r):
        owner = lax.rem(z + r, nz)
        item, member = lax.div(owner, place.half), lax.rem(owner, place.half)
        return remote(
            att_grad.at[part(item, frames), part(member, wide)], dout.at[part(z, frames)],
            att_send.at[r - 1], att_recv.at[r - 1], (place.b, owner),
        )

    for r in range(1, nz):
        place.start(att_copy, r)
    own = pltpu.make_async_copy(att_grad.at[part(group, frames), part(k, wide)], dout.at[part(z, frames)], load.at[0])
    own.start()
    qkv_load = pltpu.make_async_copy(qkv_in, qkv, load.at[1])
    qkv_load.start()
    dn_job = Scatter(place, dn_grad, dn_share, rest[:per])
    up_job = Scatter(place, up_grad, up_share, rest[per : 2 * per])
    out_job = Scatter(place, out_grad, out_share, rest[2 * per :])
    nx = len(place.rest)
    dn_job.stage(0)
    up_job.stage(0)
    out_job.stage(0)
    dn_job.stage(1)
    up_job.stage(1)
    own.wait()
    qkv_load.wait()

    blocks = keys // QUERIES
    total = pairs * blocks

    def probs_copy(it):
        slot = lax.rem(it, 2)
        pair, q = lax.div(it, blocks), lax.rem(it, blocks)
        return pltpu.make_async_copy(probs.at[pair, :, part(q, QUERIES)], pbuf.at[slot], psem.at[slot])

    probs_copy(0).start()
    for r in range(1, nz):
        att_copy(r).wait_recv()
    hooks = {}

    def hook(it, *steps):
        hooks.setdefault(min(it, total - 1), []).extend(steps)

    hook(total // 8, (dn_job, 2))
    hook(total * 4 // 8, (up_job, 2))
    hook(total * 5 // 8, (out_job, 1))
    hook(total * 6 // 8, (dn_job, 3))

    def body(it, carry):
        pair, q = lax.div(it, blocks), lax.rem(it, blocks)
        at, slot = part(q, QUERIES), lax.rem(it, 2)
        for when, steps in hooks.items():
            pl.when(it == when)(lambda steps=steps: perform(steps))

        @pl.when(it + 1 < total)
        def _():
            probs_copy(it + 1).start()

        probs_copy(it).wait()

        @pl.when(q == 0)
        def _():
            dk[...] = jnp.zeros_like(dk)
            dv[...] = jnp.zeros_like(dv)

        do = dout[at, part(pair, 128)]
        q_t[...] = qkv[0, pair, at, :].T
        do_t[...] = do.T
        block = lax.div(pair, pz)
        column = lambda t: part((block * 3 + t) * pz + lax.rem(pair, pz), 128)
        dqkv[at, column(0)] = backward_tile(qkv, do, do_t, q_t, pair, lambda i: pbuf[slot, i], dk, dv)

        @pl.when(q == blocks - 1)
        def _():
            dqkv[:, column(1)] = dk[...].T.astype(BF16)
            dqkv[:, column(2)] = dv[...].T.astype(BF16)

        return carry

    lax.fori_loop(0, total, body, 0)
    first = {id(dn_job): 4, id(up_job): 3, id(out_job): 2}
    for t in range(2, dn_job.stages + 3):
        for lag, job in enumerate((dn_job, up_job, out_job)):
            if first[id(job)] <= t - lag < job.stages:
                job.stage(t - lag)
    place.drain()


def attention_back(nb, nz, att_grad, qkv, probs, up_grad, dn_grad, out_grad):
    _, pairs, keys, _ = qkv.shape
    S, V, D = jax.ShapeDtypeStruct, pltpu.VMEM, pltpu.SemaphoreType.DMA
    grads = (dn_grad, up_grad, out_grad)
    share = lambda g: S((g.shape[0] // nb, g.shape[1] // nz), F32)
    scratch = [
        V((3, pairs, keys, 128), BF16),
        V((keys, pairs * 128), BF16),
        V((2, 2, QUERIES, keys), BF16),
        V((128, keys), F32),
        V((128, keys), F32),
        V((128, QUERIES), BF16),
        V((128, QUERIES), BF16),
        D((2,)), D((2,)), D((nz - 1,)), D((nz - 1,)),
    ]
    for g in grads:
        scratch += Scatter.scratch(nb, nz, g.shape[0] // nb, g.shape[1])
    return pl.pallas_call(
        functools.partial(attention_kernel, nb, nz),
        out_shape=[S((keys, 3 * pairs * 128), BF16), share(up_grad), share(dn_grad), share(out_grad)],
        in_specs=[ANY] * 6,
        out_specs=[WHOLE] * 4,
        scratch_shapes=scratch,
        compiler_params=pltpu.CompilerParams(
            collective_id=1, has_side_effects=True, vmem_limit_bytes=VMEM_LIMIT
        ),
    )(att_grad, qkv, probs, up_grad, dn_grad, out_grad)


def first_kernel(
    nb, nz, dqkv, everything, qkvw, x, skip_x, skip_w, mixed, middle_grad, norms, second_sums,
    input_grad, skip_grad, qkv_share, skip_share, norm_share,
    qkv_grad, skip_w_grad, weight, joined, mixed_low, ahead, mine, from_mate, to_partner, from_partner,
    sums, packed, norm_in, norm_line, load, swap_send, swap_recv, norm_send, norm_recv, *rest,
):
    place = Place(nb, nz)
    z, group, k, half = place.z, place.group, place.k, place.half
    frames = x.shape[0] // 2
    width = x.shape[1]
    per = len(rest) // 2
    place.greet()
    qkv_job = Scatter(place, qkv_grad, qkv_share, rest[:per], True)
    skip_job = Scatter(place, skip_w_grad, skip_share, rest[per:])
    loads = [
        pltpu.make_async_copy(x, joined.at[:, pl.ds(0, width)], load.at[0]),
        pltpu.make_async_copy(skip_x, joined.at[:, pl.ds(width, width)], load.at[1]),
        pltpu.make_async_copy(skip_w, weight, load.at[2]),
    ]
    for one in loads:
        one.start()

    def mate_copy(r, t):
        slot = (r - 1) * 2 + t
        return remote(
            ahead.at[slot], from_mate.at[slot], swap_send.at[slot], swap_recv.at[slot], (place.b, place.mate(r))
        )

    for r in range(1, half):
        for t in (0, 1):
            block = lax.rem(k + r, half) + t * half
            ahead[(r - 1) * 2 + t] = nt(dqkv[part(block, frames), :], qkvw[...]).astype(BF16)
            place.start(mate_copy, r, t)
    for t in (0, 1):
        mine[t] = nt(dqkv[part(k + t * half, frames), :], qkvw[...])
    qkv_grad[...] = nn(everything[...].T, dqkv[...]).astype(BF16)
    qkv_job.stage(0)
    for r in range(1, half):
        for t in (0, 1):
            mate_copy(r, t).wait_recv()
            slot = (r - 1) * 2 + t

            def body(at):
                mine[t, at] = mine[t, at] + from_mate[slot, at].astype(F32)

            rowwise(frames, 16, body)
    sem = 2 * (half - 1)
    across = lambda: remote(to_partner, from_partner, swap_send.at[sem], swap_recv.at[sem], (place.b, place.partner))

    def narrow(at):
        to_partner[at] = mine[1 - group, at].astype(BF16)

    rowwise(frames, 16, narrow)
    place.start(across)
    qkv_job.stage(1)

    sums[...] = jnp.zeros_like(sums)
    gain = norms[0:1, :]

    def back(item, grad):
        def body(i, carry):
            at = part(i, 32)
            to = pl.ds(pl.multiple_of(item * frames + i * 32, 32), 32)
            part_grad = norm_back(grad(at), mixed[to, :], gain, sums.at[0], sums.at[1])
            mixed_low[to, :] = (middle_grad[to, :] + part_grad).astype(BF16)
            return carry

        lax.fori_loop(0, frames // 32, body, 0)

    back(group, lambda at: mine[group, at])
    across().wait_recv()
    back(1 - group, lambda at: from_partner[at].astype(F32))
    for one in loads:
        one.wait()
    skip_w_grad[...] = nn(joined[...].T, mixed_low[...]).astype(BF16)
    skip_job.stage(0)

    total = lambda a: jnp.sum(a, 0, keepdims=True)
    for i, v in enumerate((sums[0], sums[1], second_sums[0], second_sums[1])):
        packed[i : i + 1, :] = total(v)
    packed[4:8, :] = jnp.zeros_like(packed[4:8, :])
    bits = [0] + place.rest
    norm_copy = lambda i: remote(
        packed, norm_in.at[i], norm_send.at[i], norm_recv.at[i], place.at(1 << bits[i])
    )
    c = norm_share.shape[1]
    line_copy = lambda r: remote(
        packed.at[:, part(lax.rem(z + r, nz), c)], norm_line.at[r - 1],
        norm_send.at[len(bits) + r - 1], norm_recv.at[len(bits) + r - 1], (place.b, lax.rem(z + r, nz)),
    )

    def norm_step(i):
        if i > 0:
            norm_copy(i - 1).wait()
            packed[...] = packed[...] + norm_in[i - 1]
        if i < len(bits):
            norm_copy(i).start()
        else:
            for r in range(1, nz):
                line_copy(r).start()

    norm_step(0)
    skip_job.stage(1)
    norm_step(1)
    qkv_job.stage(2)
    for t in range(2):
        (input_grad, skip_grad)[t][...] = nt(mixed_low[...], weight[pl.ds(t * width, width), :])
        norm_step(2 + t)
    for i in range(4, len(bits) + 1):
        norm_step(i)
    skip_job.stage(2)
    qkv_job.stage(3)
    for t in range(3, max(skip_job.stages, qkv_job.stages - 1)):
        if t < skip_job.stages:
            skip_job.stage(t)
        if t + 1 < qkv_job.stages:
            qkv_job.stage(t + 1)
    value = packed[:, part(z, c)]
    for r in range(1, nz):
        line_copy(r).wait()
        value = value + norm_line[r - 1]
    norm_share[...] = value
    place.drain()


def first_back(nb, nz, dqkv, everything, qkvw, x, skip_x, skip_w, mixed, middle_grad, norms, second_sums):
    rows, width = x.shape
    frames = rows // 2
    half = nz // 2
    c = width // nz
    S, V, D = jax.ShapeDtypeStruct, pltpu.VMEM, pltpu.SemaphoreType.DMA
    qkv_wide = qkvw.shape[1]
    bits = nb.bit_length() - 1
    swaps = 2 * (half - 1)
    scratch = [
        V(qkvw.shape, BF16),
        V(skip_w.shape, BF16),
        V(skip_w.shape, BF16),
        V((rows, 2 * width), BF16),
        V((rows, width), BF16),
        V((max(swaps, 1), frames, width), BF16),
        V((2, frames, width), F32),
        V((max(swaps, 1), frames, width), BF16),
        V((frames, width), BF16),
        V((frames, width), BF16),
        V((2, 8, width), F32),
        V((8, width), F32),
        V((bits, 8, width), F32),
        V((nz - 1, 8, c), F32),
        D((3,)), D((swaps + 1,)), D((swaps + 1,)), D((bits + nz - 1,)), D((bits + nz - 1,)),
    ]
    scratch += Scatter.scratch(nb, nz, qkvw.shape[0] // nb, qkv_wide, True)
    scratch += Scatter.scratch(nb, nz, skip_w.shape[0] // nb, width)
    return pl.pallas_call(
        functools.partial(first_kernel, nb, nz),
        out_shape=[
            S((rows, width), F32),
            S((rows, width), F32),
            S((qkvw.shape[0] // nb, qkv_wide // 2), F32),
            S((skip_w.shape[0] // nb, c), F32),
            S((8, c), F32),
        ],
        in_specs=[WHOLE] * 3 + [ANY] * 3 + [WHOLE] * 4,
        out_specs=[WHOLE] * 5,
        scratch_shapes=scratch,
        compiler_params=pltpu.CompilerParams(
            collective_id=2, has_side_effects=True, vmem_limit_bytes=VMEM_LIMIT
        ),
    )(dqkv, everything, qkvw, x, skip_x, skip_w, mixed, middle_grad, norms, second_sums)


def shards(
    inputs,
    skip_input,
    lengths,
    skip_weight,
    query_weight,
    key_weight,
    value_weight,
    out_weight,
    up_weight,
    down_weight,
    first_gain,
    first_shift,
    second_gain,
    second_shift,
    cotangent,
):
    nb, nz = lax.axis_size("batch"), lax.axis_size("seq")
    shape = inputs.shape
    flat = lambda a: a.reshape(shape[0] * shape[1], shape[2])
    x, skip_x, cot = flat(inputs), flat(skip_input), flat(cotangent)
    norms = jnp.stack([first_gain, first_shift, second_gain, second_shift]).astype(F32)
    norms = jnp.pad(norms, ((0, 4), (0, 0)))
    qkv_shard = jnp.concatenate([query_weight, key_weight, value_weight], 1)
    (mixed, everything, gains, skip_w, qkvw, out_t, up, down_t, qkv, probs, attended) = forward(
        nb, nz, lengths, x, skip_x, norms, skip_weight, qkv_shard, out_weight.T, up_weight, down_weight.T
    )
    output, middle_grad, att_grad, out_grad, up_grad, dn_grad, second_sums = ffn(
        mixed, attended, out_t, gains, cot, up, down_t
    )
    dqkv, up_share, dn_share, out_share = attention_back(
        nb, nz, att_grad, qkv, probs, up_grad, dn_grad, out_grad
    )
    input_grad, skip_grad, qkv_share, skip_share, norm_share = first_back(
        nb, nz, dqkv, everything, qkvw, x, skip_x, skip_w, mixed, middle_grad, gains, second_sums
    )
    c = query_weight.shape[1]
    return (
        output.reshape(shape),
        input_grad.reshape(shape),
        skip_grad.reshape(shape),
        skip_share,
        qkv_share[:, :c],
        qkv_share[:, c : 2 * c],
        qkv_share[:, 2 * c :],
        out_share.T,
        up_share,
        dn_share.T,
        norm_share[0],
        norm_share[1],
        norm_share[2],
        norm_share[3],
    )


def solution(mesh):
    rows = P("batch", "seq", None)
    weight, turned, norm = P("batch", "seq"), P("seq", "batch"), P("seq")
    return jax.shard_map(
        shards,
        mesh=mesh,
        in_specs=(rows, rows, P("batch"), *[weight] * 4, turned, weight, turned, *[norm] * 4, rows),
        out_specs=(rows, rows, rows, *[weight] * 4, turned, weight, turned, *[norm] * 4),
        check_vma=False,
    )
```

time: 1210 us -> 461 us (0.38)
  waiting for transfers between devices: 593 us -> 0 us
  Pallas kernels: 0 us -> 441 us
  matrix products: 205 us -> 0 us
  blocking collectives: 161 us -> 0 us
  local copies, waits for them, and re-layouts: 122 us -> 16.9 us
  other arithmetic: 83.4 us -> 2.2 us
  starting transfers between devices: 18 us -> 0 us
  between operations: 15.7 us -> 0.71 us
    pallas_call x0 -> x4, Pallas kernels: none -> 441 us  [the longest x1 173 us: forward(): pl.pallas_call(functools.partial(forward_kernel, nb, nz), out_shape=out_s...]
    reduce_scatter x9 -> x0, waiting for transfers between devices: 238 us -> none  [the longest x1 75 us: shards(): lax.psum_scatter(up_grad.astype(jnp.bfloat16), 'batch', scatter_dimension...]
    dot_general x29 -> x0, matrix products: 205 us -> none  [the longest x4 29.4 us: block_scores(): jnp.einsum('iqhd,ikhd->ihqk', query_block, key_heads, preferred_element_t...]
    unnamed x28 -> x0, waiting for transfers between devices: 142 us -> none
    all_gather x9 -> x0, blocking collectives: 139 us -> none  [the longest x1 23.3 us: shards(): lax.all_gather(second_shift, 'seq', axis=0, tiled=True)]
    all_to_all x4 -> x0, waiting for transfers between devices: 131 us -> none  [the longest x1 60.9 us: shards(): lax.all_to_all(grads_heads, 'seq', split_axis=1, concat_axis=3, tiled=True)]
    all_gather x9 -> x0, waiting for transfers between devices: 81.4 us -> none  [the longest x1 29.7 us: shards(): lax.all_gather(value_part, 'batch', axis=0, tiled=True)]
    convert_element_type x25 -> x0, other arithmetic: 50.3 us -> none  [the longest x1 20.2 us: shards(): active = gelu_exact(hidden).astype(jnp.bfloat16)]
  transfers between devices with their start and end apart: 27 -> 0, of which waited for: 17 -> 0; matrix products, arithmetic and copies ran while one was open for 21% -> 0% of each run, Pallas kernels for 0% -> 0%
where the time goes in v2:
time: 461 us
  Pallas kernels  441 us (96%)
  local copies, waits for them, and re-layouts  16.9 us (4%)
    pallas_call x1, Pallas kernels, forward(): pl.pallas_call(functools.partial(forward_kernel, nb, nz), out_shape=out_s...  173 us
    pallas_call x1, Pallas kernels, attention_back(): pl.pallas_call(functools.partial(attention_kernel, nb, nz), out_shape=[S(...  115 us
    pallas_call x1, Pallas kernels, first_back(): pl.pallas_call(functools.partial(first_kernel, nb, nz), out_shape=[S((row...  105 us
    pallas_call x1, Pallas kernels, ffn(): pl.pallas_call(functools.partial(ffn_kernel, steps), grid=(steps,), in_sp...  47.3 us
    unnamed x18, local copies, waits for them, and re-layouts  11.1 us

profile of v2, /device:TPU:0, one launch (start us, length us, event | category | flops | bytes accessed | tf_op | source)
XLA Modules:
  0.0 460.7 jit_solution(8164527065690784926)
XLA Ops:
  0.6 0.7 stack.15
  1.3 0.7 stack.16
  2.0 0.7 stack.17
  2.6 0.7 stack.18
  3.3 0.6 fusion.7.norms
  3.9 1.6 copy.29
  5.5 1.6 pad_maximum_fusion.qkv_w
  7.1 1.8 copy.30
  8.8 172.8 %shard_map.254 = (f32[512,1024]{1,0:T(8,128)}, bf16[1024,1024]{1,0:T(8,128)(2,1)}, f32[8,1024]{1,0:T(8,128)}, bf16[2048,1024]{1,0:T(8,128)(2,1)}, bf16[1024,1536...) custom-call(s32[2]{0:T(128)} %lengths.1, ...), custom_call_target="tpu_custom_call" | custom-call | tf_op jit(solution)/shard_map/pallas_call | solution.py:758
  181.7 47.3 %shard_map.255 = (bf16[512,1024]{1,0:T(8,128)(2,1)}, f32[512,1024]{1,0:T(8,128)}, bf16[512,1024]{1,0:T(8,128)(2,1)}, bf16[1024,1024]{1,0:T(8,128)(2,1)}, bf16[10...) custom-call(f32[512,1024]{1,0:T(8,128)} %get-tuple-element.41.mixed, ...), custom_call_target="tpu_custom_call" | custom-call | tf_op jit(solution)/shard_map/pallas_call | solution.py:830
  229.0 115.4 %shard_map.256 = (bf16[1024,1536]{1,0:T(8,128)(2,1)}, f32[128,1024]{1,0:T(8,128)}, f32[128,1024]{1,0:T(8,128)}, f32[128,256]{1,0:T(8,128)}) custom-call(bf16[512,1024]{1,0:T(8,128)(2,1)} %get-tuple-element.48.att_grad, bf16[3,4,1024,128]{3,2,1,0:T(8,128)(2,1)} %get-tuple-element.49.qkv_in, bf16[4,2,1024,1024]{3,2,1,0:T(8,128)(2,1)} %get-tuple-element.50.probs, ...), custom_call_target="tpu_custom_call" | custom-call | tf_op jit(solution)/shard_map/pallas_call | solution.py:974
  344.4 0.0 copy-start.4
  344.4 0.0 copy-start.2
  344.5 105.2 %shard_map.257 = (f32[512,1024]{1,0:T(8,128)}, f32[512,1024]{1,0:T(8,128)}, f32[128,768]{1,0:T(8,128)}, f32[256,256]{1,0:T(8,128)}, f32[8,256]{1,0:T(8,128)}) custom-call(bf16[1024,1536]{1,0:T(8,128)(2,1)} %get-tuple-element.54.dqkv, bf16[1024,1024]{1,0:T(8,128)(2,1)} %get-tuple-element.55.everything, bf16[1024,1536]{1,0:T(8,128)(2,1)} %get-tuple-element.56.qkvw, ...), custom_call_target="tpu_custom_call" | custom-call | tf_op jit(solution)/shard_map/pallas_call | solution.py:1139
  449.7 0.0 copy-done.4
  449.7 0.0 copy-start
  449.7 0.8 copy.31
  450.5 1.4 fusion.9
  451.9 1.8 fusion.8
  453.7 0.0 copy-done.2
  453.7 1.0 copy.32
  454.7 3.2 copy.37
  457.8 0.0 copy-done
  457.8 0.0 copy-start.3
  457.8 0.0 copy-start.1
  457.8 1.3 copy.38
  459.2 0.0 copy-done.3
  459.2 0.7 copy.39
  459.9 0.0 copy-done.1
  459.9 0.8 copy.40
Async XLA Ops:
  344.4 105.3 %copy-start.4 = (f32[128,256]{1,0:T(8,128)S(1)}, f32[128,256]{1,0:T(8,128)}, u32[]{:S(2)}) copy-start(f32[128,256]{1,0:T(8,128)} %get-tuple-element.64) | copy-start | bytes 393220
  344.4 109.2 %copy-start.2 = (f32[128,1024]{1,0:T(8,128)S(1)}, f32[128,1024]{1,0:T(8,128)}, u32[]{:S(2)}) copy-start(f32[128,1024]{1,0:T(8,128)} %get-tuple-element.66) | copy-start | bytes 1572868
  449.7 8.1 %copy-start = (f32[512,1024]{1,0:T(8,128)S(1)}, f32[512,1024]{1,0:T(8,128)}, u32[]{:S(2)}) copy-start(f32[512,1024]{1,0:T(8,128)} %get-tuple-element.61) | copy-start | bytes 6291460
  457.8 1.3 copy-start.3
  457.8 2.0 copy-start.1

commit v3 on v2

--- a/solution.py
+++ b/solution.py
@@ -254,29 +254,43 @@
 
 class Scatter:
     @staticmethod
-    def scratch(nb, nz, r, wide, paired=False):
+    def scratch(nb, nz, r, wide, paired=False, sums=True, plane=True, line=True):
         c = wide // (2 if paired else nz)
         lines = 2 if paired else 2 * (nz - 1)
         count = nb // 2 + 2 * (nb // 2 - 1) + lines
-        return [
-            pltpu.VMEM((nb // 2, r, wide), BF16),
-            pltpu.VMEM((nb // 2, r, wide), BF16),
-            pltpu.VMEM((2 * (nb // 2 - 1), r // 2, wide), BF16),
-            pltpu.VMEM((lines, r, c), BF16),
+        made = [pltpu.VMEM((nb // 2 if plane else 1, r, wide), BF16)] if sums else []
+        if plane:
+            made += [
+                pltpu.VMEM((nb // 2, r, wide), BF16),
+                pltpu.VMEM((2 * (nb // 2 - 1), r // 2, wide), BF16),
+            ]
+        if line:
+            made += [pltpu.VMEM((lines, r, c), BF16)]
+        return made + [
             pltpu.SemaphoreType.DMA((nb // 2,)),
             pltpu.SemaphoreType.DMA((count,)),
             pltpu.SemaphoreType.DMA((count,)),
         ]
 
-    def __init__(self, place, full, share, scratch, paired=False):
+    def __init__(self, place, full, share, scratch, paired=False, sums=True, plane=True, line=True):
         self.p, self.full, self.share, self.paired = place, full, share, paired
-        self.sums, self.core, self.flat, self.got, self.local, self.send, self.recv = scratch
-        _, self.r, self.wide = self.sums.shape
-        self.c = self.got.shape[2]
+        scratch = list(scratch)
+        self.sums = scratch.pop(0) if sums else None
+        self.core, self.flat = (scratch.pop(0), scratch.pop(0)) if plane else (None, None)
+        self.got = scratch.pop(0) if line else None
+        self.local, self.send, self.recv = scratch
+        self.has_plane, self.has_line = plane, line
+        _, self.r, self.wide = (full if plane else self.sums).shape
+        self.c = self.wide // (2 if paired else place.nz)
         self.zsteps = 1 if paired else place.nz - 1
-        self.stages = 2 + len(place.rest) + self.zsteps
+        self.nx = len(place.rest)
+        self.plane_stages = 2 + self.nx
+        self.stages = (self.plane_stages if plane else 1) + (self.zsteps if line else 0)
         self.zsem = place.nb // 2 + 2 * (place.nb // 2 - 1)
         self.masks = sorted(span(place.rest))
+
+    def sum(self, m):
+        return self.full.at[m] if self.sums is None else self.sums.at[m >> 1]
 
     def add(self, target, source):
         def body(at):
@@ -284,17 +298,14 @@
 
         rowwise(target.shape[0], 16, body)
 
-    def block(self, mask):
-        return self.full.at[part(flip(self.p.b, mask), self.r)]
-
     def corecopy(self, i, m):
-        return remote(self.block(m | 1), self.core.at[i], self.send.at[i], self.recv.at[i], self.p.at(1))
+        return remote(self.full.at[m | 1], self.core.at[i], self.send.at[i], self.recv.at[i], self.p.at(1))
 
     def load(self, i, m):
-        return pltpu.make_async_copy(self.block(m), self.sums.at[i], self.local.at[i])
+        return pltpu.make_async_copy(self.full.at[m], self.sum(m), self.local.at[i])
 
     def rows(self, m, half):
-        return self.sums.at[m >> 1, part(half, self.r // 2)]
+        return self.sum(m).at[part(half, self.r // 2)]
 
     def plane(self, j):
         p = self.p
@@ -313,7 +324,7 @@
         )
 
     def column(self, index):
-        return self.sums.at[0, :, part(index, self.c)]
+        return self.sum(0).at[:, part(index, self.c)]
 
     def line(self, way, step):
         p, n = self.p, self.p.nz
@@ -344,6 +355,9 @@
         )
         return copy, 2 * p.k + s != p.z
 
+    def lineout(self, way, step):
+        return self.line(way, step)[:2]
+
     def zstart(self, step):
         p = self.p
         if self.paired:
@@ -352,9 +366,6 @@
             return
         for way in (1, -1):
             p.start(self.lineout, way, step)
-
-    def lineout(self, way, step):
-        return self.line(way, step)[:2]
 
     def zwait(self, step):
         p = self.p
@@ -379,47 +390,51 @@
                     self.add(self.column(column), self.got.at[slot])
 
     def stage(self, t):
-        p = self.p
-        nx = len(p.rest)
-        if t == 0:
-            for i, m in enumerate(self.masks):
-                p.start(self.corecopy, i, m)
-                self.load(i, m).start()
-        if t == 1:
-            for i, m in enumerate(self.masks):
-                self.load(i, m).wait()
-                self.corecopy(i, m).wait_recv()
-                self.add(self.sums.at[i], self.core.at[i])
-        j = t - 1
-        if 1 <= j <= nx:
-            for half, m, bit, slot in self.plane(j - 1):
-                self.planecopy(half, m, bit, slot).wait_recv()
-                self.add(self.rows(m, half), self.flat.at[slot])
-        if 0 <= j < nx:
-            for half, m, bit, slot in self.plane(j):
-                p.start(self.planecopy, half, m, bit, slot)
-        s = t - 1 - nx
-        if 1 <= s <= self.zsteps:
-            self.zwait(s)
-        if 0 <= s < self.zsteps:
-            self.zstart(s + 1)
-        if t == self.stages - 1:
-            self.finish()
+        p, nx = self.p, self.nx
+        s = t - (self.plane_stages - 1 if self.has_plane else 0)
+        if self.has_plane:
+            if t == 0:
+                for i, m in enumerate(self.masks):
+                    p.start(self.corecopy, i, m)
+                    if self.sums is not None:
+                        self.load(i, m).start()
+            if t == 1:
+                for i, m in enumerate(self.masks):
+                    if self.sums is not None:
+                        self.load(i, m).wait()
+                    self.corecopy(i, m).wait_recv()
+                    self.add(self.sum(m), self.core.at[i])
+            j = t - 1
+            if 1 <= j <= nx:
+                for half, m, bit, slot in self.plane(j - 1):
+                    self.planecopy(half, m, bit, slot).wait_recv()
+                    self.add(self.rows(m, half), self.flat.at[slot])
+            if 0 <= j < nx:
+                for half, m, bit, slot in self.plane(j):
+                    p.start(self.planecopy, half, m, bit, slot)
+        if self.has_line:
+            if 1 <= s <= self.zsteps:
+                self.zwait(s)
+            if 0 <= s < self.zsteps:
+                self.zstart(s + 1)
+            if t == self.stages - 1:
+                self.finish()
 
     def finish(self):
         p = self.p
         if self.paired:
             mine = (2 * p.k == p.z) | (2 * p.k + 1 == p.z)
-            own = part(lax.rem(p.z, 2), self.c)
+            own = lax.rem(p.z, 2)
             terms = [(self.got.at[t], lax.div(p.z, 2) + t * p.half != p.z) for t in (0, 1)]
         else:
             mine = None
-            own = part(p.z, self.c)
+            own = p.z
             n = p.nz
             terms = [(self.got.at[n - 2], p.z > 0), (self.got.at[2 * n - 3], p.z < n - 1)]
+        source = self.column(own)
 
         def first(at):
-            value = self.sums[0, at, own].astype(F32)
+            value = source[at].astype(F32)
             self.share[at] = value if mine is None else jnp.where(mine, value, 0.0)
 
         rowwise(self.r, 16, first)
@@ -434,8 +449,11 @@
 
 
 def perform(steps):
-    for job, t in steps:
-        job.stage(t)
+    for step in steps:
+        if callable(step):
+            step()
+        else:
+            step[0].stage(step[1])
 
 
 def normalise(v):
@@ -520,8 +538,8 @@
 
 
 def forward_kernel(
-    nb, nz, lengths, x, skip_x, norms, skip_w, qkv_w, out_w, up_w, down_w,
-    mixed_out, normed_out, norms_out, skip_out, qkvw_out, out_out, up_out, down_out, qkv_out, probs, attended_out,
+    nb, nz, lengths, x, skip_x, norms, skip_w, qkv_w, out_w, ff_w,
+    mixed_out, normed_out, norms_out, skip_out, qkvw_out, out_out, ff0_out, ff1_out, ff2_out, qkv_out, probs, attended_out,
     skip, qkvw, joined, mixed, normed, everything, gains, qkv, dist, pbuf, attended,
     load, norm_send, norm_recv, swap_send, swap_recv, flush, psem, att_send, att_recv, *rest,
 ):
@@ -535,15 +553,15 @@
     pairs = 2 * pz
     place.greet()
 
-    skip_s, qkvw_s, out_s, up_s, down_s = [rest[3 * i : 3 * i + 3] for i in range(5)]
-    skip_job = Gather(place, skip_w, skip, skip_s)
-    qkv_job = Gather(place, qkv_w, qkvw, qkvw_s, True)
-    out_job = Gather(place, out_w, out_out, out_s)
-    up_job = Gather(place, up_w, up_out, up_s)
-    down_job = Gather(place, down_w, down_out, down_s)
+    jobs = [rest[3 * i : 3 * i + 3] for i in range(6)]
+    skip_job = Gather(place, skip_w, skip, jobs[0])
+    qkv_job = Gather(place, qkv_w, qkvw, jobs[1], True)
+    out_job = Gather(place, out_w, out_out, jobs[2])
+    ff = [Gather(place, ff_w.at[i], o, jobs[3 + i]) for i, o in enumerate((ff0_out, ff1_out, ff2_out))]
     last = nz - 1
-
-    skip_job.stage(0)
+    go = lambda job, *stages: [job.stage(t) for t in stages if t < job.stages]
+
+    go(skip_job, 0)
     loads = [
         pltpu.make_async_copy(x, joined.at[:, pl.ds(0, width)], load.at[0]),
         pltpu.make_async_copy(skip_x, joined.at[:, pl.ds(width, width)], load.at[1]),
@@ -556,21 +574,20 @@
     )
     for r in range(1, nz):
         place.start(norm_copy, r)
-    for t in range(1, last):
-        skip_job.stage(t)
-    qkv_job.stage(0)
-    skip_job.stage(last)
-    out_job.stage(0)
-    qkv_job.stage(1)
-    for t in range(1, last + 1):
-        out_job.stage(t)
-    skip_job.stage(last + 1)
-    up_job.stage(0)
-    for t in range(last + 2, skip_job.stages):
-        skip_job.stage(t)
-    up_job.stage(1)
-    qkv_job.stage(2)
-    out_job.stage(last + 1)
+    go(skip_job, *range(1, last))
+    go(qkv_job, 0)
+    distances(dist, lengths[group])
+    go(skip_job, last)
+    go(out_job, 0)
+    go(skip_job, last + 1)
+    go(out_job, *range(1, last))
+    go(ff[0], 0, 1)
+    go(skip_job, last + 2)
+    go(qkv_job, 1)
+    go(out_job, last)
+    go(ff[0], 2)
+    for t in range(last + 3, skip_job.stages):
+        go(skip_job, t)
     flushes = []
 
     def out_copy(src, dst):
@@ -607,6 +624,10 @@
         lax.fori_loop(0, frames // 32, body, 0)
         if turn == 0:
             place.start(across)
+            go(qkv_job, 2)
+            go(out_job, last + 1)
+            for t in range(3, last + 1):
+                go(ff[0], t)
         else:
             own = pltpu.make_async_copy(normed.at[item], everything.at[part(z, frames)], load.at[0])
             own.start()
@@ -619,26 +640,28 @@
     for r in range(1, half):
         place.start(mate_copy, normed.at[group], z, r, r)
     out_copy(mixed, mixed_out)
+    go(ff[1], 0, 1)
+    go(qkv_job, 3)
+    go(out_job, last + 2)
     across().wait_recv()
     for r in range(1, half):
         block = everything.at[part(place.partner, frames)]
         place.start(mate_copy, block, place.partner, r, half - 1 + r)
-    distances(dist, lengths[group])
-    up_job.stage(2)
-    qkv_job.stage(3)
-    for t in range(last + 2, out_job.stages):
-        out_job.stage(t)
-    for t in range(4, qkv_job.stages):
-        qkv_job.stage(t)
+    go(ff[1], 2)
+    go(ff[0], last + 1)
+    for t in range(3, last + 1):
+        go(ff[1], t)
+    go(qkv_job, *range(4, qkv_job.stages))
+    go(out_job, *range(last + 3, out_job.stages))
     out_copy(qkvw, qkvw_out)
-    for t in range(3, last + 1):
-        up_job.stage(t)
-    down_job.stage(0)
+    go(ff[2], 0)
+    go(ff[0], last + 2)
     own.wait()
     for r in range(1, half):
         mate_copy(normed.at[group], z, r, r).wait_recv()
         mate_copy(normed.at[group], z, r, half - 1 + r).wait_recv()
     out_copy(everything, normed_out)
+    go(ff[2], 1)
 
     project(everything, qkvw, qkv, pz)
     out_copy(qkv, qkv_out)
@@ -670,11 +693,12 @@
     def hook(it, *steps):
         hooks.setdefault(min(it, total - 1), []).extend(steps)
 
-    for t in range(1, last):
-        hook(t, (down_job, t))
-    hook(last, (up_job, last + 1), (down_job, last))
-    hook(total * 5 // 8, (up_job, last + 2))
-    hook(total * 6 // 8, (down_job, last + 1))
+    rest_of = lambda job, t: [(job, s) for s in range(t, job.stages)]
+    hook(0, *[(ff[2], t) for t in range(2, last)], (ff[1], last + 1))
+    hook(total // 8, (ff[2], last), *rest_of(ff[0], last + 3))
+    hook(total * 3 // 8, (ff[1], last + 2), (ff[2], last + 1))
+    hook(total * 6 // 8, *rest_of(ff[1], last + 3))
+    hook(total * 7 // 8, (ff[2], last + 2))
 
     def body(it, carry):
         pair, q = lax.div(it, blocks), lax.rem(it, blocks)
@@ -702,10 +726,7 @@
     lax.fori_loop(0, total, body, 0)
     for pair in range(pairs):
         att_own(pair).start()
-    for t in range(last + 3, up_job.stages):
-        up_job.stage(t)
-    for t in range(last + 2, down_job.stages):
-        down_job.stage(t)
+    go(ff[2], *range(last + 3, ff[2].stages))
     for pair in range(pairs):
         for r in range(1, nz):
             att_copy(pair, r).wait()
@@ -718,7 +739,7 @@
     place.drain()
 
 
-def forward(nb, nz, lengths, x, skip_x, norms, skip_w, qkv_w, out_w, up_w, down_w):
+def forward(nb, nz, lengths, x, skip_x, norms, skip_w, qkv_w, out_w, ff_w):
     rows, width = x.shape
     frames = rows // 2
     keys = nz * frames
@@ -732,8 +753,7 @@
         S(full(skip_w, nz), BF16),
         S(full(qkv_w, 2), BF16),
         S(full(out_w, nz), BF16),
-        S(full(up_w, nz), BF16),
-        S(full(down_w, nz), BF16),
+        *[S((nb * ff_w.shape[1], nz * ff_w.shape[2]), BF16)] * 3,
         S((3, pairs, keys, 128), BF16),
         S((pairs, 2, keys, keys), BF16),
         S((rows, width), BF16),
@@ -753,109 +773,195 @@
     ]
     scratch += [D((3,)), D((nz - 1,)), D((nz - 1,)), D((nz - 1,)), D((nz - 1,)), D((8,)), D((2,))]
     scratch += [D((pairs * (nz - 1),)), D((pairs * (nz - 1),))]
-    for _ in range(5):
+    for _ in range(6):
         scratch += Gather.scratch(nb, nz)
     return pl.pallas_call(
         functools.partial(forward_kernel, nb, nz),
         out_shape=out_shape,
-        in_specs=[pl.BlockSpec(memory_space=pltpu.SMEM)] + [ANY] * 8,
+        in_specs=[pl.BlockSpec(memory_space=pltpu.SMEM)] + [ANY] * 7,
         out_specs=[ANY] * len(out_shape),
         scratch_shapes=scratch,
         compiler_params=pltpu.CompilerParams(
             collective_id=0, has_side_effects=True, vmem_limit_bytes=VMEM_LIMIT
         ),
-    )(lengths, x, skip_x, norms, skip_w, qkv_w, out_w, up_w, down_w)
+    )(lengths, x, skip_x, norms, skip_w, qkv_w, out_w, ff_w)
 
 
 def ffn_kernel(
-    steps, mixed, attended, out_t, norms, cot, up, dn,
-    output, middle_grad, att_grad, out_grad, up_grad, dn_grad, sums,
-    middle, ffn_in, ffn_in_t, cot_t, acc, gacc,
+    nb, nz, mixed_in, attended_in, out_in, norms, cot_in, ff0, ff1, ff2, ff_w,
+    output_out, middle_out, att_out, out_grad, part0, part1, grad2, grad3, sums, ff3,
+    middle, attended, out_t, cot, weights, grads, ffn_in, ffn_in_t, cot_t, acc, gacc, low,
+    load, wload, flush, *rest,
 ):
-    j = pl.program_id(0)
-    rows = mixed.shape[0]
+    place = Place(nb, nz)
+    rows, d = mixed_in.shape
+    r = grads.shape[2]
+    cw = ff_w.shape[2] // 2
+    subs = nz // 2
+    total = 4 * subs
+    place.greet()
+    gather = Gather(place, ff_w.at[3], ff3, rest[:3])
+    per = (len(rest) - 3) // 2
+    jobs = [
+        Scatter(place, grads.at[i], None, rest[3 + i * per : 3 + (i + 1) * per], sums=False, line=False) for i in (0, 1)
+    ]
+    go = lambda job, *stages: [job.stage(t) for t in stages if t < job.stages]
+    last = nz - 1
+    go(gather, 0)
+    loads = [
+        pltpu.make_async_copy(src, dst, load.at[i])
+        for i, (src, dst) in enumerate(
+            ((attended_in, attended), (out_in, out_t), (mixed_in, middle), (cot_in, cot))
+        )
+    ]
+    weight_load = lambda i: pltpu.make_async_copy((ff0, ff1, ff2, ff3)[i], weights.at[i % 2], wload.at[i % 2])
+    for one in loads:
+        one.start()
+    weight_load(0).start()
+    weight_load(1).start()
     gain, shift = norms[2:3, :], norms[3:4, :]
-
-    @pl.when(j == 0)
-    def _():
-        middle[...] = nt(attended[...], out_t[...])
-
-        def body(at):
-            v = middle[at, :] + mixed[at, :]
-            middle[at, :] = v
-            n, _ = normalise(v)
-            ffn_in[at, :] = (n * gain + shift).astype(BF16)
-
-        rowwise(rows, 32, body)
-        ffn_in_t[...] = ffn_in[...].T
-        cot_t[...] = cot[...].T
-        acc[...] = jnp.zeros_like(acc)
-        gacc[...] = jnp.zeros_like(gacc)
-
-    hidden = nn(ffn_in[...], up[...])
-    active_grad = nn(cot[...], dn[...])
-    cdf = 0.5 * (1.0 + lax.erf(hidden * 0.7071067811865476))
-    active = (hidden * cdf).astype(BF16)
-    density = jnp.exp2(hidden * hidden * (-0.5 * LOG2E)) * 0.3989422804014327
-    hidden_grad = (active_grad * (cdf + hidden * density)).astype(BF16)
-    acc[...] += nt(active, dn[...])
-    gacc[...] += nt(hidden_grad, up[...])
-    dn_grad[...] = nn(cot_t[...], active).astype(BF16)
-    up_grad[...] = nn(ffn_in_t[...], hidden_grad).astype(BF16)
-
-    @pl.when(j == steps - 1)
-    def _():
-        sums[...] = jnp.zeros_like(sums)
-
-        def body(at):
-            v = middle[at, :]
-            output[at, :] = (v + acc[at, :]).astype(BF16)
-            back = norm_back(gacc[at, :], v, gain, sums.at[0], sums.at[1])
-            grad = cot[at, :].astype(F32) + back
-            middle_grad[at, :] = grad
-            ffn_in[at, :] = grad.astype(BF16)
-
-        rowwise(rows, 32, body)
-        att_grad[...] = nn(ffn_in[...], out_t[...]).astype(BF16)
-        out_grad[...] = nn(ffn_in[...].T, attended[...]).astype(BF16)
-
-
-def ffn(mixed, attended, out_t, norms, cot, up, dn):
+    for one in loads[:3]:
+        one.wait()
+    acc[...] = nt(attended[...], out_t[...])
+    go(gather, 1)
+
+    def enter(at):
+        v = middle[at, :] + acc[at, :]
+        middle[at, :] = v
+        n, _ = normalise(v)
+        ffn_in[at, :] = (n * gain + shift).astype(BF16)
+        acc[at, :] = v
+        gacc[at, :] = jnp.zeros_like(v)
+
+    rowwise(rows, 32, enter)
+    ffn_in_t[...] = ffn_in[...].T
+    loads[3].wait()
+    cot_t[...] = cot[...].T
+    go(gather, *range(2, last))
+    weight_load(0).wait()
+
+    hooks = {}
+
+    def hook(it, *steps):
+        hooks.setdefault(min(it, total - 1), []).extend(steps)
+
+    rest_of = lambda job, t: [(job, s) for s in range(t, job.stages)]
+    hook(total // 8, (gather, last))
+    hook(total * 2 // 8, lambda: weight_load(1).wait(), lambda: weight_load(2).start(), (gather, last + 1), (jobs[0], 0))
+    hook(total * 3 // 8, (jobs[0], 1))
+    hook(total * 4 // 8, lambda: weight_load(2).wait(), (gather, last + 2), (jobs[1], 0))
+    hook(total * 5 // 8, *rest_of(gather, last + 3), lambda: weight_load(3).start(), (jobs[1], 1))
+    hook(total * 6 // 8, lambda: weight_load(3).wait(), (jobs[0], 2), lambda: flush_copy(0).start())
+    hook(total * 7 // 8, *rest_of(jobs[0], 3), (jobs[1], 2))
+
+    def flush_copy(i):
+        pairs = (
+            (grads.at[2], grad2), (grads.at[3], grad3), (grads.at[0, 0], part0), (grads.at[1, 0], part1),
+            (low, output_out), (gacc, middle_out), (attended, att_out),
+        )
+        return pltpu.make_async_copy(*pairs[i], flush.at[i])
+
+    def body(it, carry):
+        for when, steps in hooks.items():
+            pl.when(it == when)(lambda steps=steps: perform(steps))
+        chunk, sub = lax.div(it, subs), lax.rem(it, subs)
+        slot = lax.rem(chunk, 2)
+        first = [(2 * sub + i) * 2 for i in (0, 1)]
+        up = jnp.concatenate([weights[slot, :, part(f, cw)] for f in first], 1)
+        dn = jnp.concatenate([weights[slot, :, part(f + 1, cw)] for f in first], 1)
+        hidden = nn(ffn_in[...], up)
+        active_grad = nn(cot[...], dn)
+        cdf = 0.5 * (1.0 + lax.erf(hidden * 0.7071067811865476))
+        active = (hidden * cdf).astype(BF16)
+        density = jnp.exp2(hidden * hidden * (-0.5 * LOG2E)) * 0.3989422804014327
+        hidden_grad = (active_grad * (cdf + hidden * density)).astype(BF16)
+        acc[...] += nt(active, dn)
+        gacc[...] += nt(hidden_grad, up)
+        up_grad = nn(ffn_in_t[...], hidden_grad).astype(BF16)
+        dn_grad = nn(cot_t[...], active).astype(BF16)
+        for j in range(nb):
+            m = flip(place.b, j)
+            block = slice(j * r, (j + 1) * r)
+            for i in (0, 1):
+                cols = slice(i * cw, (i + 1) * cw)
+                grads[chunk, m, :, part(first[i], cw)] = up_grad[block, cols]
+                grads[chunk, m, :, part(first[i] + 1, cw)] = dn_grad[block, cols]
+        return carry
+
+    lax.fori_loop(0, total, body, 0)
+    flush_copy(1).start()
+    flush_copy(2).start()
+    sums[...] = jnp.zeros_like(sums)
+
+    def leave(at):
+        low[at, :] = acc[at, :].astype(BF16)
+        back = norm_back(gacc[at, :], middle[at, :], gain, sums.at[0], sums.at[1])
+        grad = cot[at, :].astype(F32) + back
+        gacc[at, :] = grad
+        ffn_in[at, :] = grad.astype(BF16)
+
+    rowwise(rows, 32, leave)
+    flush_copy(4).start()
+    flush_copy(5).start()
+    grad_t = ffn_in[...].T
+    for j in range(nb):
+        out_grad[flip(place.b, j)] = nn(grad_t[j * r : (j + 1) * r, :], attended[...]).astype(BF16)
+    attended[...] = nn(ffn_in[...], out_t[...]).astype(BF16)
+    flush_copy(6).start()
+    go(jobs[1], *range(3, jobs[1].stages))
+    flush_copy(3).start()
+    for i in range(7):
+        flush_copy(i).wait()
+    place.drain()
+
+
+def ffn(nb, nz, mixed, attended, out_t, norms, cot, ff0, ff1, ff2, ff_w):
     rows, d = mixed.shape
-    ff = up.shape[1]
-    block = min(512, ff)
-    steps = ff // block
-    V, S = pltpu.VMEM, jax.ShapeDtypeStruct
-    column = pl.BlockSpec((d, block), lambda j: (0, j))
+    _, r, width = ff_w.shape
+    wide = nz * width
+    V, S, D = pltpu.VMEM, jax.ShapeDtypeStruct, pltpu.SemaphoreType.DMA
+    scratch = [
+        V((rows, d), F32),
+        V((rows, d), BF16),
+        V((d, d), BF16),
+        V((rows, d), BF16),
+        V((2, d, wide), BF16),
+        V((4, nb, r, wide), BF16),
+        V((rows, d), BF16),
+        V((d, rows), BF16),
+        V((d, rows), BF16),
+        V((rows, d), F32),
+        V((rows, d), F32),
+        V((rows, d), BF16),
+        D((4,)), D((2,)), D((7,)),
+    ]
+    scratch += Gather.scratch(nb, nz)
+    for _ in range(2):
+        scratch += Scatter.scratch(nb, nz, r, wide, sums=False, line=False)
     return pl.pallas_call(
-        functools.partial(ffn_kernel, steps),
-        grid=(steps,),
-        in_specs=[WHOLE] * 5 + [column, column],
-        out_specs=[WHOLE] * 4 + [column, column, WHOLE],
+        functools.partial(ffn_kernel, nb, nz),
         out_shape=[
             S((rows, d), BF16),
             S((rows, d), F32),
             S((rows, d), BF16),
-            S((d, d), BF16),
-            S((d, ff), BF16),
-            S((d, ff), BF16),
+            S((nb, r, d), BF16),
+            *[S((r, wide), BF16)] * 2,
+            *[S((nb, r, wide), BF16)] * 2,
             S((2, 8, d), F32),
+            S((d, wide), BF16),
         ],
-        scratch_shapes=[
-            V((rows, d), F32),
-            V((rows, d), BF16),
-            V((d, rows), BF16),
-            V((d, rows), BF16),
-            V((rows, d), F32),
-            V((rows, d), F32),
-        ],
-        compiler_params=pltpu.CompilerParams(vmem_limit_bytes=VMEM_LIMIT),
-    )(mixed, attended, out_t, norms, cot, up, dn)
+        in_specs=[ANY] * 3 + [WHOLE] + [ANY] * 5,
+        out_specs=[ANY] * 3 + [WHOLE] + [ANY] * 4 + [WHOLE, ANY],
+        scratch_shapes=scratch,
+        compiler_params=pltpu.CompilerParams(
+            collective_id=3, has_side_effects=True, vmem_limit_bytes=VMEM_LIMIT
+        ),
+    )(mixed, attended, out_t, norms, cot, ff0, ff1, ff2, ff_w)
 
 
 def attention_kernel(
-    nb, nz, att_grad, qkv_in, probs, up_grad, dn_grad, out_grad,
-    dqkv, up_share, dn_share, out_share,
+    nb, nz, att_grad, qkv_in, probs, part0, part1, grad2, grad3, out_grad,
+    dqkv, ff_share, out_share,
     qkv, dout, pbuf, dk, dv, q_t, do_t, load, psem, att_send, att_recv, *rest,
 ):
     place = Place(nb, nz)
@@ -864,7 +970,6 @@
     frames = keys // nz
     wide = pairs * 128
     pz = pairs // 2
-    per = len(rest) // 3
     place.greet()
 
     def att_copy(r):
@@ -881,15 +986,26 @@
     own.start()
     qkv_load = pltpu.make_async_copy(qkv_in, qkv, load.at[1])
     qkv_load.start()
-    dn_job = Scatter(place, dn_grad, dn_share, rest[:per])
-    up_job = Scatter(place, up_grad, up_share, rest[per : 2 * per])
-    out_job = Scatter(place, out_grad, out_share, rest[2 * per :])
-    nx = len(place.rest)
-    dn_job.stage(0)
-    up_job.stage(0)
-    out_job.stage(0)
-    dn_job.stage(1)
-    up_job.stage(1)
+    rest = list(rest)
+
+    def job(full, share, **kind):
+        count = 3 + sum(kind.get(key, True) and size for key, size in (("sums", 1), ("plane", 2), ("line", 1)))
+        mine = [rest.pop(0) for _ in range(count)]
+        return Scatter(place, full, share, mine, **kind)
+
+    early = [job(None, ff_share.at[i], plane=False) for i in (0, 1)]
+    late = [job(g, ff_share.at[2 + i]) for i, g in enumerate((grad2, grad3))]
+    out_job = job(out_grad, out_share)
+    go = lambda job, *stages: [job.stage(t) for t in stages if t < job.stages]
+    early_loads = [
+        pltpu.make_async_copy(p, e.sums.at[0], load.at[2 + i]) for i, (p, e) in enumerate(zip((part0, part1), early))
+    ]
+    for one in early_loads:
+        one.start()
+    go(late[0], 0)
+    go(late[1], 0)
+    go(out_job, 0)
+    go(late[0], 1)
     own.wait()
     qkv_load.wait()
 
@@ -909,10 +1025,16 @@
     def hook(it, *steps):
         hooks.setdefault(min(it, total - 1), []).extend(steps)
 
-    hook(total // 8, (dn_job, 2))
-    hook(total * 4 // 8, (up_job, 2))
-    hook(total * 5 // 8, (out_job, 1))
-    hook(total * 6 // 8, (dn_job, 3))
+    zs = place.nz - 1
+    rest_of = lambda job, t: [(job, s) for s in range(t, job.stages)]
+    hook(0, (late[1], 1), *[lambda one=one: one.wait() for one in early_loads], (early[0], 0), (early[1], 0))
+    hook(total // 8, (late[0], 2), (early[0], 1), (early[1], 1))
+    hook(total * 2 // 8, (out_job, 1), *[(early[0], t) for t in range(2, zs)], *[(early[1], t) for t in range(2, zs)])
+    hook(total * 3 // 8, (late[1], 2), (early[0], zs), (early[1], zs))
+    hook(total * 4 // 8, (late[0], 3))
+    hook(total * 5 // 8, (out_job, 2), (late[0], 4))
+    hook(total * 6 // 8, (late[1], 3), (late[0], 5))
+    hook(total * 7 // 8, (late[1], 4), (out_job, 3))
 
     def body(it, carry):
         pair, q = lax.div(it, blocks), lax.rem(it, blocks)
@@ -946,19 +1068,17 @@
         return carry
 
     lax.fori_loop(0, total, body, 0)
-    first = {id(dn_job): 4, id(up_job): 3, id(out_job): 2}
-    for t in range(2, dn_job.stages + 3):
-        for lag, job in enumerate((dn_job, up_job, out_job)):
-            if first[id(job)] <= t - lag < job.stages:
-                job.stage(t - lag)
+    for t in range(4, out_job.stages + 1):
+        go(out_job, t)
+        go(late[1], t + 1)
+        go(late[0], t + 2)
     place.drain()
 
 
-def attention_back(nb, nz, att_grad, qkv, probs, up_grad, dn_grad, out_grad):
+def attention_back(nb, nz, att_grad, qkv, probs, part0, part1, grad2, grad3, out_grad):
     _, pairs, keys, _ = qkv.shape
     S, V, D = jax.ShapeDtypeStruct, pltpu.VMEM, pltpu.SemaphoreType.DMA
-    grads = (dn_grad, up_grad, out_grad)
-    share = lambda g: S((g.shape[0] // nb, g.shape[1] // nz), F32)
+    _, r, wide = grad2.shape
     scratch = [
         V((3, pairs, keys, 128), BF16),
         V((keys, pairs * 128), BF16),
@@ -967,26 +1087,32 @@
         V((128, keys), F32),
         V((128, QUERIES), BF16),
         V((128, QUERIES), BF16),
-        D((2,)), D((2,)), D((nz - 1,)), D((nz - 1,)),
+        D((4,)), D((2,)), D((nz - 1,)), D((nz - 1,)),
     ]
-    for g in grads:
-        scratch += Scatter.scratch(nb, nz, g.shape[0] // nb, g.shape[1])
+    for _ in range(2):
+        scratch += Scatter.scratch(nb, nz, r, wide, plane=False)
+    for g in (grad2, grad3, out_grad):
+        scratch += Scatter.scratch(nb, nz, r, g.shape[2])
     return pl.pallas_call(
         functools.partial(attention_kernel, nb, nz),
-        out_shape=[S((keys, 3 * pairs * 128), BF16), share(up_grad), share(dn_grad), share(out_grad)],
-        in_specs=[ANY] * 6,
-        out_specs=[WHOLE] * 4,
+        out_shape=[
+            S((keys, 3 * pairs * 128), BF16),
+            S((4, r, wide // nz), F32),
+            S((r, out_grad.shape[2] // nz), F32),
+        ],
+        in_specs=[ANY] * 8,
+        out_specs=[WHOLE] * 3,
         scratch_shapes=scratch,
         compiler_params=pltpu.CompilerParams(
             collective_id=1, has_side_effects=True, vmem_limit_bytes=VMEM_LIMIT
         ),
-    )(att_grad, qkv, probs, up_grad, dn_grad, out_grad)
+    )(att_grad, qkv, probs, part0, part1, grad2, grad3, out_grad)
 
 
 def first_kernel(
     nb, nz, dqkv, everything, qkvw, x, skip_x, skip_w, mixed, middle_grad, norms, second_sums,
     input_grad, skip_grad, qkv_share, skip_share, norm_share,
-    qkv_grad, skip_w_grad, weight, joined, mixed_low, ahead, mine, from_mate, to_partner, from_partner,
+    qkv_grad, skip_w_grad, weight, joined, joined_t, mixed_low, ahead, mine, from_mate, to_partner, from_partner,
     sums, packed, norm_in, norm_line, load, swap_send, swap_recv, norm_send, norm_recv, *rest,
 ):
     place = Place(nb, nz)
@@ -995,8 +1121,8 @@
     width = x.shape[1]
     per = len(rest) // 2
     place.greet()
-    qkv_job = Scatter(place, qkv_grad, qkv_share, rest[:per], True)
-    skip_job = Scatter(place, skip_w_grad, skip_share, rest[per:])
+    qkv_job = Scatter(place, qkv_grad, qkv_share, rest[:per], True, sums=False)
+    skip_job = Scatter(place, skip_w_grad, skip_share, rest[per:], sums=False)
     loads = [
         pltpu.make_async_copy(x, joined.at[:, pl.ds(0, width)], load.at[0]),
         pltpu.make_async_copy(skip_x, joined.at[:, pl.ds(width, width)], load.at[1]),
@@ -1012,31 +1138,43 @@
         )
 
     for r in range(1, half):
-        for t in (0, 1):
-            block = lax.rem(k + r, half) + t * half
-            ahead[(r - 1) * 2 + t] = nt(dqkv[part(block, frames), :], qkvw[...]).astype(BF16)
-            place.start(mate_copy, r, t)
-    for t in (0, 1):
-        mine[t] = nt(dqkv[part(k + t * half, frames), :], qkvw[...])
-    qkv_grad[...] = nn(everything[...].T, dqkv[...]).astype(BF16)
+        for s in (0, 1):
+            block = lax.rem(k + r, half) + (1 - group if s == 0 else group) * half
+            ahead[(r - 1) * 2 + s] = nt(dqkv[part(block, frames), :], qkvw[...]).astype(BF16)
+        place.start(mate_copy, r, 0)
+    for s in (0, 1):
+        block = k + (1 - group if s == 0 else group) * half
+        mine[s] = nt(dqkv[part(block, frames), :], qkvw[...])
+    turned = everything[...].T
+    rq = qkv_grad.shape[1]
+    for j in range(nb):
+        qkv_grad[flip(place.b, j)] = nn(turned[j * rq : (j + 1) * rq, :], dqkv[...]).astype(BF16)
     qkv_job.stage(0)
-    for r in range(1, half):
-        for t in (0, 1):
-            mate_copy(r, t).wait_recv()
-            slot = (r - 1) * 2 + t
+
+    def add_mates(s):
+        for r in range(1, half):
+            mate_copy(r, s).wait_recv()
+            slot = (r - 1) * 2 + s
 
             def body(at):
-                mine[t, at] = mine[t, at] + from_mate[slot, at].astype(F32)
+                mine[s, at] = mine[s, at] + from_mate[slot, at].astype(F32)
 
             rowwise(frames, 16, body)
+
+    add_mates(0)
     sem = 2 * (half - 1)
     across = lambda: remote(to_partner, from_partner, swap_send.at[sem], swap_recv.at[sem], (place.b, place.partner))
 
     def narrow(at):
-        to_partner[at] = mine[1 - group, at].astype(BF16)
+        to_partner[at] = mine[0, at].astype(BF16)
 
     rowwise(frames, 16, narrow)
     place.start(across)
+    for r in range(1, half):
+        place.start(mate_copy, r, 1)
+    for one in loads:
+        one.wait()
+    joined_t[...] = joined[...].T
     qkv_job.stage(1)
 
     sums[...] = jnp.zeros_like(sums)
@@ -1052,12 +1190,13 @@
 
         lax.fori_loop(0, frames // 32, body, 0)
 
-    back(group, lambda at: mine[group, at])
+    add_mates(1)
+    back(group, lambda at: mine[1, at])
     across().wait_recv()
     back(1 - group, lambda at: from_partner[at].astype(F32))
-    for one in loads:
-        one.wait()
-    skip_w_grad[...] = nn(joined[...].T, mixed_low[...]).astype(BF16)
+    rs = skip_w_grad.shape[1]
+    for j in range(nb):
+        skip_w_grad[flip(place.b, j)] = nn(joined_t[j * rs : (j + 1) * rs, :], mixed_low[...]).astype(BF16)
     skip_job.stage(0)
 
     total = lambda a: jnp.sum(a, 0, keepdims=True)
@@ -1118,10 +1257,11 @@
     bits = nb.bit_length() - 1
     swaps = 2 * (half - 1)
     scratch = [
-        V(qkvw.shape, BF16),
-        V(skip_w.shape, BF16),
+        V((nb, qkvw.shape[0] // nb, qkv_wide), BF16),
+        V((nb, skip_w.shape[0] // nb, width), BF16),
         V(skip_w.shape, BF16),
         V((rows, 2 * width), BF16),
+        V((2 * width, rows), BF16),
         V((rows, width), BF16),
         V((max(swaps, 1), frames, width), BF16),
         V((2, frames, width), F32),
@@ -1134,8 +1274,8 @@
         V((nz - 1, 8, c), F32),
         D((3,)), D((swaps + 1,)), D((swaps + 1,)), D((bits + nz - 1,)), D((bits + nz - 1,)),
     ]
-    scratch += Scatter.scratch(nb, nz, qkvw.shape[0] // nb, qkv_wide, True)
-    scratch += Scatter.scratch(nb, nz, skip_w.shape[0] // nb, width)
+    scratch += Scatter.scratch(nb, nz, qkvw.shape[0] // nb, qkv_wide, True, sums=False)
+    scratch += Scatter.scratch(nb, nz, skip_w.shape[0] // nb, width, sums=False)
     return pl.pallas_call(
         functools.partial(first_kernel, nb, nz),
         out_shape=[
@@ -1178,15 +1318,21 @@
     norms = jnp.stack([first_gain, first_shift, second_gain, second_shift]).astype(F32)
     norms = jnp.pad(norms, ((0, 4), (0, 0)))
     qkv_shard = jnp.concatenate([query_weight, key_weight, value_weight], 1)
-    (mixed, everything, gains, skip_w, qkvw, out_t, up, down_t, qkv, probs, attended) = forward(
-        nb, nz, lengths, x, skip_x, norms, skip_weight, qkv_shard, out_weight.T, up_weight, down_weight.T
+    cw = up_weight.shape[1] // 4
+    chunks = lambda w: w.reshape(w.shape[0], 4, cw)
+    ff_w = jnp.concatenate([chunks(up_weight), chunks(down_weight.T)], 2).transpose(1, 0, 2)
+    (mixed, everything, gains, skip_w, qkvw, out_t, ff0, ff1, ff2, qkv, probs, attended) = forward(
+        nb, nz, lengths, x, skip_x, norms, skip_weight, qkv_shard, out_weight.T, ff_w
     )
-    output, middle_grad, att_grad, out_grad, up_grad, dn_grad, second_sums = ffn(
-        mixed, attended, out_t, gains, cot, up, down_t
+    output, middle_grad, att_grad, out_grad, part0, part1, grad2, grad3, second_sums, _ = ffn(
+        nb, nz, mixed, attended, out_t, gains, cot, ff0, ff1, ff2, ff_w
     )
-    dqkv, up_share, dn_share, out_share = attention_back(
-        nb, nz, att_grad, qkv, probs, up_grad, dn_grad, out_grad
+    dqkv, ff_share, out_share = attention_back(
+        nb, nz, att_grad, qkv, probs, part0, part1, grad2, grad3, out_grad
     )
+    up_share, dn_share = [
+        ff_share[:, :, i * cw : (i + 1) * cw].transpose(1, 0, 2).reshape(up_weight.shape) for i in (0, 1)
+    ]
     input_grad, skip_grad, qkv_share, skip_share, norm_share = first_back(
         nb, nz, dqkv, everything, qkvw, x, skip_x, skip_w, mixed, middle_grad, gains, second_sums
     )

time: 461 us -> 418 us (0.907)
  Pallas kernels: 441 us -> 395 us
    pallas_call x1, Pallas kernels: 115 us -> 78.4 us  [attention_back(): pl.pallas_call(functools.partial(attention_kernel, nb, nz), out_shape=[S(...]
    pallas_call x1, Pallas kernels: 47.3 us -> 80.8 us  [ffn(): pl.pallas_call(functools.partial(ffn_kernel, nb, nz), out_shape=[S((rows,...]
    pallas_call x1, Pallas kernels: 173 us -> 142 us  [forward(): pl.pallas_call(functools.partial(forward_kernel, nb, nz), out_shape=out_s...]
    pallas_call x1, Pallas kernels: 105 us -> 94.3 us  [first_back(): pl.pallas_call(functools.partial(first_kernel, nb, nz), out_shape=[S((row...]
where the time goes in v3:
time: 418 us; the launch traced here: 417 us
  Pallas kernels  395 us (94%)
  local copies, waits for them, and re-layouts  18.6 us (4%)
    pallas_call x1, Pallas kernels, forward(): pl.pallas_call(functools.partial(forward_kernel, nb, nz), out_shape=out_s...  142 us
    pallas_call x1, Pallas kernels, first_back(): pl.pallas_call(functools.partial(first_kernel, nb, nz), out_shape=[S((row...  94.3 us
    pallas_call x1, Pallas kernels, ffn(): pl.pallas_call(functools.partial(ffn_kernel, nb, nz), out_shape=[S((rows,...  80.8 us
    pallas_call x1, Pallas kernels, attention_back(): pl.pallas_call(functools.partial(attention_kernel, nb, nz), out_shape=[S(...  78.4 us
    unnamed x18, local copies, waits for them, and re-layouts  10.2 us

profile of v3, /device:TPU:0, one launch (start us, length us, event | category | flops | bytes accessed | tf_op | source)
XLA Modules:
  0.0 417.4 jit_solution(13954588523381300102)
XLA Ops:
  0.6 0.7 stack.15
  1.3 0.7 stack.16
  2.0 0.7 stack.17
  2.6 0.7 stack.18
  3.3 0.6 fusion.7.norms
  3.9 1.6 copy.31
  5.5 1.6 pad_maximum_fusion.qkv_w
  7.1 1.1 copy.32
  8.2 0.1 copy.33
  8.3 1.1 copy.34
  9.4 0.8 maximum_bitcast_fusion.ff_w
  10.3 141.5 %shard_map.254 = (f32[512,1024]{1,0:T(8,128)}, bf16[1024,1024]{1,0:T(8,128)(2,1)}, f32[8,1024]{1,0:T(8,128)}, bf16[2048,1024]{1,0:T(8,128)(2,1)}, bf16[1024,1536...) custom-call(s32[2]{0:T(128)} %lengths.1, ...), custom_call_target="tpu_custom_call" | custom-call | tf_op jit(solution)/shard_map/pallas_call | solution.py:778
  151.8 80.8 %shard_map.255 = (bf16[512,1024]{1,0:T(8,128)(2,1)}, f32[512,1024]{1,0:T(8,128)}, bf16[512,1024]{1,0:T(8,128)(2,1)}, bf16[8,128,1024]{2,1,0:T(8,128)(2,1)}, bf16...) custom-call(f32[512,1024]{1,0:T(8,128)} %get-tuple-element.43.mixed_, ...), custom_call_target="tpu_custom_call" | custom-call | tf_op jit(solution)/shard_map/pallas_call | solution.py:941
  232.6 78.4 %shard_map.256 = (bf16[1024,1536]{1,0:T(8,128)(2,1)}, f32[4,128,512]{2,1,0:T(8,128)}, f32[128,256]{1,0:T(8,128)}) custom-call(bf16[512,1024]{1,0:T(8,128)(2,1)} %get-tuple-element.51.att_grad, bf16[3,4,1024,128]{3,2,1,0:T(8,128)(2,1)} %get-tuple-element.52.qkv_in, bf16[4,2,1024,1024]{3,2,1,0:T(8,128)(2,1)} %get-tuple-element.53.probs, ...), custom_call_target="tpu_custom_call" | custom-call | tf_op jit(solution)/shard_map/pallas_call | solution.py:1096
  311.0 0.0 copy-start.4
  311.0 0.0 copy-start.2
  311.1 94.3 %shard_map.257 = (f32[512,1024]{1,0:T(8,128)}, f32[512,1024]{1,0:T(8,128)}, f32[128,768]{1,0:T(8,128)}, f32[256,256]{1,0:T(8,128)}, f32[8,256]{1,0:T(8,128)}) custom-call(bf16[1024,1536]{1,0:T(8,128)(2,1)} %get-tuple-element.59.dqkv, bf16[1024,1024]{1,0:T(8,128)(2,1)} %get-tuple-element.60.everything, bf16[1024,1536]{1,0:T(8,128)(2,1)} %get-tuple-element.61.qkvw, ...), custom_call_target="tpu_custom_call" | custom-call | tf_op jit(solution)/shard_map/pallas_call | solution.py:1279
  405.4 0.0 copy-done.4
  405.4 0.8 copy.37
  406.1 1.4 fusion.9
  407.6 1.8 fusion.8
  409.4 0.0 copy-done.2
  409.4 0.1 slice_bitcast_fusion
  409.5 0.0 copy-start.1
  409.5 1.0 copy.36
  410.5 0.2 copy.35
  410.7 1.0 copy.38
  411.7 0.0 copy-start
  411.7 2.4 copy.43
  414.1 0.0 copy-done.1
  414.1 1.3 copy.44
  415.4 0.0 copy-done
  415.4 0.0 copy-start.3
  415.4 1.3 copy.45
  416.7 0.0 copy-done.3
  416.7 0.7 copy.46
Async XLA Ops:
  311.0 94.3 %copy-start.4 = (f32[128,256]{1,0:T(8,128)S(1)}, f32[128,256]{1,0:T(8,128)}, u32[]{:S(2)}) copy-start(f32[128,256]{1,0:T(8,128)} %get-tuple-element.69) | copy-start | bytes 393220
  311.0 98.3 %copy-start.2 = (f32[4,128,512]{2,1,0:T(8,128)S(1)}, f32[4,128,512]{2,1,0:T(8,128)}, u32[]{:S(2)}) copy-start(f32[4,128,512]{2,1,0:T(8,128)} %get-tuple-element.70) | copy-start | bytes 3145732
  409.5 4.6 %copy-start.1 = (f32[512,1024]{1,0:T(8,128)S(1)}, f32[512,1024]{1,0:T(8,128)}, u32[]{:S(2)}) copy-start(f32[512,1024]{1,0:T(8,128)} %get-tuple-element.65) | copy-start | bytes 6291460
  411.7 3.7 copy-start
  415.4 1.3 copy-start.3

commit v4 on v3

--- a/solution.py
+++ b/solution.py
@@ -118,25 +118,27 @@
 class Gather:
     @staticmethod
     def sems(nb, nz):
-        return 2 * (nz - 1) + 2 * (nb // 2 - 1) + nb
+        return max(2 * (nz - 1), 6) + 2 * (nb // 2 - 1) + nb
 
     @staticmethod
     def scratch(nb, nz):
         count = Gather.sems(nb, nz)
-        return [pltpu.SemaphoreType.DMA] + [pltpu.SemaphoreType.DMA((count,))] * 2
-
-    def __init__(self, place, shard, full, scratch, paired=False):
-        self.p, self.shard, self.full, self.paired = place, shard, full, paired
+        return [pltpu.SemaphoreType.DMA((3,))] + [pltpu.SemaphoreType.DMA((count,))] * 2
+
+    def __init__(self, place, shard, full, scratch, paired=False, h=0, of=1):
+        self.p, self.full, self.paired, self.h, self.of = place, full, paired, h, of
+        self.shards = shard if paired else [shard]
+        self.shard = self.shards[0]
         self.local, self.send, self.recv = scratch
-        self.r, self.c = shard.shape
+        self.r, self.c = self.shard.shape
         nb, nz = place.nb, place.nz
-        self.xy0 = 2 * (nz - 1)
+        self.xy0 = max(2 * (nz - 1), 6)
         self.core0 = self.xy0 + 2 * (nb // 2 - 1)
         self.zsteps = 1 if paired else nz - 1
         self.stages = self.zsteps + len(place.rest) + 2
 
     def column(self, index):
-        return self.full.at[part(self.p.b, self.r), part(index, self.c)]
+        return self.full.at[part(self.p.b * self.of + self.h, self.r), part(index, self.c)]
 
     def line(self, way, step):
         p, n = self.p, self.p.nz
@@ -155,7 +157,8 @@
         p = self.p
         if self.paired:
             for t in (0, 1):
-                p.start(self.paircopy, t)
+                for i in range(len(self.shards)):
+                    p.start(self.paircopy, t, i)
             return
         for way in (1, -1):
             p.start(self.lineout, way, step)
@@ -164,35 +167,47 @@
         out, _, can_send, _ = self.line(way, step)
         return out(), can_send
 
-    def paircopy(self, t):
-        p = self.p
+    def paircopy(self, t, i):
+        p, count = self.p, len(self.shards)
         target = lax.div(p.z, 2) + t * p.half
-        slot = lax.rem(p.z, 2)
-        copy = remote(self.shard, self.column(slot), self.send.at[t], self.recv.at[slot], (p.b, target))
+        slot = lax.rem(p.z, 2) * count + i
+        copy = remote(
+            self.shards[i], self.column(slot), self.send.at[t * count + i], self.recv.at[slot], (p.b, target)
+        )
         return copy, target != p.z
 
     def zwait(self, step):
         p = self.p
         if self.paired:
             for s in (0, 1):
-                land = self.column(s)
-                copy = remote(land, land, self.send.at[s], self.recv.at[s], (p.b, p.partner))
-                pl.when(2 * p.k + s != p.z)(lambda copy=copy: copy.wait_recv())
+
+                @pl.when(2 * p.k + s != p.z)
+                def _(s=s):
+                    for i in range(len(self.shards)):
+                        slot = s * len(self.shards) + i
+                        land = self.column(slot)
+                        remote(land, land, self.send.at[slot], self.recv.at[slot], (p.b, p.partner)).wait_recv()
+
             return
         for way in (1, -1):
             _, into, _, can_get = self.line(way, step)
             pl.when(can_get)(lambda into=into: into().wait_recv())
 
-    def owncopy(self):
-        p = self.p
+    def owncopy(self, act):
+        p, count = self.p, len(self.shards)
+        place = lax.rem(p.z, 2) if self.paired else p.z
+        copies = lambda: [
+            pltpu.make_async_copy(shard, self.column(place * count + i), self.local.at[i])
+            for i, shard in enumerate(self.shards)
+        ]
         if self.paired:
-            mine = (2 * p.k == p.z) | (2 * p.k + 1 == p.z)
-            return pltpu.make_async_copy(self.shard, self.column(lax.rem(p.z, 2)), self.local), mine
-        return pltpu.make_async_copy(self.shard, self.column(p.z), self.local), None
+            pl.when((2 * p.k == p.z) | (2 * p.k + 1 == p.z))(lambda: [act(copy) for copy in copies()][:0] or None)
+        else:
+            act(copies()[0])
 
     def rows(self, mask, half):
         h = self.r // 2
-        return self.full.at[part(flip(self.p.b, mask) * 2 + half, h)]
+        return self.full.at[part((flip(self.p.b, mask) * self.of + self.h) * 2 + half, h)]
 
     def hop(self, sem, mask, half, bit, incoming):
         block = self.rows(mask | bit if incoming else mask, half)
@@ -217,22 +232,14 @@
         p = self.p
         nx = len(p.rest)
         if t == 0:
-            own, mine = self.owncopy()
-            if mine is None:
-                own.start()
-            else:
-                pl.when(mine)(lambda: own.start())
+            self.owncopy(lambda copy: copy.start())
             self.zstart(1)
         if 1 <= t <= self.zsteps:
             self.zwait(t)
             if t < self.zsteps:
                 self.zstart(t + 1)
             else:
-                own, mine = self.owncopy()
-                if mine is None:
-                    own.wait()
-                else:
-                    pl.when(mine)(lambda: own.wait())
+                self.owncopy(lambda copy: copy.wait())
         j = t - self.zsteps
         if 1 <= j <= nx:
             for half, m, bit, sem in self.plane(j - 1):
@@ -294,7 +301,7 @@
 
     def add(self, target, source):
         def body(at):
-            target[at] = (target[at].astype(F32) + source[at].astype(F32)).astype(target.dtype)
+            target[at] = target[at] + source[at]
 
         rowwise(target.shape[0], 16, body)
 
@@ -538,10 +545,11 @@
 
 
 def forward_kernel(
-    nb, nz, lengths, x, skip_x, norms, skip_w, qkv_w, out_w, ff_w,
-    mixed_out, normed_out, norms_out, skip_out, qkvw_out, out_out, ff0_out, ff1_out, ff2_out, qkv_out, probs, attended_out,
-    skip, qkvw, joined, mixed, normed, everything, gains, qkv, dist, pbuf, attended,
-    load, norm_send, norm_recv, swap_send, swap_recv, flush, psem, att_send, att_recv, *rest,
+    nb, nz, lengths, x, skip_x, gain_one, shift_one, gain_two, shift_two,
+    skip_w, query_w, key_w, value_w, out_w, up_w, down_w,
+    mixed_out, normed_out, norms_out, skip_out, qkvw_out, out_out, ff0_out, ff1_out, ff2_out, ff3_w, qkv_out, probs, attended_out,
+    skip, qkvw, joined, mixed, normed, everything, norms, gains, turned, ff_w, qkv, dist, pbuf, attended,
+    load, ff_load, norm_send, norm_recv, swap_send, swap_recv, flush, psem, att_send, att_recv, *rest,
 ):
     place = Place(nb, nz)
     z, group, k, half = place.z, place.group, place.k, place.half
@@ -549,45 +557,73 @@
     width = x.shape[1]
     keys = nz * frames
     c = norms.shape[1]
+    cw = up_w.shape[1] // 4
     pz = c // 128
     pairs = 2 * pz
     place.greet()
 
-    jobs = [rest[3 * i : 3 * i + 3] for i in range(6)]
-    skip_job = Gather(place, skip_w, skip, jobs[0])
-    qkv_job = Gather(place, qkv_w, qkvw, jobs[1], True)
-    out_job = Gather(place, out_w, out_out, jobs[2])
-    ff = [Gather(place, ff_w.at[i], o, jobs[3 + i]) for i, o in enumerate((ff0_out, ff1_out, ff2_out))]
+    jobs = [rest[3 * i : 3 * i + 3] for i in range(7)]
+    rs = skip_w.shape[0] // 2
+    skips = [Gather(place, skip_w.at[pl.ds(h * rs, rs)], skip, jobs[h], h=h, of=2) for h in (0, 1)]
+    qkv_job = Gather(place, [query_w, key_w, value_w], qkvw, jobs[2], True)
+    out_job = Gather(place, turned, out_out, jobs[3])
+    ff = [Gather(place, ff_w.at[i], o, jobs[4 + i]) for i, o in enumerate((ff0_out, ff1_out, ff2_out))]
     last = nz - 1
-    go = lambda job, *stages: [job.stage(t) for t in stages if t < job.stages]
-
-    go(skip_job, 0)
+
+    def go(job, *stages):
+        for t in stages:
+            if t < job.stages:
+                job.stage(t)
+
+    def both(*stages):
+        for t in stages:
+            go(skips[0], t)
+            go(skips[1], t)
+
+    both(0)
     loads = [
         pltpu.make_async_copy(x, joined.at[:, pl.ds(0, width)], load.at[0]),
         pltpu.make_async_copy(skip_x, joined.at[:, pl.ds(width, width)], load.at[1]),
-        pltpu.make_async_copy(norms, gains.at[:, part(z, c)], load.at[2]),
     ]
-    for one in loads:
+    up_loads = [
+        pltpu.make_async_copy(up_w.at[:, pl.ds(i * cw, cw)], ff_w.at[i, :, pl.ds(0, cw)], ff_load.at[i]) for i in range(4)
+    ]
+    for one in loads + up_loads:
         one.start()
+    norms[...] = jnp.zeros_like(norms)
+    for i, ref in enumerate((gain_one, shift_one, gain_two, shift_two)):
+        norms[i : i + 1, :] = ref[...].astype(F32).reshape(1, c)
+    own_norms = pltpu.make_async_copy(norms, gains.at[:, part(z, c)], load.at[2])
+    own_norms.start()
     norm_copy = lambda r: remote(
         norms, gains.at[:, part(z, c)], norm_send.at[r - 1], norm_recv.at[r - 1], (place.b, lax.rem(z + r, nz))
     )
     for r in range(1, nz):
         place.start(norm_copy, r)
-    go(skip_job, *range(1, last))
+    turned[...] = out_w[...].T
+    down_t = down_w[...].T
+    for i in range(4):
+        ff_w[i, :, cw:] = down_t[:, i * cw : (i + 1) * cw]
+    both(*range(1, last))
     go(qkv_job, 0)
-    distances(dist, lengths[group])
-    go(skip_job, last)
+    go(skips[0], last)
     go(out_job, 0)
-    go(skip_job, last + 1)
-    go(out_job, *range(1, last))
-    go(ff[0], 0, 1)
-    go(skip_job, last + 2)
+    go(skips[1], last)
+    for one in up_loads:
+        one.wait()
+    go(skips[0], last + 1)
+    go(out_job, 1)
+    go(skips[1], last + 1)
+    go(out_job, *range(2, last))
+    go(ff[0], 0)
+    go(skips[0], last + 2)
+    go(ff[0], 1)
+    go(skips[1], last + 2)
+    go(ff[0], *range(2, last))
     go(qkv_job, 1)
     go(out_job, last)
-    go(ff[0], 2)
-    for t in range(last + 3, skip_job.stages):
-        go(skip_job, t)
+    go(ff[1], 0)
+    both(*range(last + 3, skips[0].stages))
     flushes = []
 
     def out_copy(src, dst):
@@ -596,6 +632,8 @@
         copy.start()
 
     out_copy(skip, skip_out)
+    out_copy(ff_w.at[3], ff3_w)
+    own_norms.wait()
     for one in loads:
         one.wait()
     for r in range(1, nz):
@@ -626,8 +664,8 @@
             place.start(across)
             go(qkv_job, 2)
             go(out_job, last + 1)
-            for t in range(3, last + 1):
-                go(ff[0], t)
+            go(ff[0], last)
+            go(ff[1], 1)
         else:
             own = pltpu.make_async_copy(normed.at[item], everything.at[part(z, frames)], load.at[0])
             own.start()
@@ -640,21 +678,20 @@
     for r in range(1, half):
         place.start(mate_copy, normed.at[group], z, r, r)
     out_copy(mixed, mixed_out)
-    go(ff[1], 0, 1)
+    go(ff[1], *range(2, last))
+    distances(dist, lengths[group])
     go(qkv_job, 3)
     go(out_job, last + 2)
+    go(ff[0], last + 1)
     across().wait_recv()
     for r in range(1, half):
         block = everything.at[part(place.partner, frames)]
         place.start(mate_copy, block, place.partner, r, half - 1 + r)
-    go(ff[1], 2)
-    go(ff[0], last + 1)
-    for t in range(3, last + 1):
-        go(ff[1], t)
+    go(ff[1], last)
+    go(ff[2], 0)
     go(qkv_job, *range(4, qkv_job.stages))
     go(out_job, *range(last + 3, out_job.stages))
     out_copy(qkvw, qkvw_out)
-    go(ff[2], 0)
     go(ff[0], last + 2)
     own.wait()
     for r in range(1, half):
@@ -685,7 +722,7 @@
         return pltpu.make_async_copy(
             attended.at[pair, part(z, frames)],
             attended_out.at[part(group, frames), part(k * pairs + pair, 128)],
-            flush.at[len(flushes)],
+            flush.at[7 + pair],
         )
 
     hooks = {}
@@ -696,9 +733,10 @@
     rest_of = lambda job, t: [(job, s) for s in range(t, job.stages)]
     hook(0, *[(ff[2], t) for t in range(2, last)], (ff[1], last + 1))
     hook(total // 8, (ff[2], last), *rest_of(ff[0], last + 3))
-    hook(total * 3 // 8, (ff[1], last + 2), (ff[2], last + 1))
+    hook(total * 3 // 8, (ff[1], last + 2))
+    hook(total * 4 // 8, (ff[2], last + 1))
     hook(total * 6 // 8, *rest_of(ff[1], last + 3))
-    hook(total * 7 // 8, (ff[2], last + 2))
+    hook(total - 1, (ff[2], last + 2))
 
     def body(it, carry):
         pair, q = lax.div(it, blocks), lax.rem(it, blocks)
@@ -739,72 +777,75 @@
     place.drain()
 
 
-def forward(nb, nz, lengths, x, skip_x, norms, skip_w, qkv_w, out_w, ff_w):
+def forward(nb, nz, lengths, x, skip_x, norms, skip_w, qkv_w, out_w, up_w, down_w):
     rows, width = x.shape
     frames = rows // 2
     keys = nz * frames
-    pairs = 2 * norms.shape[1] // 128
+    c = width // nz
+    pairs = 2 * c // 128
+    r = up_w.shape[0]
+    chunk = up_w.shape[1] // 2
     S, V, D = jax.ShapeDtypeStruct, pltpu.VMEM, pltpu.SemaphoreType.DMA
-    full = lambda w, n: (nb * w.shape[0], n * w.shape[1])
     out_shape = [
         S((rows, width), F32),
         S((keys, width), BF16),
-        S((norms.shape[0], width), F32),
-        S(full(skip_w, nz), BF16),
-        S(full(qkv_w, 2), BF16),
-        S(full(out_w, nz), BF16),
-        *[S((nb * ff_w.shape[1], nz * ff_w.shape[2]), BF16)] * 3,
+        S((8, width), F32),
+        S((nb * skip_w.shape[0], width), BF16),
+        S((nb * r, 6 * c), BF16),
+        S((nb * r, width), BF16),
+        *[S((nb * r, nz * chunk), BF16)] * 3,
+        S((r, chunk), BF16),
         S((3, pairs, keys, 128), BF16),
         S((pairs, 2, keys, keys), BF16),
         S((rows, width), BF16),
     ]
     scratch = [
-        V(full(skip_w, nz), BF16),
-        V(full(qkv_w, 2), BF16),
+        V((nb * skip_w.shape[0], width), BF16),
+        V((nb * r, 6 * c), BF16),
         V((rows, 2 * width), BF16),
         V((rows, width), F32),
         V((2, frames, width), BF16),
         V((keys, width), BF16),
-        V((norms.shape[0], width), F32),
+        V((8, c), F32),
+        V((8, width), F32),
+        V((r, c), BF16),
+        V((4, r, chunk), BF16),
         V((3, pairs, keys, 128), BF16),
         V((keys, keys), F32),
         V((2, 2, QUERIES, keys), BF16),
         V((pairs, keys, 128), BF16),
     ]
-    scratch += [D((3,)), D((nz - 1,)), D((nz - 1,)), D((nz - 1,)), D((nz - 1,)), D((8,)), D((2,))]
+    scratch += [D((3,)), D((4,)), D((nz - 1,)), D((nz - 1,)), D((nz - 1,)), D((nz - 1,)), D((7 + pairs,)), D((2,))]
     scratch += [D((pairs * (nz - 1),)), D((pairs * (nz - 1),))]
-    for _ in range(6):
+    for _ in range(7):
         scratch += Gather.scratch(nb, nz)
     return pl.pallas_call(
         functools.partial(forward_kernel, nb, nz),
         out_shape=out_shape,
-        in_specs=[pl.BlockSpec(memory_space=pltpu.SMEM)] + [ANY] * 7,
+        in_specs=[pl.BlockSpec(memory_space=pltpu.SMEM), ANY, ANY, *[WHOLE] * 4, *[ANY] * 4, WHOLE, ANY, WHOLE],
         out_specs=[ANY] * len(out_shape),
         scratch_shapes=scratch,
         compiler_params=pltpu.CompilerParams(
             collective_id=0, has_side_effects=True, vmem_limit_bytes=VMEM_LIMIT
         ),
-    )(lengths, x, skip_x, norms, skip_w, qkv_w, out_w, ff_w)
+    )(lengths, x, skip_x, *norms, skip_w, *qkv_w, out_w, up_w, down_w)
 
 
 def ffn_kernel(
     nb, nz, mixed_in, attended_in, out_in, norms, cot_in, ff0, ff1, ff2, ff_w,
-    output_out, middle_out, att_out, out_grad, part0, part1, grad2, grad3, sums, ff3,
+    output_out, middle_out, att_out, out_grad, part0, grad1, grad2, grad3, sums, ff3,
     middle, attended, out_t, cot, weights, grads, ffn_in, ffn_in_t, cot_t, acc, gacc, low,
     load, wload, flush, *rest,
 ):
     place = Place(nb, nz)
     rows, d = mixed_in.shape
     r = grads.shape[2]
-    cw = ff_w.shape[2] // 2
+    cw = ff_w.shape[1] // 2
     subs = nz // 2
     total = 4 * subs
     place.greet()
-    gather = Gather(place, ff_w.at[3], ff3, rest[:3])
-    per = (len(rest) - 3) // 2
-    jobs = [
-        Scatter(place, grads.at[i], None, rest[3 + i * per : 3 + (i + 1) * per], sums=False, line=False) for i in (0, 1)
-    ]
+    gather = Gather(place, ff_w, ff3, rest[:3])
+    job = Scatter(place, grads.at[0], None, rest[3:], sums=False, line=False)
     go = lambda job, *stages: [job.stage(t) for t in stages if t < job.stages]
     last = nz - 1
     go(gather, 0)
@@ -847,16 +888,15 @@
 
     rest_of = lambda job, t: [(job, s) for s in range(t, job.stages)]
     hook(total // 8, (gather, last))
-    hook(total * 2 // 8, lambda: weight_load(1).wait(), lambda: weight_load(2).start(), (gather, last + 1), (jobs[0], 0))
-    hook(total * 3 // 8, (jobs[0], 1))
-    hook(total * 4 // 8, lambda: weight_load(2).wait(), (gather, last + 2), (jobs[1], 0))
-    hook(total * 5 // 8, *rest_of(gather, last + 3), lambda: weight_load(3).start(), (jobs[1], 1))
-    hook(total * 6 // 8, lambda: weight_load(3).wait(), (jobs[0], 2), lambda: flush_copy(0).start())
-    hook(total * 7 // 8, *rest_of(jobs[0], 3), (jobs[1], 2))
+    hook(total * 2 // 8, lambda: weight_load(1).wait(), lambda: weight_load(2).start(), (gather, last + 1), (job, 0))
+    hook(total * 4 // 8, lambda: weight_load(2).wait(), (gather, last + 2), lambda: flush_copy(3).start(), (job, 1))
+    hook(total * 5 // 8, *rest_of(gather, last + 3), lambda: weight_load(3).start())
+    hook(total * 6 // 8, lambda: weight_load(3).wait(), lambda: flush_copy(0).start(), (job, 2))
+    hook(total * 7 // 8, *rest_of(job, 3))
 
     def flush_copy(i):
         pairs = (
-            (grads.at[2], grad2), (grads.at[3], grad3), (grads.at[0, 0], part0), (grads.at[1, 0], part1),
+            (grads.at[2], grad2), (grads.at[3], grad3), (grads.at[0, 0], part0), (grads.at[1], grad1),
             (low, output_out), (gacc, middle_out), (attended, att_out),
         )
         return pltpu.make_async_copy(*pairs[i], flush.at[i])
@@ -908,8 +948,6 @@
         out_grad[flip(place.b, j)] = nn(grad_t[j * r : (j + 1) * r, :], attended[...]).astype(BF16)
     attended[...] = nn(ffn_in[...], out_t[...]).astype(BF16)
     flush_copy(6).start()
-    go(jobs[1], *range(3, jobs[1].stages))
-    flush_copy(3).start()
     for i in range(7):
         flush_copy(i).wait()
     place.drain()
@@ -917,7 +955,7 @@
 
 def ffn(nb, nz, mixed, attended, out_t, norms, cot, ff0, ff1, ff2, ff_w):
     rows, d = mixed.shape
-    _, r, width = ff_w.shape
+    r, width = ff_w.shape
     wide = nz * width
     V, S, D = pltpu.VMEM, jax.ShapeDtypeStruct, pltpu.SemaphoreType.DMA
     scratch = [
@@ -936,8 +974,7 @@
         D((4,)), D((2,)), D((7,)),
     ]
     scratch += Gather.scratch(nb, nz)
-    for _ in range(2):
-        scratch += Scatter.scratch(nb, nz, r, wide, sums=False, line=False)
+    scratch += Scatter.scratch(nb, nz, r, wide, sums=False, line=False)
     return pl.pallas_call(
         functools.partial(ffn_kernel, nb, nz),
         out_shape=[
@@ -945,8 +982,8 @@
             S((rows, d), F32),
             S((rows, d), BF16),
             S((nb, r, d), BF16),
-            *[S((r, wide), BF16)] * 2,
-            *[S((nb, r, wide), BF16)] * 2,
+            S((r, wide), BF16),
+            *[S((nb, r, wide), BF16)] * 3,
             S((2, 8, d), F32),
             S((d, wide), BF16),
         ],
@@ -960,7 +997,7 @@
 
 
 def attention_kernel(
-    nb, nz, att_grad, qkv_in, probs, part0, part1, grad2, grad3, out_grad,
+    nb, nz, att_grad, qkv_in, probs, part0, grad1, grad2, out_grad,
     dqkv, ff_share, out_share,
     qkv, dout, pbuf, dk, dv, q_t, do_t, load, psem, att_send, att_recv, *rest,
 ):
@@ -972,16 +1009,22 @@
     pz = pairs // 2
     place.greet()
 
-    def att_copy(r):
+    def att_copy(r, pair):
         owner = lax.rem(z + r, nz)
         item, member = lax.div(owner, place.half), lax.rem(owner, place.half)
+        slot = pair * (nz - 1) + r - 1
         return remote(
-            att_grad.at[part(item, frames), part(member, wide)], dout.at[part(z, frames)],
-            att_send.at[r - 1], att_recv.at[r - 1], (place.b, owner),
+            att_grad.at[part(item, frames), part(member * pairs + pair, 128)],
+            dout.at[part(z, frames), part(pair, 128)],
+            att_send.at[slot], att_recv.at[slot], (place.b, owner),
         )
 
-    for r in range(1, nz):
-        place.start(att_copy, r)
+    def att_start(pair):
+        for r in range(1, nz):
+            att_copy(r, pair).start()
+
+    for pair in range(min(2, pairs)):
+        att_start(pair)
     own = pltpu.make_async_copy(att_grad.at[part(group, frames), part(k, wide)], dout.at[part(z, frames)], load.at[0])
     own.start()
     qkv_load = pltpu.make_async_copy(qkv_in, qkv, load.at[1])
@@ -993,12 +1036,12 @@
         mine = [rest.pop(0) for _ in range(count)]
         return Scatter(place, full, share, mine, **kind)
 
-    early = [job(None, ff_share.at[i], plane=False) for i in (0, 1)]
-    late = [job(g, ff_share.at[2 + i]) for i, g in enumerate((grad2, grad3))]
+    early = [job(None, ff_share.at[0], plane=False)]
+    late = [job(g, ff_share.at[1 + i]) for i, g in enumerate((grad1, grad2))]
     out_job = job(out_grad, out_share)
     go = lambda job, *stages: [job.stage(t) for t in stages if t < job.stages]
     early_loads = [
-        pltpu.make_async_copy(p, e.sums.at[0], load.at[2 + i]) for i, (p, e) in enumerate(zip((part0, part1), early))
+        pltpu.make_async_copy(p, e.sums.at[0], load.at[2 + i]) for i, (p, e) in enumerate(zip((part0,), early))
     ]
     for one in early_loads:
         one.start()
@@ -1018,8 +1061,6 @@
         return pltpu.make_async_copy(probs.at[pair, :, part(q, QUERIES)], pbuf.at[slot], psem.at[slot])
 
     probs_copy(0).start()
-    for r in range(1, nz):
-        att_copy(r).wait_recv()
     hooks = {}
 
     def hook(it, *steps):
@@ -1027,14 +1068,14 @@
 
     zs = place.nz - 1
     rest_of = lambda job, t: [(job, s) for s in range(t, job.stages)]
-    hook(0, (late[1], 1), *[lambda one=one: one.wait() for one in early_loads], (early[0], 0), (early[1], 0))
-    hook(total // 8, (late[0], 2), (early[0], 1), (early[1], 1))
-    hook(total * 2 // 8, (out_job, 1), *[(early[0], t) for t in range(2, zs)], *[(early[1], t) for t in range(2, zs)])
-    hook(total * 3 // 8, (late[1], 2), (early[0], zs), (early[1], zs))
-    hook(total * 4 // 8, (late[0], 3))
-    hook(total * 5 // 8, (out_job, 2), (late[0], 4))
-    hook(total * 6 // 8, (late[1], 3), (late[0], 5))
-    hook(total * 7 // 8, (late[1], 4), (out_job, 3))
+    hook(0, *[lambda one=one: one.wait() for one in early_loads], (early[0], 0))
+    hook(total // 8, (late[1], 1), (early[0], 1))
+    hook(total * 2 // 8, (late[0], 2), *[(early[0], t) for t in range(2, zs)])
+    hook(total * 3 // 8, (out_job, 1), (early[0], zs))
+    hook(total * 4 // 8, (late[1], 2))
+    hook(total * 5 // 8, (late[0], 3), (out_job, 2))
+    hook(total * 6 // 8, (late[0], 4))
+    hook(total * 7 // 8, (late[1], 3), (late[0], 5), (out_job, 3))
 
     def body(it, carry):
         pair, q = lax.div(it, blocks), lax.rem(it, blocks)
@@ -1050,6 +1091,9 @@
 
         @pl.when(q == 0)
         def _():
+            for r in range(1, nz):
+                att_copy(r, pair).wait_recv()
+            pl.when(pair + 2 < pairs)(lambda: att_start(pair + 2))
             dk[...] = jnp.zeros_like(dk)
             dv[...] = jnp.zeros_like(dv)
 
@@ -1070,12 +1114,15 @@
     lax.fori_loop(0, total, body, 0)
     for t in range(4, out_job.stages + 1):
         go(out_job, t)
-        go(late[1], t + 1)
+        go(late[1], t)
         go(late[0], t + 2)
+    for pair in range(pairs):
+        for r in range(1, nz):
+            att_copy(r, pair).wait_send()
     place.drain()
 
 
-def attention_back(nb, nz, att_grad, qkv, probs, part0, part1, grad2, grad3, out_grad):
+def attention_back(nb, nz, att_grad, qkv, probs, part0, grad1, grad2, out_grad):
     _, pairs, keys, _ = qkv.shape
     S, V, D = jax.ShapeDtypeStruct, pltpu.VMEM, pltpu.SemaphoreType.DMA
     _, r, wide = grad2.shape
@@ -1087,31 +1134,31 @@
         V((128, keys), F32),
         V((128, QUERIES), BF16),
         V((128, QUERIES), BF16),
-        D((4,)), D((2,)), D((nz - 1,)), D((nz - 1,)),
+        D((4,)), D((2,)), D((pairs * (nz - 1),)), D((pairs * (nz - 1),)),
     ]
-    for _ in range(2):
-        scratch += Scatter.scratch(nb, nz, r, wide, plane=False)
-    for g in (grad2, grad3, out_grad):
+    scratch += Scatter.scratch(nb, nz, r, wide, plane=False)
+    for g in (grad1, grad2, out_grad):
         scratch += Scatter.scratch(nb, nz, r, g.shape[2])
     return pl.pallas_call(
         functools.partial(attention_kernel, nb, nz),
         out_shape=[
             S((keys, 3 * pairs * 128), BF16),
-            S((4, r, wide // nz), F32),
+            S((3, r, wide // nz), F32),
             S((r, out_grad.shape[2] // nz), F32),
         ],
-        in_specs=[ANY] * 8,
+        in_specs=[ANY] * 7,
         out_specs=[WHOLE] * 3,
         scratch_shapes=scratch,
         compiler_params=pltpu.CompilerParams(
             collective_id=1, has_side_effects=True, vmem_limit_bytes=VMEM_LIMIT
         ),
-    )(att_grad, qkv, probs, part0, part1, grad2, grad3, out_grad)
+    )(att_grad, qkv, probs, part0, grad1, grad2, out_grad)
 
 
 def first_kernel(
-    nb, nz, dqkv, everything, qkvw, x, skip_x, skip_w, mixed, middle_grad, norms, second_sums,
-    input_grad, skip_grad, qkv_share, skip_share, norm_share,
+    nb, nz, dqkv_in, everything_in, qkvw_in, x, skip_x, skip_w, mixed_in, middle_in, norms, second_sums, grad3,
+    input_grad, skip_grad, qkv_share, skip_share, norm_share, ff_share,
+    dqkv, everything, qkvw, mixed, middle_grad,
     qkv_grad, skip_w_grad, weight, joined, joined_t, mixed_low, ahead, mine, from_mate, to_partner, from_partner,
     sums, packed, norm_in, norm_line, load, swap_send, swap_recv, norm_send, norm_recv, *rest,
 ):
@@ -1119,17 +1166,45 @@
     z, group, k, half = place.z, place.group, place.k, place.half
     frames = x.shape[0] // 2
     width = x.shape[1]
-    per = len(rest) // 2
-    place.greet()
-    qkv_job = Scatter(place, qkv_grad, qkv_share, rest[:per], True, sums=False)
-    skip_job = Scatter(place, skip_w_grad, skip_share, rest[per:], sums=False)
     loads = [
-        pltpu.make_async_copy(x, joined.at[:, pl.ds(0, width)], load.at[0]),
-        pltpu.make_async_copy(skip_x, joined.at[:, pl.ds(width, width)], load.at[1]),
-        pltpu.make_async_copy(skip_w, weight, load.at[2]),
+        pltpu.make_async_copy(src, dst, load.at[i])
+        for i, (src, dst) in enumerate(
+            (
+                (dqkv_in, dqkv),
+                (qkvw_in, qkvw),
+                (everything_in, everything),
+                (mixed_in, mixed),
+                (middle_in, middle_grad),
+                (x, joined.at[:, pl.ds(0, width)]),
+                (skip_x, joined.at[:, pl.ds(width, width)]),
+                (skip_w, weight),
+            )
+        )
     ]
     for one in loads:
         one.start()
+    place.greet()
+    per = len(rest) // 4
+    ff_job = Scatter(place, grad3, ff_share, rest[: per + 1])
+    rest = rest[per + 1 :]
+    per = len(rest) // 3
+    qkv_job = Scatter(place, qkv_grad, qkv_share, rest[:per], True, sums=False)
+    rs = skip_w_grad.shape[2]
+    skips = [
+        Scatter(
+            place, skip_w_grad.at[h], skip_share.at[pl.ds(h * rs, rs)], rest[(1 + h) * per : (2 + h) * per], sums=False
+        )
+        for h in (0, 1)
+    ]
+
+    def go(job, *stages):
+        for t in stages:
+            if t < job.stages:
+                job.stage(t)
+
+    go(ff_job, 0)
+    for one in loads[:2]:
+        one.wait()
 
     def mate_copy(r, t):
         slot = (r - 1) * 2 + t
@@ -1145,11 +1220,13 @@
     for s in (0, 1):
         block = k + (1 - group if s == 0 else group) * half
         mine[s] = nt(dqkv[part(block, frames), :], qkvw[...])
+    loads[2].wait()
     turned = everything[...].T
     rq = qkv_grad.shape[1]
     for j in range(nb):
         qkv_grad[flip(place.b, j)] = nn(turned[j * rq : (j + 1) * rq, :], dqkv[...]).astype(BF16)
-    qkv_job.stage(0)
+    go(qkv_job, 0)
+    go(ff_job, 1)
 
     def add_mates(s):
         for r in range(1, half):
@@ -1172,10 +1249,11 @@
     place.start(across)
     for r in range(1, half):
         place.start(mate_copy, r, 1)
-    for one in loads:
+    for one in loads[3:]:
         one.wait()
     joined_t[...] = joined[...].T
-    qkv_job.stage(1)
+    go(qkv_job, 1)
+    go(ff_job, 2)
 
     sums[...] = jnp.zeros_like(sums)
     gain = norms[0:1, :]
@@ -1192,12 +1270,14 @@
 
     add_mates(1)
     back(group, lambda at: mine[1, at])
+    go(ff_job, 3)
     across().wait_recv()
     back(1 - group, lambda at: from_partner[at].astype(F32))
-    rs = skip_w_grad.shape[1]
-    for j in range(nb):
-        skip_w_grad[flip(place.b, j)] = nn(joined_t[j * rs : (j + 1) * rs, :], mixed_low[...]).astype(BF16)
-    skip_job.stage(0)
+    for h in (0, 1):
+        for j in range(nb):
+            block = slice((2 * j + h) * rs, (2 * j + h + 1) * rs)
+            skip_w_grad[h, flip(place.b, j)] = nn(joined_t[block, :], mixed_low[...]).astype(BF16)
+        go(skips[h], 0)
 
     total = lambda a: jnp.sum(a, 0, keepdims=True)
     for i, v in enumerate((sums[0], sums[1], second_sums[0], second_sums[1])):
@@ -1224,21 +1304,25 @@
                 line_copy(r).start()
 
     norm_step(0)
-    skip_job.stage(1)
+    go(qkv_job, 2)
+    go(skips[0], 1)
+    go(skips[1], 1)
     norm_step(1)
-    qkv_job.stage(2)
-    for t in range(2):
-        (input_grad, skip_grad)[t][...] = nt(mixed_low[...], weight[pl.ds(t * width, width), :])
-        norm_step(2 + t)
+    go(ff_job, 4)
+    input_grad[...] = nt(mixed_low[...], weight[pl.ds(0, width), :])
+    go(skips[0], 2)
+    norm_step(2)
+    go(qkv_job, 3)
+    skip_grad[...] = nt(mixed_low[...], weight[pl.ds(width, width), :])
+    go(skips[1], 2)
+    norm_step(3)
     for i in range(4, len(bits) + 1):
         norm_step(i)
-    skip_job.stage(2)
-    qkv_job.stage(3)
-    for t in range(3, max(skip_job.stages, qkv_job.stages - 1)):
-        if t < skip_job.stages:
-            skip_job.stage(t)
-        if t + 1 < qkv_job.stages:
-            qkv_job.stage(t + 1)
+    for t in range(3, max(skips[0].stages, qkv_job.stages - 1, ff_job.stages - 2)):
+        go(skips[0], t)
+        go(skips[1], t)
+        go(qkv_job, t + 1)
+        go(ff_job, t + 2)
     value = packed[:, part(z, c)]
     for r in range(1, nz):
         line_copy(r).wait()
@@ -1247,7 +1331,7 @@
     place.drain()
 
 
-def first_back(nb, nz, dqkv, everything, qkvw, x, skip_x, skip_w, mixed, middle_grad, norms, second_sums):
+def first_back(nb, nz, dqkv, everything, qkvw, x, skip_x, skip_w, mixed, middle_grad, norms, second_sums, grad3):
     rows, width = x.shape
     frames = rows // 2
     half = nz // 2
@@ -1257,8 +1341,13 @@
     bits = nb.bit_length() - 1
     swaps = 2 * (half - 1)
     scratch = [
+        V(dqkv.shape, BF16),
+        V(everything.shape, BF16),
+        V(qkvw.shape, BF16),
+        V((rows, width), F32),
+        V((rows, width), F32),
         V((nb, qkvw.shape[0] // nb, qkv_wide), BF16),
-        V((nb, skip_w.shape[0] // nb, width), BF16),
+        V((2, nb, skip_w.shape[0] // nb // 2, width), BF16),
         V(skip_w.shape, BF16),
         V((rows, 2 * width), BF16),
         V((2 * width, rows), BF16),
@@ -1272,10 +1361,12 @@
         V((8, width), F32),
         V((bits, 8, width), F32),
         V((nz - 1, 8, c), F32),
-        D((3,)), D((swaps + 1,)), D((swaps + 1,)), D((bits + nz - 1,)), D((bits + nz - 1,)),
+        D((8,)), D((swaps + 1,)), D((swaps + 1,)), D((bits + nz - 1,)), D((bits + nz - 1,)),
     ]
+    scratch += Scatter.scratch(nb, nz, grad3.shape[1], grad3.shape[2])
     scratch += Scatter.scratch(nb, nz, qkvw.shape[0] // nb, qkv_wide, True, sums=False)
-    scratch += Scatter.scratch(nb, nz, skip_w.shape[0] // nb, width, sums=False)
+    for _ in (0, 1):
+        scratch += Scatter.scratch(nb, nz, skip_w.shape[0] // nb // 2, width, sums=False)
     return pl.pallas_call(
         functools.partial(first_kernel, nb, nz),
         out_shape=[
@@ -1284,14 +1375,15 @@
             S((qkvw.shape[0] // nb, qkv_wide // 2), F32),
             S((skip_w.shape[0] // nb, c), F32),
             S((8, c), F32),
+            S((grad3.shape[1], grad3.shape[2] // nz), F32),
         ],
-        in_specs=[WHOLE] * 3 + [ANY] * 3 + [WHOLE] * 4,
-        out_specs=[WHOLE] * 5,
+        in_specs=[ANY] * 8 + [WHOLE] * 2 + [ANY],
+        out_specs=[WHOLE] * 6,
         scratch_shapes=scratch,
         compiler_params=pltpu.CompilerParams(
             collective_id=2, has_side_effects=True, vmem_limit_bytes=VMEM_LIMIT
         ),
-    )(dqkv, everything, qkvw, x, skip_x, skip_w, mixed, middle_grad, norms, second_sums)
+    )(dqkv, everything, qkvw, x, skip_x, skip_w, mixed, middle_grad, norms, second_sums, grad3)
 
 
 def shards(
@@ -1315,27 +1407,23 @@
     shape = inputs.shape
     flat = lambda a: a.reshape(shape[0] * shape[1], shape[2])
     x, skip_x, cot = flat(inputs), flat(skip_input), flat(cotangent)
-    norms = jnp.stack([first_gain, first_shift, second_gain, second_shift]).astype(F32)
-    norms = jnp.pad(norms, ((0, 4), (0, 0)))
-    qkv_shard = jnp.concatenate([query_weight, key_weight, value_weight], 1)
+    norms = (first_gain, first_shift, second_gain, second_shift)
+    qkv_w = (query_weight, key_weight, value_weight)
+    (mixed, everything, gains, skip_w, qkvw, out_t, ff0, ff1, ff2, ff3_w, qkv, probs, attended) = forward(
+        nb, nz, lengths, x, skip_x, norms, skip_weight, qkv_w, out_weight, up_weight, down_weight
+    )
+    output, middle_grad, att_grad, out_grad, part0, grad1, grad2, grad3, second_sums, _ = ffn(
+        nb, nz, mixed, attended, out_t, gains, cot, ff0, ff1, ff2, ff3_w
+    )
+    dqkv, ff_share, out_share = attention_back(nb, nz, att_grad, qkv, probs, part0, grad1, grad2, out_grad)
+    input_grad, skip_grad, qkv_share, skip_share, norm_share, ff_last = first_back(
+        nb, nz, dqkv, everything, qkvw, x, skip_x, skip_w, mixed, middle_grad, gains, second_sums, grad3
+    )
     cw = up_weight.shape[1] // 4
-    chunks = lambda w: w.reshape(w.shape[0], 4, cw)
-    ff_w = jnp.concatenate([chunks(up_weight), chunks(down_weight.T)], 2).transpose(1, 0, 2)
-    (mixed, everything, gains, skip_w, qkvw, out_t, ff0, ff1, ff2, qkv, probs, attended) = forward(
-        nb, nz, lengths, x, skip_x, norms, skip_weight, qkv_shard, out_weight.T, ff_w
-    )
-    output, middle_grad, att_grad, out_grad, part0, part1, grad2, grad3, second_sums, _ = ffn(
-        nb, nz, mixed, attended, out_t, gains, cot, ff0, ff1, ff2, ff_w
-    )
-    dqkv, ff_share, out_share = attention_back(
-        nb, nz, att_grad, qkv, probs, part0, part1, grad2, grad3, out_grad
-    )
+    ff_share = jnp.concatenate([ff_share, ff_last[None]], 0)
     up_share, dn_share = [
         ff_share[:, :, i * cw : (i + 1) * cw].transpose(1, 0, 2).reshape(up_weight.shape) for i in (0, 1)
     ]
-    input_grad, skip_grad, qkv_share, skip_share, norm_share = first_back(
-        nb, nz, dqkv, everything, qkvw, x, skip_x, skip_w, mixed, middle_grad, gains, second_sums
-    )
     c = query_weight.shape[1]
     return (
         output.reshape(shape),

time: 418 us -> 374 us (0.89)
  Pallas kernels: 395 us -> 360 us
  local copies, waits for them, and re-layouts: 18.6 us -> 10.9 us
    pallas_call x1, Pallas kernels: 80.8 us -> 65.8 us  [ffn(): pl.pallas_call(functools.partial(ffn_kernel, nb, nz), out_shape=[S((rows,...]
    pallas_call x1, Pallas kernels: 142 us -> 131 us  [forward(): pl.pallas_call(functools.partial(forward_kernel, nb, nz), out_shape=out_s...]
    pallas_call x1, Pallas kernels: 78.4 us -> 73.6 us  [attention_back(): pl.pallas_call(functools.partial(attention_kernel, nb, nz), out_shape=[S(...]
    pallas_call x1, Pallas kernels: 94.3 us -> 89.7 us  [first_back(): pl.pallas_call(functools.partial(first_kernel, nb, nz), out_shape=[S((row...]
where the time goes in v4:
time: 374 us; the launch traced here: 372 us
  Pallas kernels  360 us (96%)
  local copies, waits for them, and re-layouts  10.9 us (3%)
    pallas_call x1, Pallas kernels, forward(): pl.pallas_call(functools.partial(forward_kernel, nb, nz), out_shape=out_s...  131 us
    pallas_call x1, Pallas kernels, first_back(): pl.pallas_call(functools.partial(first_kernel, nb, nz), out_shape=[S((row...  89.7 us
    pallas_call x1, Pallas kernels, attention_back(): pl.pallas_call(functools.partial(attention_kernel, nb, nz), out_shape=[S(...  73.6 us
    pallas_call x1, Pallas kernels, ffn(): pl.pallas_call(functools.partial(ffn_kernel, nb, nz), out_shape=[S((rows,...  65.8 us
    unnamed x18, local copies, waits for them, and re-layouts  7.53 us

profile of v4, /device:TPU:0, one launch (start us, length us, event | category | flops | bytes accessed | tf_op | source)
XLA Modules:
  0.0 372.3 jit_solution(17923657848223248470)
XLA Ops:
  0.7 130.5 %shard_map.254 = (f32[512,1024]{1,0:T(8,128)}, bf16[1024,1024]{1,0:T(8,128)(2,1)}, f32[8,1024]{1,0:T(8,128)}, bf16[2048,1024]{1,0:T(8,128)(2,1)}, bf16[1024,1536...) custom-call(s32[2]{0:T(128)} %lengths.1, ...), custom_call_target="tpu_custom_call" | custom-call | tf_op jit(solution)/shard_map/pallas_call | solution.py:822
  131.2 65.8 %shard_map.255 = (bf16[512,1024]{1,0:T(8,128)(2,1)}, f32[512,1024]{1,0:T(8,128)}, bf16[512,1024]{1,0:T(8,128)(2,1)}, bf16[8,128,1024]{2,1,0:T(8,128)(2,1)}, bf16...) custom-call(f32[512,1024]{1,0:T(8,128)} %get-tuple-element.45.mixed_, ...), custom_call_target="tpu_custom_call" | custom-call | tf_op jit(solution)/shard_map/pallas_call | solution.py:978
  197.0 73.6 %shard_map.256 = (bf16[1024,1536]{1,0:T(8,128)(2,1)}, f32[3,128,512]{2,1,0:T(8,128)}, f32[128,256]{1,0:T(8,128)}) custom-call(bf16[512,1024]{1,0:T(8,128)(2,1)} %get-tuple-element.54.att_grad, bf16[3,4,1024,128]{3,2,1,0:T(8,128)(2,1)} %get-tuple-element.55.qkv_in, bf16[4,2,1024,1024]{3,2,1,0:T(8,128)(2,1)} %get-tuple-element.56.probs, ...), custom_call_target="tpu_custom_call" | custom-call | tf_op jit(solution)/shard_map/pallas_call | solution.py:1142
  270.6 0.0 copy-start.5
  270.6 0.0 copy-start.2
  270.6 89.7 %shard_map.257 = (f32[512,1024]{1,0:T(8,128)}, f32[512,1024]{1,0:T(8,128)}, f32[128,768]{1,0:T(8,128)}, f32[256,256]{1,0:T(8,128)}, f32[8,256]{1,0:T(8,128)}, /*index=5*/f32[128,512]{1,0:T(8,128)}) custom-call(bf16[1024,1536]{1,0:T(8,128)(2,1)} %get-tuple-element.61.dqkv_in, bf16[1024,1024]{1,0:T(8,128)(2,1)} %get-tuple-element.62.everything_in, ...), custom_call_target="tpu_custom_call" | custom-call | tf_op jit(solution)/shard_map/pallas_call | solution.py:1370
  360.3 0.0 copy-start.3
  360.3 0.0 copy-done.5
  360.3 0.8 copy.32
  361.1 1.4 fusion.4
  362.5 0.0 copy-done.2
  362.5 1.1 fusion.2
  363.6 0.0 copy-start.1
  363.6 1.0 copy.31
  364.6 0.0 copy-done.3
  364.6 0.8 fusion.3
  365.3 0.2 copy.30
  365.5 1.0 copy.33
  366.5 0.0 copy-start
  366.5 2.4 copy.38
  369.0 0.0 copy-done.1
  369.0 1.3 copy.39
  370.3 0.0 copy-done
  370.3 0.0 copy-start.4
  370.3 1.3 copy.40
  371.6 0.0 copy-done.4
  371.6 0.7 copy.41
Async XLA Ops:
  270.6 89.7 %copy-start.5 = (f32[128,256]{1,0:T(8,128)S(1)}, f32[128,256]{1,0:T(8,128)}, u32[]{:S(2)}) copy-start(f32[128,256]{1,0:T(8,128)} %get-tuple-element.72) | copy-start | bytes 393220
  270.6 91.9 %copy-start.2 = (f32[3,128,512]{2,1,0:T(8,128)S(1)}, f32[3,128,512]{2,1,0:T(8,128)}, u32[]{:S(2)}) copy-start(f32[3,128,512]{2,1,0:T(8,128)} %get-tuple-element.73) | copy-start | bytes 2359300
  360.3 4.3 %copy-start.3 = (f32[128,768]{1,0:T(8,128)S(1)}, f32[128,768]{1,0:T(8,128)}, u32[]{:S(2)}) copy-start(f32[128,768]{1,0:T(8,128)} %get-tuple-element.71) | copy-start | bytes 1179652
  363.6 5.4 %copy-start.1 = (f32[512,1024]{1,0:T(8,128)S(1)}, f32[512,1024]{1,0:T(8,128)}, u32[]{:S(2)}) copy-start(f32[512,1024]{1,0:T(8,128)} %get-tuple-element.68) | copy-start | bytes 6291460
  366.5 3.7 %copy-start = (f32[512,1024]{1,0:T(8,128)S(1)}, f32[512,1024]{1,0:T(8,128)}, u32[]{:S(2)}) copy-start(f32[512,1024]{1,0:T(8,128)} %get-tuple-element.69) | copy-start | bytes 6291460
  370.3 1.3 copy-start.4

commit v5 on v4

--- a/solution.py
+++ b/solution.py
@@ -606,24 +606,20 @@
         ff_w[i, :, cw:] = down_t[:, i * cw : (i + 1) * cw]
     both(*range(1, last))
     go(qkv_job, 0)
-    go(skips[0], last)
-    go(out_job, 0)
-    go(skips[1], last)
+    both(last)
     for one in up_loads:
         one.wait()
-    go(skips[0], last + 1)
-    go(out_job, 1)
-    go(skips[1], last + 1)
-    go(out_job, *range(2, last))
     go(ff[0], 0)
+    both(last + 1)
     go(skips[0], last + 2)
-    go(ff[0], 1)
+    go(ff[0], *range(1, last))
+    go(ff[1], 0)
     go(skips[1], last + 2)
-    go(ff[0], *range(2, last))
+    go(ff[1], *range(1, last - 1))
     go(qkv_job, 1)
-    go(out_job, last)
-    go(ff[1], 0)
+    go(ff[0], last)
     both(*range(last + 3, skips[0].stages))
+    go(ff[1], last - 1)
     flushes = []
 
     def out_copy(src, dst):
@@ -663,9 +659,6 @@
         if turn == 0:
             place.start(across)
             go(qkv_job, 2)
-            go(out_job, last + 1)
-            go(ff[0], last)
-            go(ff[1], 1)
         else:
             own = pltpu.make_async_copy(normed.at[item], everything.at[part(z, frames)], load.at[0])
             own.start()
@@ -678,27 +671,25 @@
     for r in range(1, half):
         place.start(mate_copy, normed.at[group], z, r, r)
     out_copy(mixed, mixed_out)
-    go(ff[1], *range(2, last))
+    go(ff[0], last + 1)
+    go(ff[1], last)
     distances(dist, lengths[group])
     go(qkv_job, 3)
-    go(out_job, last + 2)
-    go(ff[0], last + 1)
+    go(ff[0], last + 2)
     across().wait_recv()
     for r in range(1, half):
         block = everything.at[part(place.partner, frames)]
         place.start(mate_copy, block, place.partner, r, half - 1 + r)
-    go(ff[1], last)
-    go(ff[2], 0)
+    go(ff[1], last + 1)
     go(qkv_job, *range(4, qkv_job.stages))
-    go(out_job, *range(last + 3, out_job.stages))
     out_copy(qkvw, qkvw_out)
-    go(ff[0], last + 2)
     own.wait()
     for r in range(1, half):
         mate_copy(normed.at[group], z, r, r).wait_recv()
         mate_copy(normed.at[group], z, r, half - 1 + r).wait_recv()
     out_copy(everything, normed_out)
-    go(ff[2], 1)
+    go(ff[2], 0)
+    go(out_job, 0)
 
     project(everything, qkvw, qkv, pz)
     out_copy(qkv, qkv_out)
@@ -731,12 +722,14 @@
         hooks.setdefault(min(it, total - 1), []).extend(steps)
 
     rest_of = lambda job, t: [(job, s) for s in range(t, job.stages)]
-    hook(0, *[(ff[2], t) for t in range(2, last)], (ff[1], last + 1))
-    hook(total // 8, (ff[2], last), *rest_of(ff[0], last + 3))
-    hook(total * 3 // 8, (ff[1], last + 2))
-    hook(total * 4 // 8, (ff[2], last + 1))
-    hook(total * 6 // 8, *rest_of(ff[1], last + 3))
-    hook(total - 1, (ff[2], last + 2))
+    for t in range(1, last):
+        hook(t - 1, (ff[2], t), (out_job, t))
+    hook(last - 1, (ff[1], last + 2), (ff[2], last), (out_job, last))
+    hook(total * 4 // 16, *rest_of(ff[0], last + 3))
+    hook(total * 6 // 16, (ff[2], last + 1), (out_job, last + 1))
+    hook(total * 8 // 16, *rest_of(ff[1], last + 3))
+    hook(total * 13 // 16, (ff[2], last + 2))
+    hook(total * 15 // 16, (out_job, last + 2))
 
     def body(it, carry):
         pair, q = lax.div(it, blocks), lax.rem(it, blocks)
@@ -765,6 +758,7 @@
     for pair in range(pairs):
         att_own(pair).start()
     go(ff[2], *range(last + 3, ff[2].stages))
+    go(out_job, *range(last + 3, out_job.stages))
     for pair in range(pairs):
         for r in range(1, nz):
             att_copy(pair, r).wait()
@@ -997,8 +991,8 @@
 
 
 def attention_kernel(
-    nb, nz, att_grad, qkv_in, probs, part0, grad1, grad2, out_grad,
-    dqkv, ff_share, out_share,
+    nb, nz, att_grad, qkv_in, probs, part0, grad1, grad2,
+    dqkv, ff_share, part2,
     qkv, dout, pbuf, dk, dv, q_t, do_t, load, psem, att_send, att_recv, *rest,
 ):
     place = Place(nb, nz)
@@ -1037,8 +1031,7 @@
         return Scatter(place, full, share, mine, **kind)
 
     early = [job(None, ff_share.at[0], plane=False)]
-    late = [job(g, ff_share.at[1 + i]) for i, g in enumerate((grad1, grad2))]
-    out_job = job(out_grad, out_share)
+    late = [job(grad1, ff_share.at[1]), job(grad2, None, line=False)]
     go = lambda job, *stages: [job.stage(t) for t in stages if t < job.stages]
     early_loads = [
         pltpu.make_async_copy(p, e.sums.at[0], load.at[2 + i]) for i, (p, e) in enumerate(zip((part0,), early))
@@ -1047,7 +1040,6 @@
         one.start()
     go(late[0], 0)
     go(late[1], 0)
-    go(out_job, 0)
     go(late[0], 1)
     own.wait()
     qkv_load.wait()
@@ -1069,13 +1061,14 @@
     zs = place.nz - 1
     rest_of = lambda job, t: [(job, s) for s in range(t, job.stages)]
     hook(0, *[lambda one=one: one.wait() for one in early_loads], (early[0], 0))
-    hook(total // 8, (late[1], 1), (early[0], 1))
-    hook(total * 2 // 8, (late[0], 2), *[(early[0], t) for t in range(2, zs)])
-    hook(total * 3 // 8, (out_job, 1), (early[0], zs))
-    hook(total * 4 // 8, (late[1], 2))
-    hook(total * 5 // 8, (late[0], 3), (out_job, 2))
-    hook(total * 6 // 8, (late[0], 4))
-    hook(total * 7 // 8, (late[1], 3), (late[0], 5), (out_job, 3))
+    hook(total * 2 // 16, (early[0], 1))
+    hook(total * 4 // 16, (late[0], 2), *[(early[0], t) for t in range(2, zs)])
+    hook(total * 5 // 16, (late[1], 1))
+    hook(total * 6 // 16, (early[0], zs))
+    hook(total * 8 // 16, (late[0], 3))
+    hook(total * 10 // 16, (late[0], 4))
+    hook(total * 11 // 16, (late[1], 2))
+    hook(total * 12 // 16, (late[0], 5))
 
     def body(it, carry):
         pair, q = lax.div(it, blocks), lax.rem(it, blocks)
@@ -1112,17 +1105,18 @@
         return carry
 
     lax.fori_loop(0, total, body, 0)
-    for t in range(4, out_job.stages + 1):
-        go(out_job, t)
-        go(late[1], t)
-        go(late[0], t + 2)
+    go(late[0], *range(6, late[0].stages))
+    go(late[1], *range(3, late[1].stages))
+    part_copy = pltpu.make_async_copy(late[1].sums.at[0], part2, load.at[0])
+    part_copy.start()
     for pair in range(pairs):
         for r in range(1, nz):
             att_copy(r, pair).wait_send()
+    part_copy.wait()
     place.drain()
 
 
-def attention_back(nb, nz, att_grad, qkv, probs, part0, grad1, grad2, out_grad):
+def attention_back(nb, nz, att_grad, qkv, probs, part0, grad1, grad2):
     _, pairs, keys, _ = qkv.shape
     S, V, D = jax.ShapeDtypeStruct, pltpu.VMEM, pltpu.SemaphoreType.DMA
     _, r, wide = grad2.shape
@@ -1137,29 +1131,30 @@
         D((4,)), D((2,)), D((pairs * (nz - 1),)), D((pairs * (nz - 1),)),
     ]
     scratch += Scatter.scratch(nb, nz, r, wide, plane=False)
-    for g in (grad1, grad2, out_grad):
-        scratch += Scatter.scratch(nb, nz, r, g.shape[2])
+    scratch += Scatter.scratch(nb, nz, r, wide)
+    scratch += Scatter.scratch(nb, nz, r, wide, line=False)
     return pl.pallas_call(
         functools.partial(attention_kernel, nb, nz),
         out_shape=[
             S((keys, 3 * pairs * 128), BF16),
-            S((3, r, wide // nz), F32),
-            S((r, out_grad.shape[2] // nz), F32),
+            S((2, r, wide // nz), F32),
+            S((r, wide), BF16),
         ],
-        in_specs=[ANY] * 7,
-        out_specs=[WHOLE] * 3,
+        in_specs=[ANY] * 6,
+        out_specs=[WHOLE, WHOLE, ANY],
         scratch_shapes=scratch,
         compiler_params=pltpu.CompilerParams(
             collective_id=1, has_side_effects=True, vmem_limit_bytes=VMEM_LIMIT
         ),
-    )(att_grad, qkv, probs, part0, grad1, grad2, out_grad)
+    )(att_grad, qkv, probs, part0, grad1, grad2)
 
 
 def first_kernel(
-    nb, nz, dqkv_in, everything_in, qkvw_in, x, skip_x, skip_w, mixed_in, middle_in, norms, second_sums, grad3,
-    input_grad, skip_grad, qkv_share, skip_share, norm_share, ff_share,
+    nb, nz, dqkv_in, everything_in, qkvw_in, x, skip_x, skip_w, mixed_in, middle_in, norms, second_sums, ff_early, part2, grad3, out_grad,
+    input_grad, skip_grad, query_out, key_out, value_out, skip_share, norm_share, up_out, down_out, out_out,
+    qkv_share, ff_share, out_share,
     dqkv, everything, qkvw, mixed, middle_grad,
-    qkv_grad, skip_w_grad, weight, joined, joined_t, mixed_low, ahead, mine, from_mate, to_partner, from_partner,
+    qkv_grad, skip_w_grad, spare, joined, joined_t, mixed_low, ahead, mine, from_mate, to_partner, from_partner,
     sums, packed, norm_in, norm_line, load, swap_send, swap_recv, norm_send, norm_recv, *rest,
 ):
     place = Place(nb, nz)
@@ -1177,25 +1172,27 @@
                 (middle_in, middle_grad),
                 (x, joined.at[:, pl.ds(0, width)]),
                 (skip_x, joined.at[:, pl.ds(width, width)]),
-                (skip_w, weight),
             )
         )
     ]
+    rest = list(rest)
+
+    def job(full, share, paired=False, **kind):
+        count = 3 + sum(kind.get(key, True) and size for key, size in (("sums", 1), ("plane", 2), ("line", 1)))
+        mine = [rest.pop(0) for _ in range(count)]
+        return Scatter(place, full, share, mine, paired, **kind)
+
     for one in loads:
         one.start()
     place.greet()
-    per = len(rest) // 4
-    ff_job = Scatter(place, grad3, ff_share, rest[: per + 1])
-    rest = rest[per + 1 :]
-    per = len(rest) // 3
-    qkv_job = Scatter(place, qkv_grad, qkv_share, rest[:per], True, sums=False)
+    line_job = job(None, ff_share.at[0], plane=False)
+    ff_job = job(grad3, ff_share.at[1])
+    out_job = job(out_grad, out_share)
+    qkv_job = job(qkv_grad, qkv_share, True, sums=False)
     rs = skip_w_grad.shape[2]
-    skips = [
-        Scatter(
-            place, skip_w_grad.at[h], skip_share.at[pl.ds(h * rs, rs)], rest[(1 + h) * per : (2 + h) * per], sums=False
-        )
-        for h in (0, 1)
-    ]
+    skips = [job(skip_w_grad.at[h], skip_share.at[pl.ds(h * rs, rs)], sums=False) for h in (0, 1)]
+    loads.append(pltpu.make_async_copy(part2, line_job.sums.at[0], load.at[7]))
+    loads[7].start()
 
     def go(job, *stages):
         for t in stages:
@@ -1203,6 +1200,7 @@
                 job.stage(t)
 
     go(ff_job, 0)
+    go(out_job, 0)
     for one in loads[:2]:
         one.wait()
 
@@ -1225,8 +1223,13 @@
     rq = qkv_grad.shape[1]
     for j in range(nb):
         qkv_grad[flip(place.b, j)] = nn(turned[j * rq : (j + 1) * rq, :], dqkv[...]).astype(BF16)
+    weights = [everything.at[pl.ds(0, width)], qkvw.at[:, pl.ds(0, width)] if qkvw.shape[1] >= width else spare]
+    for i, ref in enumerate(weights):
+        loads.append(pltpu.make_async_copy(skip_w.at[pl.ds(i * width, width)], ref, load.at[8 + i]))
+        loads[-1].start()
+    go(ff_job, 1)
     go(qkv_job, 0)
-    go(ff_job, 1)
+    go(out_job, 1)
 
     def add_mates(s):
         for r in range(1, half):
@@ -1249,11 +1252,12 @@
     place.start(across)
     for r in range(1, half):
         place.start(mate_copy, r, 1)
-    for one in loads[3:]:
+    for one in loads[3:8]:
         one.wait()
     joined_t[...] = joined[...].T
     go(qkv_job, 1)
     go(ff_job, 2)
+    go(out_job, 2)
 
     sums[...] = jnp.zeros_like(sums)
     gain = norms[0:1, :]
@@ -1270,6 +1274,7 @@
 
     add_mates(1)
     back(group, lambda at: mine[1, at])
+    go(qkv_job, 2)
     go(ff_job, 3)
     across().wait_recv()
     back(1 - group, lambda at: from_partner[at].astype(F32))
@@ -1304,25 +1309,43 @@
                 line_copy(r).start()
 
     norm_step(0)
-    go(qkv_job, 2)
+    go(out_job, 3)
+    go(qkv_job, 3)
+    go(line_job, 0)
     go(skips[0], 1)
     go(skips[1], 1)
     norm_step(1)
     go(ff_job, 4)
-    input_grad[...] = nt(mixed_low[...], weight[pl.ds(0, width), :])
+    go(out_job, 4)
+    go(line_job, 1)
+    for one in loads[8:]:
+        one.wait()
+    input_grad[...] = nt(mixed_low[...], weights[0][...])
     go(skips[0], 2)
     norm_step(2)
-    go(qkv_job, 3)
-    skip_grad[...] = nt(mixed_low[...], weight[pl.ds(width, width), :])
+    go(ff_job, 5)
+    go(out_job, 5)
+    go(line_job, 2)
+    go(qkv_job, *range(4, qkv_job.stages))
+    skip_grad[...] = nt(mixed_low[...], weights[1][...])
     go(skips[1], 2)
     norm_step(3)
+    go(ff_job, *range(6, ff_job.stages))
+    go(out_job, *range(6, out_job.stages))
+    go(line_job, *range(3, line_job.stages))
     for i in range(4, len(bits) + 1):
         norm_step(i)
-    for t in range(3, max(skips[0].stages, qkv_job.stages - 1, ff_job.stages - 2)):
+    for i, ref in enumerate((query_out, key_out, value_out)):
+        ref[...] = qkv_share[:, i * c : (i + 1) * c]
+    out_out[...] = out_share[...].T
+    cw = ff_share.shape[2] // 2
+    for i in range(4):
+        source = ff_early.at[i] if i < 2 else ff_share.at[i - 2]
+        up_out[:, i * cw : (i + 1) * cw] = source[:, :cw]
+        down_out[i * cw : (i + 1) * cw, :] = source[:, cw:].T
+    for t in range(3, skips[0].stages):
         go(skips[0], t)
         go(skips[1], t)
-        go(qkv_job, t + 1)
-        go(ff_job, t + 2)
     value = packed[:, part(z, c)]
     for r in range(1, nz):
         line_copy(r).wait()
@@ -1331,7 +1354,7 @@
     place.drain()
 
 
-def first_back(nb, nz, dqkv, everything, qkvw, x, skip_x, skip_w, mixed, middle_grad, norms, second_sums, grad3):
+def first_back(nb, nz, dqkv, everything, qkvw, x, skip_x, skip_w, mixed, middle_grad, norms, second_sums, ff_early, part2, grad3, out_grad):
     rows, width = x.shape
     frames = rows // 2
     half = nz // 2
@@ -1340,7 +1363,11 @@
     qkv_wide = qkvw.shape[1]
     bits = nb.bit_length() - 1
     swaps = 2 * (half - 1)
+    r, wide = ff_early.shape[1:]
     scratch = [
+        V((r, 3 * c), F32),
+        V((2, r, wide), F32),
+        V((r, c), F32),
         V(dqkv.shape, BF16),
         V(everything.shape, BF16),
         V(qkvw.shape, BF16),
@@ -1348,7 +1375,7 @@
         V((rows, width), F32),
         V((nb, qkvw.shape[0] // nb, qkv_wide), BF16),
         V((2, nb, skip_w.shape[0] // nb // 2, width), BF16),
-        V(skip_w.shape, BF16),
+        V((width, width) if qkv_wide < width else (16, 128), BF16),
         V((rows, 2 * width), BF16),
         V((2 * width, rows), BF16),
         V((rows, width), BF16),
@@ -1361,9 +1388,11 @@
         V((8, width), F32),
         V((bits, 8, width), F32),
         V((nz - 1, 8, c), F32),
-        D((8,)), D((swaps + 1,)), D((swaps + 1,)), D((bits + nz - 1,)), D((bits + nz - 1,)),
+        D((10,)), D((swaps + 1,)), D((swaps + 1,)), D((bits + nz - 1,)), D((bits + nz - 1,)),
     ]
+    scratch += Scatter.scratch(nb, nz, grad3.shape[1], grad3.shape[2], plane=False)
     scratch += Scatter.scratch(nb, nz, grad3.shape[1], grad3.shape[2])
+    scratch += Scatter.scratch(nb, nz, out_grad.shape[1], out_grad.shape[2])
     scratch += Scatter.scratch(nb, nz, qkvw.shape[0] // nb, qkv_wide, True, sums=False)
     for _ in (0, 1):
         scratch += Scatter.scratch(nb, nz, skip_w.shape[0] // nb // 2, width, sums=False)
@@ -1372,18 +1401,20 @@
         out_shape=[
             S((rows, width), F32),
             S((rows, width), F32),
-            S((qkvw.shape[0] // nb, qkv_wide // 2), F32),
+            *[S((r, c), F32)] * 3,
             S((skip_w.shape[0] // nb, c), F32),
             S((8, c), F32),
-            S((grad3.shape[1], grad3.shape[2] // nz), F32),
+            S((r, 2 * wide), F32),
+            S((2 * wide, r), F32),
+            S((c, r), F32),
         ],
-        in_specs=[ANY] * 8 + [WHOLE] * 2 + [ANY],
-        out_specs=[WHOLE] * 6,
+        in_specs=[ANY] * 8 + [WHOLE] * 3 + [ANY] * 3,
+        out_specs=[WHOLE] * 10,
         scratch_shapes=scratch,
         compiler_params=pltpu.CompilerParams(
             collective_id=2, has_side_effects=True, vmem_limit_bytes=VMEM_LIMIT
         ),
-    )(dqkv, everything, qkvw, x, skip_x, skip_w, mixed, middle_grad, norms, second_sums, grad3)
+    )(dqkv, everything, qkvw, x, skip_x, skip_w, mixed, middle_grad, norms, second_sums, ff_early, part2, grad3, out_grad)
 
 
 def shards(
@@ -1415,27 +1446,24 @@
     output, middle_grad, att_grad, out_grad, part0, grad1, grad2, grad3, second_sums, _ = ffn(
         nb, nz, mixed, attended, out_t, gains, cot, ff0, ff1, ff2, ff3_w
     )
-    dqkv, ff_share, out_share = attention_back(nb, nz, att_grad, qkv, probs, part0, grad1, grad2, out_grad)
-    input_grad, skip_grad, qkv_share, skip_share, norm_share, ff_last = first_back(
-        nb, nz, dqkv, everything, qkvw, x, skip_x, skip_w, mixed, middle_grad, gains, second_sums, grad3
+    dqkv, ff_early, part2 = attention_back(nb, nz, att_grad, qkv, probs, part0, grad1, grad2)
+    input_grad, skip_grad, query_share, key_share, value_share, skip_share, norm_share, up_share, down_share, out_share = (
+        first_back(
+            nb, nz, dqkv, everything, qkvw, x, skip_x, skip_w, mixed, middle_grad, gains, second_sums, ff_early, part2,
+            grad3, out_grad,
+        )
     )
-    cw = up_weight.shape[1] // 4
-    ff_share = jnp.concatenate([ff_share, ff_last[None]], 0)
-    up_share, dn_share = [
-        ff_share[:, :, i * cw : (i + 1) * cw].transpose(1, 0, 2).reshape(up_weight.shape) for i in (0, 1)
-    ]
-    c = query_weight.shape[1]
     return (
         output.reshape(shape),
         input_grad.reshape(shape),
         skip_grad.reshape(shape),
         skip_share,
-        qkv_share[:, :c],
-        qkv_share[:, c : 2 * c],
-        qkv_share[:, 2 * c :],
-        out_share.T,
+        query_share,
+        key_share,
+        value_share,
+        out_share,
         up_share,
-        dn_share.T,
+        down_share,
         norm_share[0],
         norm_share[1],
         norm_share[2],

time: 374 us -> 354 us (0.947)
  Pallas kernels: 360 us -> 343 us
    pallas_call x1, Pallas kernels: 73.6 us -> 49.8 us  [attention_back(): pl.pallas_call(functools.partial(attention_kernel, nb, nz), out_shape=[S(...]
    unnamed x18 -> x30, local copies, waits for them, and re-layouts: 7.53 us -> 8.56 us
where the time goes in v5:
time: 354 us
  Pallas kernels  343 us (97%)
  local copies, waits for them, and re-layouts  10 us (3%)
    pallas_call x1, Pallas kernels, forward(): pl.pallas_call(functools.partial(forward_kernel, nb, nz), out_shape=out_s...  134 us
    pallas_call x1, Pallas kernels, first_back(): pl.pallas_call(functools.partial(first_kernel, nb, nz), out_shape=[S((row...  93.1 us
    pallas_call x1, Pallas kernels, ffn(): pl.pallas_call(functools.partial(ffn_kernel, nb, nz), out_shape=[S((rows,...  66.5 us
    pallas_call x1, Pallas kernels, attention_back(): pl.pallas_call(functools.partial(attention_kernel, nb, nz), out_shape=[S(...  49.8 us
    unnamed x30, local copies, waits for them, and re-layouts  8.56 us

profile of v5, /device:TPU:0, one launch (start us, length us, event | category | flops | bytes accessed | tf_op | source)
XLA Modules:
  0.0 354.1 jit_solution(8103024564150135430)
XLA Ops:
  0.6 133.9 %shard_map.254 = (f32[512,1024]{1,0:T(8,128)}, bf16[1024,1024]{1,0:T(8,128)(2,1)}, f32[8,1024]{1,0:T(8,128)}, bf16[2048,1024]{1,0:T(8,128)(2,1)}, bf16[1024,1536...) custom-call(s32[2]{0:T(128)} %lengths.1, ...), custom_call_target="tpu_custom_call" | custom-call | tf_op jit(solution)/shard_map/pallas_call | solution.py:816
  134.6 66.5 %shard_map.255 = (bf16[512,1024]{1,0:T(8,128)(2,1)}, f32[512,1024]{1,0:T(8,128)}, bf16[512,1024]{1,0:T(8,128)(2,1)}, bf16[8,128,1024]{2,1,0:T(8,128)(2,1)}, bf16...) custom-call(f32[512,1024]{1,0:T(8,128)} %get-tuple-element.49.mixed_, ...), custom_call_target="tpu_custom_call" | custom-call | tf_op jit(solution)/shard_map/pallas_call | solution.py:972
  201.1 49.8 %shard_map.256 = (bf16[1024,1536]{1,0:T(8,128)(2,1)}, f32[2,128,512]{2,1,0:T(8,128)}, bf16[128,2048]{1,0:T(8,128)(2,1)}) custom-call(bf16[512,1024]{1,0:T(8,128)(2,1)} %get-tuple-element.58.att_grad, bf16[3,4,1024,128]{3,2,1,0:T(8,128)(2,1)} %get-tuple-element.59.qkv_in, bf16[4,2,1024,1024]{3,2,1,0:T(8,128)(2,1)} %get-tuple-element.60.probs, ...), custom_call_target="tpu_custom_call" | custom-call | tf_op jit(solution)/shard_map/pallas_call | solution.py:1136
  250.9 0.0 copy-start.2
  250.9 93.1 %shard_map.257 = (f32[512,1024]{1,0:T(8,128)}, f32[512,1024]{1,0:T(8,128)}, f32[128,256]{1,0:T(8,128)}, f32[128,256]{1,0:T(8,128)}, f32[128,256]{1,0:T(8,128)}, ...) custom-call(bf16[1024,1536]{1,0:T(8,128)(2,1)} %get-tuple-element.64, ...), custom_call_target="tpu_custom_call" | custom-call | tf_op jit(solution)/shard_map/pallas_call | solution.py:1399
  344.0 0.0 copy-start.1
  344.0 1.5 fusion
  345.5 0.0 copy-done.2
  345.5 0.0 copy-start
  345.5 1.0 copy.39
  346.5 0.0 copy-done.1
  346.5 1.3 copy.40
  347.8 0.0 copy-done
  347.8 0.0 copy-start.5
  347.8 0.0 copy-start.9
  347.8 0.0 copy-start.8
  347.8 0.0 copy-start.7
  347.8 0.0 copy-start.6
  347.9 0.0 copy-start.4
  347.9 0.0 copy-start.3
  347.9 1.3 copy.41
  349.2 0.0 copy-done.5
  349.2 0.7 copy.42
  349.9 0.0 copy-done.9
  349.9 0.7 copy.43
  350.6 0.0 copy-done.8
  350.6 0.7 copy.44
  351.2 0.0 copy-done.7
  351.2 0.7 copy.45
  351.9 0.0 copy-done.6
  351.9 0.7 copy.46
  352.5 0.0 copy-done.4
  352.5 0.8 copy.47
  353.3 0.0 copy-done.3
  353.3 0.8 copy.48
Async XLA Ops:
  250.9 94.6 %copy-start.2 = (bf16[512,1024]{1,0:T(8,128)(2,1)S(1)}, bf16[512,1024]{1,0:T(8,128)(2,1)}, u32[]{:S(2)}) copy-start(bf16[512,1024]{1,0:T(8,128)(2,1)} %get-tuple-element.57) | copy-start | bytes 3145732
  344.0 2.5 copy-start.1
  345.5 2.3 copy-start
  347.8 1.4 copy-start.5
  347.8 2.1 copy-start.9
  347.8 2.7 copy-start.8
  347.8 3.4 copy-start.7
  347.8 4.0 %copy-start.6 = (f32[256,128]{1,0:T(8,128)S(1)}, f32[256,128]{1,0:T(8,128)}, u32[]{:S(2)}) copy-start(f32[256,128]{1,0:T(8,128)} %get-tuple-element.109) | copy-start | bytes 393220
  347.9 4.7 %copy-start.4 = (f32[128,1024]{1,0:T(8,128)S(1)}, f32[128,1024]{1,0:T(8,128)}, u32[]{:S(2)}) copy-start(f32[128,1024]{1,0:T(8,128)} %get-tuple-element.110) | copy-start | bytes 1572868
  347.9 5.5 %copy-start.3 = (f32[1024,128]{1,0:T(8,128)S(1)}, f32[1024,128]{1,0:T(8,128)}, u32[]{:S(2)}) copy-start(f32[1024,128]{1,0:T(8,128)} %get-tuple-element.111) | copy-start | bytes 1572868

commit v6 on v5

--- a/solution.py
+++ b/solution.py
@@ -11,7 +11,7 @@
 HEAD_DIM = 64
 EPSILON = 1e-05
 LOG2E = 1.4426950408889634
-QUERIES = 256
+QUERIES = 512
 F32 = jnp.float32
 BF16 = jnp.bfloat16
 MESH = pl.DeviceIdType.MESH
@@ -827,8 +827,8 @@
 
 def ffn_kernel(
     nb, nz, mixed_in, attended_in, out_in, norms, cot_in, ff0, ff1, ff2, ff_w,
-    output_out, middle_out, att_out, out_grad, part0, grad1, grad2, grad3, sums, ff3,
-    middle, attended, out_t, cot, weights, grads, ffn_in, ffn_in_t, cot_t, acc, gacc, low,
+    output_out, middle_out, att_out, out_grad_out, part0, grad1, grad2, grad3, sums, ff3,
+    middle, attended, out_t, cot, weights, grads, ffn_in, ffn_in_t, cot_t, acc, gacc, low, out_grad,
     load, wload, flush, *rest,
 ):
     place = Place(nb, nz)
@@ -882,16 +882,23 @@
 
     rest_of = lambda job, t: [(job, s) for s in range(t, job.stages)]
     hook(total // 8, (gather, last))
-    hook(total * 2 // 8, lambda: weight_load(1).wait(), lambda: weight_load(2).start(), (gather, last + 1), (job, 0))
-    hook(total * 4 // 8, lambda: weight_load(2).wait(), (gather, last + 2), lambda: flush_copy(3).start(), (job, 1))
-    hook(total * 5 // 8, *rest_of(gather, last + 3), lambda: weight_load(3).start())
-    hook(total * 6 // 8, lambda: weight_load(3).wait(), lambda: flush_copy(0).start(), (job, 2))
-    hook(total * 7 // 8, *rest_of(job, 3))
+    hook(total * 2 // 8, lambda: weight_load(1).wait(), lambda: weight_load(2).start(), (job, 0))
+    hook(total * 3 // 8, (gather, last + 1))
+    hook(total * 4 // 8, lambda: weight_load(2).wait(), lambda: flush_copy(3).start(), (job, 1))
+    hook(
+        total * 6 // 8,
+        (gather, last + 2),
+        *rest_of(gather, last + 3),
+        lambda: weight_load(3).start(),
+        lambda: flush_copy(0).start(),
+        lambda: weight_load(3).wait(),
+    )
+    hook(total * 7 // 8, (job, 2))
 
     def flush_copy(i):
         pairs = (
             (grads.at[2], grad2), (grads.at[3], grad3), (grads.at[0, 0], part0), (grads.at[1], grad1),
-            (low, output_out), (gacc, middle_out), (attended, att_out),
+            (low, output_out), (gacc, middle_out), (attended, att_out), (out_grad, out_grad_out),
         )
         return pltpu.make_async_copy(*pairs[i], flush.at[i])
 
@@ -924,7 +931,6 @@
 
     lax.fori_loop(0, total, body, 0)
     flush_copy(1).start()
-    flush_copy(2).start()
     sums[...] = jnp.zeros_like(sums)
 
     def leave(at):
@@ -940,9 +946,12 @@
     grad_t = ffn_in[...].T
     for j in range(nb):
         out_grad[flip(place.b, j)] = nn(grad_t[j * r : (j + 1) * r, :], attended[...]).astype(BF16)
+    flush_copy(7).start()
     attended[...] = nn(ffn_in[...], out_t[...]).astype(BF16)
     flush_copy(6).start()
-    for i in range(7):
+    go(job, *range(3, job.stages))
+    flush_copy(2).start()
+    for i in range(8):
         flush_copy(i).wait()
     place.drain()
 
@@ -965,7 +974,8 @@
         V((rows, d), F32),
         V((rows, d), F32),
         V((rows, d), BF16),
-        D((4,)), D((2,)), D((7,)),
+        V((nb, r, d), BF16),
+        D((4,)), D((2,)), D((8,)),
     ]
     scratch += Gather.scratch(nb, nz)
     scratch += Scatter.scratch(nb, nz, r, wide, sums=False, line=False)
@@ -982,7 +992,7 @@
             S((d, wide), BF16),
         ],
         in_specs=[ANY] * 3 + [WHOLE] + [ANY] * 5,
-        out_specs=[ANY] * 3 + [WHOLE] + [ANY] * 4 + [WHOLE, ANY],
+        out_specs=[ANY] * 8 + [WHOLE, ANY],
         scratch_shapes=scratch,
         compiler_params=pltpu.CompilerParams(
             collective_id=3, has_side_effects=True, vmem_limit_bytes=VMEM_LIMIT
@@ -992,8 +1002,8 @@
 
 def attention_kernel(
     nb, nz, att_grad, qkv_in, probs, part0, grad1, grad2,
-    dqkv, ff_share, part2,
-    qkv, dout, pbuf, dk, dv, q_t, do_t, load, psem, att_send, att_recv, *rest,
+    dqkv_out, ff_share, part2,
+    dqkv, qkv, dout, pbuf, dk, dv, q_t, do_t, load, psem, att_send, att_recv, *rest,
 ):
     place = Place(nb, nz)
     z, group, k = place.z, place.group, place.k
@@ -1105,6 +1115,8 @@
         return carry
 
     lax.fori_loop(0, total, body, 0)
+    dqkv_copy = pltpu.make_async_copy(dqkv, dqkv_out, load.at[1])
+    dqkv_copy.start()
     go(late[0], *range(6, late[0].stages))
     go(late[1], *range(3, late[1].stages))
     part_copy = pltpu.make_async_copy(late[1].sums.at[0], part2, load.at[0])
@@ -1113,6 +1125,7 @@
         for r in range(1, nz):
             att_copy(r, pair).wait_send()
     part_copy.wait()
+    dqkv_copy.wait()
     place.drain()
 
 
@@ -1121,6 +1134,7 @@
     S, V, D = jax.ShapeDtypeStruct, pltpu.VMEM, pltpu.SemaphoreType.DMA
     _, r, wide = grad2.shape
     scratch = [
+        V((keys, 3 * pairs * 128), BF16),
         V((3, pairs, keys, 128), BF16),
         V((keys, pairs * 128), BF16),
         V((2, 2, QUERIES, keys), BF16),
@@ -1141,7 +1155,7 @@
             S((r, wide), BF16),
         ],
         in_specs=[ANY] * 6,
-        out_specs=[WHOLE, WHOLE, ANY],
+        out_specs=[ANY, WHOLE, ANY],
         scratch_shapes=scratch,
         compiler_params=pltpu.CompilerParams(
             collective_id=1, has_side_effects=True, vmem_limit_bytes=VMEM_LIMIT
@@ -1151,11 +1165,11 @@
 
 def first_kernel(
     nb, nz, dqkv_in, everything_in, qkvw_in, x, skip_x, skip_w, mixed_in, middle_in, norms, second_sums, ff_early, part2, grad3, out_grad,
-    input_grad, skip_grad, query_out, key_out, value_out, skip_share, norm_share, up_out, down_out, out_out,
-    qkv_share, ff_share, out_share,
+    input_out, skip_out, query_out, key_out, value_out, skip_share, norm_share, up_out, down_out, out_out,
+    input_grad, skip_grad, qkv_share, ff_share, out_share,
     dqkv, everything, qkvw, mixed, middle_grad,
     qkv_grad, skip_w_grad, spare, joined, joined_t, mixed_low, ahead, mine, from_mate, to_partner, from_partner,
-    sums, packed, norm_in, norm_line, load, swap_send, swap_recv, norm_send, norm_recv, *rest,
+    sums, packed, norm_in, norm_line, load, swap_send, swap_recv, norm_send, norm_recv, flush, *rest,
 ):
     place = Place(nb, nz)
     z, group, k, half = place.z, place.group, place.k, place.half
@@ -1321,6 +1335,8 @@
     for one in loads[8:]:
         one.wait()
     input_grad[...] = nt(mixed_low[...], weights[0][...])
+    flushes = [pltpu.make_async_copy(input_grad, input_out, flush.at[0])]
+    flushes[0].start()
     go(skips[0], 2)
     norm_step(2)
     go(ff_job, 5)
@@ -1328,13 +1344,19 @@
     go(line_job, 2)
     go(qkv_job, *range(4, qkv_job.stages))
     skip_grad[...] = nt(mixed_low[...], weights[1][...])
+    flushes.append(pltpu.make_async_copy(skip_grad, skip_out, flush.at[1]))
+    flushes[1].start()
     go(skips[1], 2)
+    go(skips[0], 3)
     norm_step(3)
     go(ff_job, *range(6, ff_job.stages))
     go(out_job, *range(6, out_job.stages))
+    go(skips[1], 3)
     go(line_job, *range(3, line_job.stages))
     for i in range(4, len(bits) + 1):
         norm_step(i)
+    go(skips[0], 4)
+    go(skips[1], 4)
     for i, ref in enumerate((query_out, key_out, value_out)):
         ref[...] = qkv_share[:, i * c : (i + 1) * c]
     out_out[...] = out_share[...].T
@@ -1343,9 +1365,11 @@
         source = ff_early.at[i] if i < 2 else ff_share.at[i - 2]
         up_out[:, i * cw : (i + 1) * cw] = source[:, :cw]
         down_out[i * cw : (i + 1) * cw, :] = source[:, cw:].T
-    for t in range(3, skips[0].stages):
+    for t in range(5, skips[0].stages):
         go(skips[0], t)
         go(skips[1], t)
+    for one in flushes:
+        one.wait()
     value = packed[:, part(z, c)]
     for r in range(1, nz):
         line_copy(r).wait()
@@ -1365,6 +1389,8 @@
     swaps = 2 * (half - 1)
     r, wide = ff_early.shape[1:]
     scratch = [
+        V((rows, width), F32),
+        V((rows, width), F32),
         V((r, 3 * c), F32),
         V((2, r, wide), F32),
         V((r, c), F32),
@@ -1388,7 +1414,7 @@
         V((8, width), F32),
         V((bits, 8, width), F32),
         V((nz - 1, 8, c), F32),
-        D((10,)), D((swaps + 1,)), D((swaps + 1,)), D((bits + nz - 1,)), D((bits + nz - 1,)),
+        D((10,)), D((swaps + 1,)), D((swaps + 1,)), D((bits + nz - 1,)), D((bits + nz - 1,)), D((2,)),
     ]
     scratch += Scatter.scratch(nb, nz, grad3.shape[1], grad3.shape[2], plane=False)
     scratch += Scatter.scratch(nb, nz, grad3.shape[1], grad3.shape[2])
@@ -1409,7 +1435,7 @@
             S((c, r), F32),
         ],
         in_specs=[ANY] * 8 + [WHOLE] * 3 + [ANY] * 3,
-        out_specs=[WHOLE] * 10,
+        out_specs=[ANY] * 2 + [WHOLE] * 8,
         scratch_shapes=scratch,
         compiler_params=pltpu.CompilerParams(
             collective_id=2, has_side_effects=True, vmem_limit_bytes=VMEM_LIMIT

time: 354 us -> 341 us (0.963)
  Pallas kernels: 343 us -> 330 us
    pallas_call x1, Pallas kernels: 66.5 us -> 59.4 us  [ffn(): pl.pallas_call(functools.partial(ffn_kernel, nb, nz), out_shape=[S((rows,...]
    pallas_call x1, Pallas kernels: 93.1 us -> 89.3 us  [first_back(): pl.pallas_call(functools.partial(first_kernel, nb, nz), out_shape=[S((row...]
where the time goes in v6:
time: 341 us
  Pallas kernels  330 us (97%)
  local copies, waits for them, and re-layouts  10 us (3%)
    pallas_call x1, Pallas kernels, forward(): pl.pallas_call(functools.partial(forward_kernel, nb, nz), out_shape=out_s...  131 us
    pallas_call x1, Pallas kernels, first_back(): pl.pallas_call(functools.partial(first_kernel, nb, nz), out_shape=[S((row...  89.3 us
    pallas_call x1, Pallas kernels, ffn(): pl.pallas_call(functools.partial(ffn_kernel, nb, nz), out_shape=[S((rows,...  59.4 us
    pallas_call x1, Pallas kernels, attention_back(): pl.pallas_call(functools.partial(attention_kernel, nb, nz), out_shape=[S(...  51 us
    unnamed x30, local copies, waits for them, and re-layouts  8.56 us

profile of v6, /device:TPU:0, one launch (start us, length us, event | category | flops | bytes accessed | tf_op | source)
XLA Modules:
  0.0 341.1 jit_solution(12313999318030379719)
XLA Ops:
  0.6 130.6 %shard_map.254 = (f32[512,1024]{1,0:T(8,128)}, bf16[1024,1024]{1,0:T(8,128)(2,1)}, f32[8,1024]{1,0:T(8,128)}, bf16[2048,1024]{1,0:T(8,128)(2,1)}, bf16[1024,1536...) custom-call(s32[2]{0:T(128)} %lengths.1, ...), custom_call_target="tpu_custom_call" | custom-call | tf_op jit(solution)/shard_map/pallas_call | solution.py:816
  131.3 59.4 %shard_map.255 = (bf16[512,1024]{1,0:T(8,128)(2,1)}, f32[512,1024]{1,0:T(8,128)}, bf16[512,1024]{1,0:T(8,128)(2,1)}, bf16[8,128,1024]{2,1,0:T(8,128)(2,1)}, bf16...) custom-call(f32[512,1024]{1,0:T(8,128)} %get-tuple-element.49.mixed_, ...), custom_call_target="tpu_custom_call" | custom-call | tf_op jit(solution)/shard_map/pallas_call | solution.py:982
  190.7 51.0 %shard_map.256 = (bf16[1024,1536]{1,0:T(8,128)(2,1)}, f32[2,128,512]{2,1,0:T(8,128)}, bf16[128,2048]{1,0:T(8,128)(2,1)}) custom-call(bf16[512,1024]{1,0:T(8,128)(2,1)} %get-tuple-element.58.att_grad, bf16[3,4,1024,128]{3,2,1,0:T(8,128)(2,1)} %get-tuple-element.59.qkv_in, bf16[4,2,1024,1024]{3,2,1,0:T(8,128)(2,1)} %get-tuple-element.60.probs, ...), custom_call_target="tpu_custom_call" | custom-call | tf_op jit(solution)/shard_map/pallas_call | solution.py:1150
  241.7 0.0 copy-start.2
  241.7 89.3 %shard_map.257 = (f32[512,1024]{1,0:T(8,128)}, f32[512,1024]{1,0:T(8,128)}, f32[128,256]{1,0:T(8,128)}, f32[128,256]{1,0:T(8,128)}, f32[128,256]{1,0:T(8,128)}, ...) custom-call(bf16[1024,1536]{1,0:T(8,128)(2,1)} %get-tuple-element.64, ...), custom_call_target="tpu_custom_call" | custom-call | tf_op jit(solution)/shard_map/pallas_call | solution.py:1425
  331.0 0.0 copy-start.1
  331.0 1.5 fusion
  332.5 0.0 copy-done.2
  332.5 0.0 copy-start
  332.5 1.0 copy.39
  333.4 0.0 copy-done.1
  333.4 1.3 copy.40
  334.8 0.0 copy-done
  334.8 0.0 copy-start.5
  334.8 0.0 copy-start.9
  334.8 0.0 copy-start.8
  334.8 0.0 copy-start.7
  334.8 0.0 copy-start.6
  334.8 0.0 copy-start.4
  334.8 0.0 copy-start.3
  334.8 1.3 copy.41
  336.1 0.0 copy-done.5
  336.1 0.7 copy.42
  336.8 0.0 copy-done.9
  336.8 0.7 copy.43
  337.5 0.0 copy-done.8
  337.5 0.7 copy.44
  338.1 0.0 copy-done.7
  338.2 0.7 copy.45
  338.8 0.0 copy-done.6
  338.8 0.7 copy.46
  339.5 0.0 copy-done.4
  339.5 0.8 copy.47
  340.3 0.0 copy-done.3
  340.3 0.8 copy.48
Async XLA Ops:
  241.7 90.8 %copy-start.2 = (bf16[512,1024]{1,0:T(8,128)(2,1)S(1)}, bf16[512,1024]{1,0:T(8,128)(2,1)}, u32[]{:S(2)}) copy-start(bf16[512,1024]{1,0:T(8,128)(2,1)} %get-tuple-element.57) | copy-start | bytes 3145732
  331.0 2.5 copy-start.1
  332.5 2.3 copy-start
  334.8 1.4 copy-start.5
  334.8 2.1 copy-start.9
  334.8 2.7 copy-start.8
  334.8 3.4 copy-start.7
  334.8 4.0 %copy-start.6 = (f32[256,128]{1,0:T(8,128)S(1)}, f32[256,128]{1,0:T(8,128)}, u32[]{:S(2)}) copy-start(f32[256,128]{1,0:T(8,128)} %get-tuple-element.109) | copy-start | bytes 393220
  334.8 4.7 %copy-start.4 = (f32[128,1024]{1,0:T(8,128)S(1)}, f32[128,1024]{1,0:T(8,128)}, u32[]{:S(2)}) copy-start(f32[128,1024]{1,0:T(8,128)} %get-tuple-element.110) | copy-start | bytes 1572868
  334.8 5.5 %copy-start.3 = (f32[1024,128]{1,0:T(8,128)S(1)}, f32[1024,128]{1,0:T(8,128)}, u32[]{:S(2)}) copy-start(f32[1024,128]{1,0:T(8,128)} %get-tuple-element.111) | copy-start | bytes 1572868

commit v7 on v6

--- a/solution.py
+++ b/solution.py
@@ -718,18 +718,23 @@
 
     hooks = {}
 
+    placed = {}
+
     def hook(it, *steps):
-        hooks.setdefault(min(it, total - 1), []).extend(steps)
+        at = min(it, total - 1)
+        for step in steps:
+            if not callable(step):
+                at = max(at, placed.get(id(step[0]), 0))
+                placed[id(step[0])] = at
+            hooks.setdefault(at, []).append(step)
 
     rest_of = lambda job, t: [(job, s) for s in range(t, job.stages)]
     for t in range(1, last):
         hook(t - 1, (ff[2], t), (out_job, t))
-    hook(last - 1, (ff[1], last + 2), (ff[2], last), (out_job, last))
-    hook(total * 4 // 16, *rest_of(ff[0], last + 3))
-    hook(total * 6 // 16, (ff[2], last + 1), (out_job, last + 1))
-    hook(total * 8 // 16, *rest_of(ff[1], last + 3))
-    hook(total * 13 // 16, (ff[2], last + 2))
-    hook(total * 15 // 16, (out_job, last + 2))
+    hook(2, (ff[1], last + 2), (out_job, last), (ff[2], last), *rest_of(ff[0], last + 3))
+    hook(4, (out_job, last + 1), (ff[2], last + 1))
+    hook(5, *rest_of(ff[1], last + 3))
+    hook(7, (out_job, last + 2), (ff[2], last + 2))
 
     def body(it, carry):
         pair, q = lax.div(it, blocks), lax.rem(it, blocks)
@@ -837,12 +842,10 @@
     cw = ff_w.shape[1] // 2
     subs = nz // 2
     total = 4 * subs
-    place.greet()
     gather = Gather(place, ff_w, ff3, rest[:3])
     job = Scatter(place, grads.at[0], None, rest[3:], sums=False, line=False)
     go = lambda job, *stages: [job.stage(t) for t in stages if t < job.stages]
     last = nz - 1
-    go(gather, 0)
     loads = [
         pltpu.make_async_copy(src, dst, load.at[i])
         for i, (src, dst) in enumerate(
@@ -854,6 +857,8 @@
         one.start()
     weight_load(0).start()
     weight_load(1).start()
+    place.greet()
+    go(gather, 0)
     gain, shift = norms[2:3, :], norms[3:4, :]
     for one in loads[:3]:
         one.wait()
@@ -877,8 +882,15 @@
 
     hooks = {}
 
+    placed = {}
+
     def hook(it, *steps):
-        hooks.setdefault(min(it, total - 1), []).extend(steps)
+        at = min(it, total - 1)
+        for step in steps:
+            if not callable(step):
+                at = max(at, placed.get(id(step[0]), 0))
+                placed[id(step[0])] = at
+            hooks.setdefault(at, []).append(step)
 
     rest_of = lambda job, t: [(job, s) for s in range(t, job.stages)]
     hook(total // 8, (gather, last))
@@ -1011,6 +1023,8 @@
     frames = keys // nz
     wide = pairs * 128
     pz = pairs // 2
+    qkv_load = pltpu.make_async_copy(qkv_in, qkv, load.at[1])
+    qkv_load.start()
     place.greet()
 
     def att_copy(r, pair):
@@ -1031,8 +1045,6 @@
         att_start(pair)
     own = pltpu.make_async_copy(att_grad.at[part(group, frames), part(k, wide)], dout.at[part(z, frames)], load.at[0])
     own.start()
-    qkv_load = pltpu.make_async_copy(qkv_in, qkv, load.at[1])
-    qkv_load.start()
     rest = list(rest)
 
     def job(full, share, **kind):
@@ -1065,8 +1077,15 @@
     probs_copy(0).start()
     hooks = {}
 
+    placed = {}
+
     def hook(it, *steps):
-        hooks.setdefault(min(it, total - 1), []).extend(steps)
+        at = min(it, total - 1)
+        for step in steps:
+            if not callable(step):
+                at = max(at, placed.get(id(step[0]), 0))
+                placed[id(step[0])] = at
+            hooks.setdefault(at, []).append(step)
 
     zs = place.nz - 1
     rest_of = lambda job, t: [(job, s) for s in range(t, job.stages)]
@@ -1228,7 +1247,8 @@
         for s in (0, 1):
             block = lax.rem(k + r, half) + (1 - group if s == 0 else group) * half
             ahead[(r - 1) * 2 + s] = nt(dqkv[part(block, frames), :], qkvw[...]).astype(BF16)
-        place.start(mate_copy, r, 0)
+            if s == 0:
+                place.start(mate_copy, r, 0)
     for s in (0, 1):
         block = k + (1 - group if s == 0 else group) * half
         mine[s] = nt(dqkv[part(block, frames), :], qkvw[...])

time: 341 us -> 340 us (level)
  no operation moved by 1% of the time
where the time goes in v7:
time: 340 us
  Pallas kernels  329 us (97%)
  local copies, waits for them, and re-layouts  10 us (3%)
    pallas_call x1, Pallas kernels, forward(): pl.pallas_call(functools.partial(forward_kernel, nb, nz), out_shape=out_s...  129 us
    pallas_call x1, Pallas kernels, first_back(): pl.pallas_call(functools.partial(first_kernel, nb, nz), out_shape=[S((row...  88.5 us
    pallas_call x1, Pallas kernels, ffn(): pl.pallas_call(functools.partial(ffn_kernel, nb, nz), out_shape=[S((rows,...  60.6 us
    pallas_call x1, Pallas kernels, attention_back(): pl.pallas_call(functools.partial(attention_kernel, nb, nz), out_shape=[S(...  51.2 us
    unnamed x30, local copies, waits for them, and re-layouts  8.56 us

profile of v7, /device:TPU:0, one launch (start us, length us, event | category | flops | bytes accessed | tf_op | source)
XLA Modules:
  0.0 340.0 jit_solution(12688474455596883601)
XLA Ops:
  0.6 128.9 %shard_map.254 = (f32[512,1024]{1,0:T(8,128)}, bf16[1024,1024]{1,0:T(8,128)(2,1)}, f32[8,1024]{1,0:T(8,128)}, bf16[2048,1024]{1,0:T(8,128)(2,1)}, bf16[1024,1536...) custom-call(s32[2]{0:T(128)} %lengths.1, ...), custom_call_target="tpu_custom_call" | custom-call | tf_op jit(solution)/shard_map/pallas_call | solution.py:821
  129.6 60.6 %shard_map.255 = (bf16[512,1024]{1,0:T(8,128)(2,1)}, f32[512,1024]{1,0:T(8,128)}, bf16[512,1024]{1,0:T(8,128)(2,1)}, bf16[8,128,1024]{2,1,0:T(8,128)(2,1)}, bf16...) custom-call(f32[512,1024]{1,0:T(8,128)} %get-tuple-element.49.mixed_, ...), custom_call_target="tpu_custom_call" | custom-call | tf_op jit(solution)/shard_map/pallas_call | solution.py:994
  190.2 51.2 %shard_map.256 = (bf16[1024,1536]{1,0:T(8,128)(2,1)}, f32[2,128,512]{2,1,0:T(8,128)}, bf16[128,2048]{1,0:T(8,128)(2,1)}) custom-call(bf16[512,1024]{1,0:T(8,128)(2,1)} %get-tuple-element.58.att_grad, bf16[3,4,1024,128]{3,2,1,0:T(8,128)(2,1)} %get-tuple-element.59.qkv_in, bf16[4,2,1024,1024]{3,2,1,0:T(8,128)(2,1)} %get-tuple-element.60.probs, ...), custom_call_target="tpu_custom_call" | custom-call | tf_op jit(solution)/shard_map/pallas_call | solution.py:1169
  241.4 0.0 copy-start.2
  241.4 88.5 %shard_map.257 = (f32[512,1024]{1,0:T(8,128)}, f32[512,1024]{1,0:T(8,128)}, f32[128,256]{1,0:T(8,128)}, f32[128,256]{1,0:T(8,128)}, f32[128,256]{1,0:T(8,128)}, ...) custom-call(bf16[1024,1536]{1,0:T(8,128)(2,1)} %get-tuple-element.64, ...), custom_call_target="tpu_custom_call" | custom-call | tf_op jit(solution)/shard_map/pallas_call | solution.py:1445
  329.9 0.0 copy-start.1
  329.9 1.5 fusion
  331.4 0.0 copy-done.2
  331.4 0.0 copy-start
  331.4 1.0 copy.39
  332.4 0.0 copy-done.1
  332.4 1.3 copy.40
  333.7 0.0 copy-done
  333.7 0.0 copy-start.5
  333.7 0.0 copy-start.9
  333.7 0.0 copy-start.8
  333.7 0.0 copy-start.7
  333.7 0.0 copy-start.6
  333.7 0.0 copy-start.4
  333.7 0.0 copy-start.3
  333.7 1.3 copy.41
  335.0 0.0 copy-done.5
  335.1 0.7 copy.42
  335.8 0.0 copy-done.9
  335.8 0.7 copy.43
  336.4 0.0 copy-done.8
  336.4 0.7 copy.44
  337.1 0.0 copy-done.7
  337.1 0.7 copy.45
  337.7 0.0 copy-done.6
  337.7 0.7 copy.46
  338.4 0.0 copy-done.4
  338.4 0.8 copy.47
  339.2 0.0 copy-done.3
  339.2 0.8 copy.48
Async XLA Ops:
  241.4 90.0 %copy-start.2 = (bf16[512,1024]{1,0:T(8,128)(2,1)S(1)}, bf16[512,1024]{1,0:T(8,128)(2,1)}, u32[]{:S(2)}) copy-start(bf16[512,1024]{1,0:T(8,128)(2,1)} %get-tuple-element.57) | copy-start | bytes 3145732
  329.9 2.5 copy-start.1
  331.4 2.3 copy-start
  333.7 1.4 copy-start.5
  333.7 2.1 copy-start.9
  333.7 2.7 copy-start.8
  333.7 3.4 copy-start.7
  333.7 4.0 %copy-start.6 = (f32[256,128]{1,0:T(8,128)S(1)}, f32[256,128]{1,0:T(8,128)}, u32[]{:S(2)}) copy-start(f32[256,128]{1,0:T(8,128)} %get-tuple-element.109) | copy-start | bytes 393220
  333.7 4.7 %copy-start.4 = (f32[128,1024]{1,0:T(8,128)S(1)}, f32[128,1024]{1,0:T(8,128)}, u32[]{:S(2)}) copy-start(f32[128,1024]{1,0:T(8,128)} %get-tuple-element.110) | copy-start | bytes 1572868
  333.7 5.5 %copy-start.3 = (f32[1024,128]{1,0:T(8,128)S(1)}, f32[1024,128]{1,0:T(8,128)}, u32[]{:S(2)}) copy-start(f32[1024,128]{1,0:T(8,128)} %get-tuple-element.111) | copy-start | bytes 1572868
